TPU v7x, 32 devices: a whole 2x2x4 slice. The times are simulated.
32 devices in a mesh: section: 2 (over x), seq: 4 (over y, core), fsdp: 4 (over z).
Axes of the slice: x: 2, y: 2, z: 4, core: 2. Of those that a mesh axis runs over, the one named last changes fastest.
Arguments:
- tokens: bfloat16 [2, 4, 1024, 1536], P(None, 'fsdp', 'seq'), may hold values from -6 to 6
- in_weight: bfloat16 [2, 1536, 4608], P('section', 'fsdp'), may hold values from -0.15625 to 0.15625
- conv_kernel: bfloat16 [2, 1536, 3], P('section', 'fsdp'), may hold values from -3 to 3
- out_weight: bfloat16 [2, 1536, 1536], P('section', 'fsdp'), may hold values from -0.15625 to 0.15625
- gate_weight: bfloat16 [2, 1536, 6912], P('section', 'fsdp'), may hold values from -0.15625 to 0.15625
- up_weight: bfloat16 [2, 1536, 6912], P('section', 'fsdp'), may hold values from -0.15625 to 0.15625
- down_weight: bfloat16 [2, 6912, 1536], P('section', 'fsdp'), may hold values from -0.078125 to 0.078125
- mixer_gain: bfloat16 [2, 1536], P('section', 'fsdp'), may hold values from 0.099609375 to 1.8984375
- ffn_gain: bfloat16 [2, 1536], P('section', 'fsdp'), may hold values from 0.099609375 to 1.8984375
- cotangent: bfloat16 [2, 4, 1024, 1536], P(None, 'fsdp', 'seq'), may hold values from -6 to 6
Outputs:
- section_out: bfloat16 [2, 2, 4, 1024, 1536], P('section', None, 'fsdp', 'seq')
- section_grad: float32 [2, 2, 4, 1024, 1536], P('section', None, 'fsdp', 'seq')
- in_weight_grad: float32 [2, 1536, 4608], P('section', 'fsdp')
- conv_kernel_grad: float32 [2, 1536, 3], P('section', 'fsdp')
- out_weight_grad: float32 [2, 1536, 1536], P('section', 'fsdp')
- gate_weight_grad: float32 [2, 1536, 6912], P('section', 'fsdp')
- up_weight_grad: float32 [2, 1536, 6912], P('section', 'fsdp')
- down_weight_grad: float32 [2, 6912, 1536], P('section', 'fsdp')
- mixer_gain_grad: float32 [2, 1536], P('section', 'fsdp')
- ffn_gain_grad: float32 [2, 1536], P('section', 'fsdp')
All inputs are finite; a program needn't handle non-finite values.
Results may differ from a plain program's by a relative error of at most 0.022.
Values may be sent and summed in bfloat16 or wider, within the bound.
A program may use at most 448 MiB of HBM per device.

v0:
```python
import jax
import jax.numpy as jnp
from jax import lax
from jax.sharding import PartitionSpec as P

EPSILON = 1e-05


def from_behind(value, axis, steps):
    count = lax.axis_size(axis)
    leading, last = (max(0, -steps), min(count, count - steps))
    return lax.ppermute(value, axis, [(source, source + steps) for source in range(leading, last)])


def rms_scale(stream):
    return lax.rsqrt(jnp.mean(stream * stream, -1, keepdims=True) + EPSILON)


def times_transposed(left, matrix):
    return lax.dot_general(
        left, matrix, (((1,), (1,)), ((), ())), preferred_element_type=jnp.float32
    )


def block_forward(stream, weights):
    (
        in_matrix,
        conv_taps,
        out_matrix,
        gate_matrix,
        up_matrix,
        down_matrix,
        mixer_scale,
        ffn_scale,
    ) = weights
    model_width = stream.shape[1]
    scale_mix = rms_scale(stream)
    normed = (stream * scale_mix * mixer_scale.astype(jnp.float32)).astype(jnp.bfloat16)
    projected = jnp.dot(normed, in_matrix, preferred_element_type=jnp.float32)
    b_gate = projected[:, :model_width]
    c_gate = projected[:, model_width : 2 * model_width]
    x_value = projected[:, 2 * model_width :]
    conv_input = (b_gate * x_value).astype(jnp.bfloat16)
    earlier_rows = from_behind(conv_input[-2:], "seq", 1)
    extended = jnp.concatenate([earlier_rows, conv_input], 0).astype(jnp.float32)
    taps = conv_taps.astype(jnp.float32)
    conv_out = taps[:, 0] * extended[:-2] + taps[:, 1] * extended[1:-1] + taps[:, 2] * extended[2:]
    gated = (c_gate * conv_out).astype(jnp.bfloat16)
    middle = stream + jnp.dot(gated, out_matrix, preferred_element_type=jnp.float32)
    scale_ffn = rms_scale(middle)
    normed_ffn = (middle * scale_ffn * ffn_scale.astype(jnp.float32)).astype(jnp.bfloat16)
    gate_value = jnp.dot(normed_ffn, gate_matrix, preferred_element_type=jnp.float32)
    up_value = jnp.dot(normed_ffn, up_matrix, preferred_element_type=jnp.float32)
    hidden = (jax.nn.silu(gate_value) * up_value).astype(jnp.bfloat16)
    result = middle + jnp.dot(hidden, down_matrix, preferred_element_type=jnp.float32)
    stored = (
        stream,
        scale_mix,
        normed,
        projected,
        extended,
        conv_out,
        gated,
        middle,
        scale_ffn,
        normed_ffn,
        gate_value,
        up_value,
        hidden,
    )
    return (result, stored)


def block_backward(upstream, stored, weights):
    (
        in_matrix,
        conv_taps,
        out_matrix,
        gate_matrix,
        up_matrix,
        down_matrix,
        mixer_scale,
        ffn_scale,
    ) = weights
    (
        stream,
        scale_mix,
        normed,
        projected,
        extended,
        conv_out,
        gated,
        middle,
        scale_ffn,
        normed_ffn,
        gate_value,
        up_value,
        hidden,
    ) = stored
    model_width = stream.shape[1]
    down_grad = upstream.astype(jnp.bfloat16)
    grad_hidden = times_transposed(down_grad, down_matrix)
    sigmoid_gate = jax.nn.sigmoid(gate_value)
    grad_gate = (
        grad_hidden * up_value * sigmoid_gate * (1.0 + gate_value * (1.0 - sigmoid_gate))
    ).astype(jnp.bfloat16)
    grad_up = (grad_hidden * gate_value * sigmoid_gate).astype(jnp.bfloat16)
    grad_normed_ffn = times_transposed(grad_gate, gate_matrix) + times_transposed(
        grad_up, up_matrix
    )
    ffn_gain_part = jnp.sum(grad_normed_ffn * middle * scale_ffn, 0)
    weighted_ffn = ffn_scale.astype(jnp.float32) * grad_normed_ffn
    grad_middle = (
        upstream
        + scale_ffn * weighted_ffn
        - middle * scale_ffn**3 * jnp.mean(weighted_ffn * middle, -1, keepdims=True)
    )
    mixer_grad = grad_middle.astype(jnp.bfloat16)
    grad_gated = times_transposed(mixer_grad, out_matrix)
    b_gate = projected[:, :model_width]
    c_gate = projected[:, model_width : 2 * model_width]
    x_value = projected[:, 2 * model_width :]
    grad_cgate = grad_gated * conv_out
    grad_conv = grad_gated * c_gate
    later_rows = from_behind(grad_conv[:2], "seq", -1)
    grad_extended = jnp.concatenate([grad_conv, later_rows], 0)
    taps = conv_taps.astype(jnp.float32)
    grad_input = (
        taps[:, 0] * grad_extended[2:]
        + taps[:, 1] * grad_extended[1:-1]
        + taps[:, 2] * grad_extended[:-2]
    )
    taps_part = jnp.stack(
        [
            jnp.sum(grad_conv * extended[:-2], 0),
            jnp.sum(grad_conv * extended[1:-1], 0),
            jnp.sum(grad_conv * extended[2:], 0),
        ],
        1,
    )
    grad_projected = jnp.concatenate(
        [grad_input * x_value, grad_cgate, grad_input * b_gate], 1
    ).astype(jnp.bfloat16)
    grad_normed = times_transposed(grad_projected, in_matrix)
    mixer_gain_part = jnp.sum(grad_normed * stream * scale_mix, 0)
    weighted_mix = mixer_scale.astype(jnp.float32) * grad_normed
    grad_stream = (
        grad_middle
        + scale_mix * weighted_mix
        - stream * scale_mix**3 * jnp.mean(weighted_mix * stream, -1, keepdims=True)
    )
    record = (
        normed,
        grad_projected,
        gated,
        mixer_grad,
        normed_ffn,
        jnp.concatenate([grad_gate, grad_up], 1),
        hidden,
        down_grad,
    )
    return (grad_stream, record, (taps_part, mixer_gain_part, ffn_gain_part))


def row_products(left, right):
    return lax.dot_general(
        left, right, (((0,), (0,)), ((), ())), preferred_element_type=jnp.float32
    )


def body(
    tokens,
    in_weight,
    conv_kernel,
    out_weight,
    gate_weight,
    up_weight,
    down_weight,
    mixer_gain,
    ffn_gain,
    cotangent,
):
    section_index = lax.axis_index("section")
    section_count = lax.axis_size("section")
    slot_count = tokens.shape[0]
    tick_count = slot_count + section_count - 1
    weights = (
        lax.all_gather(in_weight[0], "fsdp", axis=0, tiled=True),
        lax.all_gather(conv_kernel[0], "fsdp", axis=0, tiled=True),
        lax.all_gather(out_weight[0], "fsdp", axis=0, tiled=True),
        lax.all_gather(gate_weight[0], "fsdp", axis=0, tiled=True),
        lax.all_gather(up_weight[0], "fsdp", axis=0, tiled=True),
        lax.all_gather(down_weight[0], "fsdp", axis=0, tiled=True),
        lax.all_gather(mixer_gain[0], "fsdp", axis=0, tiled=True),
        lax.all_gather(ffn_gain[0], "fsdp", axis=0, tiled=True),
    )
    inputs = tokens[:, 0]
    targets = cotangent[:, 0]
    piece_rows = inputs.shape[1]
    model_width = inputs.shape[2]
    slot_ids = jnp.arange(slot_count)
    saved = []
    outputs = jnp.zeros((slot_count, piece_rows, model_width), jnp.bfloat16)
    received = jnp.zeros((piece_rows, model_width), jnp.bfloat16)
    for moment in range(tick_count):
        fresh = inputs[min(moment, slot_count - 1)]
        entry = jnp.where(section_index == 0, fresh, received)
        result, stored = block_forward(entry.astype(jnp.float32), weights)
        sent = result.astype(jnp.bfloat16)
        saved.append(stored)
        outputs = jnp.where(
            (slot_ids == moment - section_index)[:, None, None], sent[None], outputs
        )
        if moment < tick_count - 1:
            received = from_behind(sent, "section", 1)
    records = []
    grads_in = jnp.zeros((slot_count, piece_rows, model_width), jnp.float32)
    returned = jnp.zeros((piece_rows, model_width), jnp.bfloat16)
    taps_total = jnp.zeros((model_width, conv_kernel.shape[2]), jnp.float32)
    mixer_total = jnp.zeros((model_width,), jnp.float32)
    ffn_total = jnp.zeros((model_width,), jnp.float32)
    for moment in range(tick_count):
        forward_tick = tick_count - 1 - moment
        last_slot = min(max(forward_tick - section_count + 1, 0), slot_count - 1)
        mine = forward_tick - section_index
        valid = (mine >= 0) & (mine < slot_count)
        upstream = jnp.where(
            section_index == section_count - 1,
            targets[last_slot].astype(jnp.float32),
            returned.astype(jnp.float32),
        )
        upstream = jnp.where(valid, upstream, 0.0)
        grad_entry, record, small_parts = block_backward(upstream, saved[forward_tick], weights)
        records.append(record)
        taps_total = taps_total + small_parts[0]
        mixer_total = mixer_total + small_parts[1]
        ffn_total = ffn_total + small_parts[2]
        grads_in = jnp.where((slot_ids == mine)[:, None, None], grad_entry[None], grads_in)
        if moment < tick_count - 1:
            returned = from_behind(grad_entry.astype(jnp.bfloat16), "section", -1)
    stacked = [jnp.concatenate([entry[column] for entry in records], 0) for column in range(8)]
    pairs = (
        (stacked[0], stacked[1]),
        (stacked[2], stacked[3]),
        (stacked[4], stacked[5]),
        (stacked[6], stacked[7]),
    )

    def reduce_rows(left, right):
        return lax.psum_scatter(
            row_products(left, right).astype(jnp.bfloat16), "fsdp", scatter_dimension=0, tiled=True
        ).astype(jnp.float32)

    matrices = [reduce_rows(left, right) for left, right in pairs]
    smalls = (
        lax.psum_scatter(taps_total, "fsdp", scatter_dimension=0, tiled=True),
        lax.psum_scatter(mixer_total, "fsdp", scatter_dimension=0, tiled=True),
        lax.psum_scatter(ffn_total, "fsdp", scatter_dimension=0, tiled=True),
    )
    gathered = (
        lax.psum(matrices[0].astype(jnp.bfloat16), "seq").astype(jnp.float32),
        lax.psum(matrices[1].astype(jnp.bfloat16), "seq").astype(jnp.float32),
        lax.psum(matrices[2].astype(jnp.bfloat16), "seq").astype(jnp.float32),
        lax.psum(matrices[3].astype(jnp.bfloat16), "seq").astype(jnp.float32),
        lax.psum(smalls[0].astype(jnp.bfloat16), "seq").astype(jnp.float32),
        lax.psum(smalls[1].astype(jnp.bfloat16), "seq").astype(jnp.float32),
        lax.psum(smalls[2].astype(jnp.bfloat16), "seq").astype(jnp.float32),
    )
    in_grad, out_grad, pair_grad, down_total, taps_grad, mixer_grad_total, ffn_grad_total = gathered
    ff_width = gate_weight.shape[2]
    return (
        outputs[None, :, None],
        grads_in[None, :, None],
        in_grad[None],
        taps_grad[None],
        out_grad[None],
        pair_grad[:, :ff_width][None],
        pair_grad[:, ff_width:][None],
        down_total[None],
        mixer_grad_total[None],
        ffn_grad_total[None],
    )


def solution(mesh):
    placed = (
        P(None, "fsdp", "seq", None),
        P("section", "fsdp", None),
        P("section", "fsdp", None),
        P("section", "fsdp", None),
        P("section", "fsdp", None),
        P("section", "fsdp", None),
        P("section", "fsdp", None),
        P("section", "fsdp"),
        P("section", "fsdp"),
        P(None, "fsdp", "seq", None),
    )
    return jax.shard_map(
        body,
        mesh=mesh,
        in_specs=placed,
        out_specs=(
            P("section", None, "fsdp", "seq", None),
            P("section", None, "fsdp", "seq", None),
            P("section", "fsdp", None),
            P("section", "fsdp", None),
            P("section", "fsdp", None),
            P("section", "fsdp", None),
            P("section", "fsdp", None),
            P("section", "fsdp", None),
            P("section", "fsdp"),
            P("section", "fsdp"),
        ),
        check_vma=False,
    )
```

profile of v0, /device:TPU:0, one launch (start us, length us, event | category | flops | bytes accessed | tf_op | source)
XLA Modules:
  0.0 3636.4 jit_solution(9427794033161390080)
XLA Ops:
  10.7 13.5 all-gather
  24.2 16.1 all-gather.4
  40.3 25.8 all-gather.2
  67.4 189.1 %all-gather.14.cloned.1.call-done = bf16[1,1536,4608]{2,1,0:T(8,128)(2,1)} async-done(((bf16[1,384,4608]{2,1,0:T(8,128)(2,1)}), bf16[1,1536,4608]{2,1,0:T(8,128)(2,1)}) %all-gather.14.cloned.1.call-update) | async-done | bytes 14155792 | tf_op jit(solution)/shard_map/all_gather | solution.py:188
  269.9 75.8 %all-gather.16.cloned.1.call-done = bf16[1,1536,1536]{2,1,0:T(8,128)(2,1)} async-done(((bf16[1,384,1536]{2,1,0:T(8,128)(2,1)}), bf16[1,1536,1536]{2,1,0:T(8,128)(2,1)}) %all-gather.16.cloned.1.call-update) | async-done | bytes 4718608 | tf_op jit(solution)/shard_map/all_gather | solution.py:190
  351.5 355.4 %all-gather.18.cloned.1.call-done = bf16[1,1536,6912]{2,1,0:T(8,128)(2,1)} async-done(((bf16[1,384,6912]{2,1,0:T(8,128)(2,1)}), bf16[1,1536,6912]{2,1,0:T(8,128)(2,1)}) %all-gather.18.cloned.1.call-update) | async-done | bytes 21233680 | tf_op jit(solution)/shard_map/all_gather | solution.py:191
  706.9 15.3 fusion.45
  722.3 345.8 %all-gather.20.cloned.1.call-done = bf16[1,1536,6912]{2,1,0:T(8,128)(2,1)} async-done(((bf16[1,384,6912]{2,1,0:T(8,128)(2,1)}), bf16[1,1536,6912]{2,1,0:T(8,128)(2,1)}) %all-gather.20.cloned.1.call-update) | async-done | bytes 21233680 | tf_op jit(solution)/shard_map/all_gather | solution.py:192
  1068.1 18.5 multiply_convert_fusion.8
  1086.5 342.7 %all-gather.22.cloned.1.call-done = bf16[1,6912,1536]{2,1,0:T(8,128)(2,1)} async-done(((bf16[1,1728,1536]{2,1,0:T(8,128)(2,1)}), bf16[1,6912,1536]{2,1,0:T(8,128)(2,1)}) %all-gather.22.cloned.1.call-update) | async-done | bytes 21233680 | tf_op jit(solution)/shard_map/all_gather | solution.py:193
  1444.0 16.6 collective-permute-done.1
  1484.4 19.8 multiply_convert_fusion.7
  1522.0 15.5 collective-permute-done.3
  1551.7 13.1 fusion.15
  1574.5 14.7 fusion.29
  1589.2 18.1 multiply_convert_fusion.5
  1607.2 12.1 fusion.27
  1619.4 13.0 multiply_reduce_fusion.2
  1663.8 20.4 collective-permute-done.6
  1684.4 24.2 multiply_convert_fusion.3
  1719.8 12.7 multiply_reduce_fusion.1
  1764.3 19.5 collective-permute-done.8
  1784.1 24.0 multiply_convert_fusion.1
  1820.1 13.0 multiply_reduce_fusion
  1860.2 31.0 convolution_convert_fusion.2
  1892.9 22.2 convolution_convert_fusion.1
  1916.7 41.8 %convolution_convert_fusion = bf16[1536,13824]{1,0:T(8,128)(2,1)} fusion(bf16[256,6912]{1,0:T(8,128)(2,1)} %get-tuple-element.85, bf16[256,6912]{1,0:T(8,128)(2,1)} %get-tuple-element.84, bf16[256,6912]{1,0:T(8,128)(2,1)} %get-tuple-element.87, bf16[256,6912]{1,0:T(8,128)(2,1)} %get-tuple-element.86, bf16[256,6912]{1,0:T(8,128)(2,1)} %get-tuple-element.90, ...), kind=kOutput, calls=%fused_computation | convolution fusion | flops 32770621440 | bytes 66060288 | tf_op jit(solution)/shard_map/dot_general | solution.py:166
  1960.7 205.7 %reduce-scatter.8.cloned.1.call-done = bf16[384,4608]{1,0:T(8,128)(2,1)} async-done(((bf16[1536,4608]{1,0:T(8,128)(2,1)}), bf16[384,4608]{1,0:T(8,128)(2,1)}) %reduce-scatter.8.cloned.1.call-update) | async-done | bytes 3538960 | tf_op jit(solution)/shard_map/reduce_scatter | solution.py:250
  2166.4 354.8 %reduce-scatter.14.cloned.1.call-done = bf16[1728,1536]{1,0:T(8,128)(2,1)} async-done(((bf16[6912,1536]{1,0:T(8,128)(2,1)}), bf16[1728,1536]{1,0:T(8,128)(2,1)}) %reduce-scatter.14.cloned.1.call-update) | async-done | bytes 5308432 | tf_op jit(solution)/shard_map/reduce_scatter | solution.py:250
  2521.2 698.7 %reduce-scatter.12.cloned.1.call-done = bf16[384,13824]{1,0:T(8,128)(2,1)} async-done(((bf16[1536,13824]{1,0:T(8,128)(2,1)}), bf16[384,13824]{1,0:T(8,128)(2,1)}) %reduce-scatter.12.cloned.1.call-update) | async-done | bytes 10616848 | tf_op jit(solution)/shard_map/reduce_scatter | solution.py:250
  3246.7 18.9 all-reduce.2
  3280.0 321.7 %all-reduce.7.cloned.1.call-done = (bf16[1,384,4608]{2,1,0:T(8,128)(2,1)}, bf16[1,384,1536]{2,1,0:T(8,128)(2,1)}, bf16[384,13824]{1,0:T(8,128)(2,1)}, bf16[1,1728,1536]{2,1,0:T(8,128)(2,1)}) async-done(((bf16[1,384,4608]{2,1,0:T(8,128)(2,1)}, bf16[1,384,1536]{2,1,0:T(8,128)(2,1)}, bf16[384,13824]{1,0:T(8,128)(2,1)}, bf16[1,1728,1536]{2,1,0:T(8,128)(2,1)}), (bf16[1,384,4608]{2,1,0:T(8,128)(2,1)}, ...) | async-done | bytes 20643856 | tf_op jit(solution)/shard_map/psum | solution.py:261
  (360 shorter events, 290.7 us)
Async XLA Ops:
  7.2 249.3 %all-gather.14.cloned.1.call-start = ((), (), s32[]{:S(2)}) async-start(), calls=%async_computation.9 | async-start | bytes 17694720 | tf_op jit(solution)/shard_map/all_gather | solution.py:188
  7.9 337.8 %all-gather.16.cloned.1.call-start = ((), (), s32[]{:S(2)}) async-start(), calls=%async_computation.10 | async-start | bytes 5898240 | tf_op jit(solution)/shard_map/all_gather | solution.py:190
  8.7 698.3 %all-gather.18.cloned.1.call-start = ((), (), s32[]{:S(2)}) async-start(), calls=%async_computation.11 | async-start | bytes 26542080 | tf_op jit(solution)/shard_map/all_gather | solution.py:191
  9.4 1058.7 %all-gather.20.cloned.1.call-start = ((), (), s32[]{:S(2)}) async-start(), calls=%async_computation.12 | async-start | bytes 26542080 | tf_op jit(solution)/shard_map/all_gather | solution.py:192
  10.0 56.2 %copy-start.8 = (bf16[2,1,256,1536]{3,2,1,0:T(8,128)(2,1)S(1)}, bf16[2,1,256,1536]{3,2,1,0:T(8,128)(2,1)}, u32[]{:S(2)}) copy-start(bf16[2,1,256,1536]{3,2,1,0:T(8,128)(2,1)} %param.10) | copy-start | bytes 4718596
  10.0 1419.2 %all-gather.22.cloned.1.call-start = ((), (), s32[]{:S(2)}) async-start(), calls=%async_computation.13 | async-start | bytes 26542080 | tf_op jit(solution)/shard_map/all_gather | solution.py:193
  10.6 1950.1 %reduce-scatter.10.cloned.1.call-start = ((), (), s32[]{:S(2)}) async-start(), calls=%async_computation.6 | async-start | bytes 5898240 | tf_op jit(solution)/shard_map/reduce_scatter | solution.py:250
  66.2 1693.4 %copy-start.62 = (f32[1536]{0:T(1024)}, f32[1536]{0:T(1024)S(1)}, u32[]{:S(2)}) copy-start(f32[1536]{0:T(1024)S(1)} %convert_reduce_fusion.1) | copy-start | bytes 18436
  67.1 196.4 %copy-start.67 = (f32[256]{0:T(256)}, f32[256]{0:T(256)S(1)}, u32[]{:S(2)}) copy-start(f32[256]{0:T(256)S(1)} %get-tuple-element.95) | copy-start | bytes 3076
  67.4 196.2 %copy-start.41 = (bf16[256,1536]{1,0:T(8,128)(2,1)}, bf16[256,1536]{1,0:T(8,128)(2,1)S(1)}, u32[]{:S(2)}) copy-start(bf16[256,1536]{1,0:T(8,128)(2,1)S(1)} %fusion.198) | copy-start | bytes 2359300
  263.8 2.8 collective-permute-start
  349.8 1079.4 %copy-start.21 = (f32[256,1536]{1,0:T(8,128)}, f32[256,1536]{1,0:T(8,128)S(1)}, u32[]{:S(2)}) copy-start(f32[256,1536]{1,0:T(8,128)S(1)} %get-tuple-element.107) | copy-start | bytes 4718596
  350.4 371.9 %copy-start.71 = (f32[256]{0:T(256)}, f32[256]{0:T(256)S(1)}, u32[]{:S(2)}) copy-start(f32[256]{0:T(256)S(1)} %get-tuple-element.97) | copy-start | bytes 3076
  1429.2 32.6 slice-start.6
  1429.2 32.6 slice-start.7
  1429.2 32.6 slice-start.8
  1429.2 32.6 slice-start.9
  1440.4 20.2 collective-permute-start.1
  1465.9 2.1 collective-permute-start.2
  1473.2 31.0 copy-start.24
  1516.1 21.4 collective-permute-start.3
  1548.5 16.3 collective-permute-start.4
  1641.2 4.0 collective-permute-start.5
  1662.5 21.7 collective-permute-start.6
  1741.8 4.2 collective-permute-start.7
  1762.9 21.0 collective-permute-start.8
  1843.0 323.4 %reduce-scatter.8.cloned.1.call-start = ((), (), s32[]{:S(2)}) async-start(), calls=%async_computation.5 | async-start | bytes 17694720 | tf_op jit(solution)/shard_map/reduce_scatter | solution.py:250
  1851.4 3.9 collective-permute-start.9
  1891.2 629.9 %reduce-scatter.14.cloned.1.call-start = ((), (), s32[]{:S(2)}) async-start(), calls=%async_computation.8 | async-start | bytes 26542080 | tf_op jit(solution)/shard_map/reduce_scatter | solution.py:250
  1915.1 1304.8 %reduce-scatter.12.cloned.1.call-start = ((), (), s32[]{:S(2)}) async-start(), calls=%async_computation.7 | async-start | bytes 53084160 | tf_op jit(solution)/shard_map/reduce_scatter | solution.py:250
  1958.6 1311.8 %reduce-scatter.16.cloned.1.call-start = ((), (), s32[]{:S(2)}) async-start(), calls=%async_computation.14 | async-start | bytes 983040
  1960.6 1641.1 %all-reduce.7.cloned.1.call-start = ((), (), s32[]{:S(2)}) async-start(), calls=%async_computation.15 | async-start | bytes 41287680 | tf_op jit(solution)/shard_map/psum | solution.py:261
  (93 other events, 696.9 us)
Sparse Core Ops, SparseCore 0:
  9.6 246.8 all-gather.13
  258.1 87.6 all-gather.15
  347.3 359.5 all-gather.17
  708.4 359.6 all-gather.19
  1069.5 359.6 all-gather.21
  1843.1 83.0 reduce-scatter.9
  1928.6 237.7 reduce-scatter.7
  2168.7 352.3 reduce-scatter.13
  2523.7 696.1 reduce-scatter.11
  3222.6 24.7 reduce-scatter.15
  3250.2 351.4 all-reduce.6
where the time goes:
time: 3640 us
  waiting for transfers between devices  2970 us (82%)
  matrix products  445 us (12%)
  blocking collectives  81.2 us (2%)
  other arithmetic  69.5 us (2%)
    reduce_scatter x4, waiting for transfers between devices, reduce_rows(): lax.psum_scatter(row_products(left, right).astype(jnp.bfloat16), 'fsdp',...  1260 us
    all_gather x1, waiting for transfers between devices, body(): lax.all_gather(gate_weight[0], 'fsdp', axis=0, tiled=True)  355 us
    all_gather x1, waiting for transfers between devices, body(): lax.all_gather(up_weight[0], 'fsdp', axis=0, tiled=True)  346 us
    all_gather x1, waiting for transfers between devices, body(): lax.all_gather(down_weight[0], 'fsdp', axis=0, tiled=True)  343 us
    psum x1, waiting for transfers between devices, body(): lax.psum(matrices[0].astype(jnp.bfloat16), 'seq').astype(jnp.float32)  322 us
    all_gather x1, waiting for transfers between devices, body(): lax.all_gather(in_weight[0], 'fsdp', axis=0, tiled=True)  189 us
    dot_general x15, matrix products, times_transposed(): lax.dot_general(left, matrix, (((1,), (1,)), ((), ())), preferred_element...  186 us
    dot_general x4, matrix products, row_products(): lax.dot_general(left, right, (((0,), (0,)), ((), ())), preferred_element_...  101 us
  transfers between devices with their start and end apart: 21, of which 18 were waited for; matrix products, arithmetic and copies ran while one was open for 6% of the time, Pallas kernels for 0%

commit v1 on v0

v1 whole, which is shorter than its diff:
```python
import jax
import jax.numpy as jnp
from jax import lax
from jax.sharding import PartitionSpec as P

EPSILON = 1e-05
PLANE = ("section", "seq")


def flip(value, bits):
    count = lax.axis_size("section") * lax.axis_size("seq")
    return lax.ppermute(value, PLANE, [(source, source ^ bits) for source in range(count)])


def flip_by_core(value, even_bits, odd_bits):
    count = lax.axis_size("section") * lax.axis_size("seq")
    pairs = [(source, source ^ (odd_bits if source & 1 else even_bits)) for source in range(count)]
    return lax.ppermute(value, PLANE, pairs)


def chip_bits():
    bits = [lax.axis_size("seq")]
    step = lax.axis_size("seq") // 2
    while step > 1:
        bits.append(step)
        step //= 2
    return bits


def half_units():
    units = [0]
    for bits in chip_bits():
        units = units + [unit | bits for unit in units]
    return units


def spread_chips(own, odd):
    bits = chip_bits()
    if len(bits) == 2:
        first = flip(own, bits[0])
        second = flip(own, bits[1])
        third = flip_by_core(jnp.where(odd, second, first), bits[1], bits[0])
        return jnp.concatenate([own, first, second, third], 0)
    held = own
    for step in bits:
        held = jnp.concatenate([held, flip(held, step)], 0)
    return held


def spread(own, odd):
    near = spread_chips(own, odd)
    return near, flip(near, 1)


def collect(near, far, odd):
    bits = chip_bits()
    if len(bits) == 2:
        rows = near.shape[0] // 4
        held = near
        third = flip_by_core(held[3 * rows :].astype(jnp.bfloat16), bits[1], bits[0]).astype(jnp.float32)
        first = held[rows : 2 * rows] + jnp.where(odd, 0.0, third)
        second = held[2 * rows : 3 * rows] + jnp.where(odd, third, 0.0)
        first = flip(first.astype(jnp.bfloat16), bits[0]).astype(jnp.float32)
        second = flip(second.astype(jnp.bfloat16), bits[1]).astype(jnp.float32)
        return held[:rows] + first + second
    held = near
    for step in reversed(bits):
        rows = held.shape[0] // 2
        held = held[:rows] + flip(held[rows:].astype(jnp.bfloat16), step).astype(jnp.float32)
    return held


def rms_scale(stream):
    return lax.rsqrt(jnp.mean(stream * stream, -1, keepdims=True) + EPSILON)


def times(left, matrix):
    return jnp.dot(left, matrix, preferred_element_type=jnp.float32)


def times_transposed(left, matrix):
    return lax.dot_general(
        left, matrix, (((1,), (1,)), ((), ())), preferred_element_type=jnp.float32
    )


def row_products(left, right):
    return lax.dot_general(
        left, right, (((0,), (0,)), ((), ())), preferred_element_type=jnp.float32
    ).astype(jnp.bfloat16)


def normed_with(stream, gain):
    return (stream * rms_scale(stream) * gain).astype(jnp.bfloat16)


def pick_columns(matrix, share, width, count):
    shards = lax.axis_size("fsdp")
    part = width // shards // count
    return jnp.concatenate(
        [
            lax.dynamic_slice(
                matrix, (0, start + shard * (width // shards) + share * part), (matrix.shape[0], part)
            )
            for start in range(0, matrix.shape[1], width)
            for shard in range(shards)
        ],
        1,
    )


def pick_rows(matrix, share, count):
    part = matrix.shape[0] // count
    return lax.dynamic_slice(matrix, (share * part, 0), (part, matrix.shape[1]))


def body(
    tokens,
    in_weight,
    conv_kernel,
    out_weight,
    gate_weight,
    up_weight,
    down_weight,
    mixer_gain,
    ffn_gain,
    cotangent,
):
    bf16, f32 = jnp.bfloat16, jnp.float32
    x_index = lax.axis_index("section")
    q_index = lax.axis_index("seq")
    seq_count = lax.axis_size("seq")
    count = lax.axis_size("section") * seq_count
    shards = lax.axis_size("fsdp")
    share = x_index * seq_count + q_index
    odd = (q_index % 2) == 1
    first_plane = x_index == 0
    width = tokens.shape[3]
    rows = tokens.shape[2]
    hidden_width = gate_weight.shape[2]
    shard_rows = width // shards
    units = half_units()
    half = len(units)

    small = jnp.concatenate(
        [mixer_gain, ffn_gain, conv_kernel[0].T], 0
    )
    small = lax.all_gather(small, ("section", "fsdp"), axis=0)
    small = small.reshape(2, shards, 5, shard_rows).transpose(0, 2, 1, 3).astype(f32)
    whole = small.reshape(2, 5, width)
    part = shard_rows // count
    taps_all = lax.dynamic_slice(
        small[:, 2:].reshape(2, 3, shards, count, part),
        (0, 0, 0, share, 0),
        (2, 3, shards, 1, part),
    ).reshape(2, 3, shards * part)

    other = share ^ seq_count

    def by_block(make):
        kept, sent = make(share), flip(make(other), seq_count)
        return jnp.where(first_plane, kept, sent), jnp.where(first_plane, sent, kept)

    def mixer_share(index):
        columns = pick_columns(in_weight[0], index, width, count)
        return jnp.concatenate(
            [columns, pick_rows(out_weight[0], index, count).reshape(shard_rows, -1)], 1
        )

    def ffn_share(index):
        return jnp.concatenate(
            [
                pick_columns(gate_weight[0], index, hidden_width, count),
                pick_columns(up_weight[0], index, hidden_width, count),
            ],
            1,
        )

    def down_share(index):
        return pick_rows(down_weight[0], index, count)

    in_columns = 3 * width // count
    ffn_columns = hidden_width // count
    mixer_parts = by_block(mixer_share)
    ffn_parts = by_block(ffn_share)
    down_parts = by_block(down_share)
    weights = []
    for block in range(2):
        mixer = lax.all_gather(mixer_parts[block], "fsdp", axis=0, tiled=True)
        pair = lax.all_gather(ffn_parts[block], "fsdp", axis=0, tiled=True)
        down = lax.all_gather(down_parts[block], "fsdp", axis=0, tiled=True)
        out = mixer[:, in_columns:].reshape(-1, width)
        weights.append((mixer[:, :in_columns], out, pair, down))

    near_ids = jnp.stack([share ^ unit for unit in units])
    far_ids = near_ids ^ 1
    ids = jnp.concatenate([near_ids, far_ids])
    has_before = (ids % seq_count) > 0
    has_after = (ids % seq_count) < seq_count - 1
    before_pick = (ids[None, :] == (ids - 1)[:, None]) & has_before[:, None]
    after_pick = (ids[None, :] == (ids + 1)[:, None]) & has_after[:, None]

    def pick_units(mask, edge):
        return jnp.sum(jnp.where(mask[:, :, None, None], edge[None].astype(f32), 0.0), 1)

    mine = lax.dynamic_index_in_dim(tokens[:, 0], x_index, 0, False)
    theirs = lax.dynamic_index_in_dim(tokens[:, 0], 1 - x_index, 0, False)

    def spread_replicated(mine, theirs):
        near = jnp.concatenate([mine, theirs], 0)
        for step in chip_bits()[1:]:
            near = jnp.concatenate([near, flip(near, step)], 0)
        return near, flip(near, 1)

    entry = spread_replicated(mine, theirs)
    stream = mine.astype(f32)
    saved = []
    outputs = []
    for block in range(2):
        in_matrix, out_matrix, pair_matrix, down_matrix = weights[block]
        mixer_scale, ffn_scale = whole[block, 0], whole[block, 1]
        taps = taps_all[block]
        if block == 0:
            normed = [normed_with(piece.astype(f32), mixer_scale) for piece in entry]
        else:
            normed = spread(normed_with(stream, mixer_scale), odd)
        projected = jnp.concatenate([times(piece, in_matrix) for piece in normed], 0)
        channels = in_columns // 3
        b_gate = projected[:, :channels]
        c_gate = projected[:, channels : 2 * channels]
        x_value = projected[:, 2 * channels :]
        conv_input = (b_gate * x_value).astype(bf16).reshape(2 * half, rows, channels)
        earlier = pick_units(before_pick, conv_input[:, -2:])
        extended = jnp.concatenate([earlier, conv_input.astype(f32)], 1)
        conv_out = (
            taps[0] * extended[:, :-2] + taps[1] * extended[:, 1:-1] + taps[2] * extended[:, 2:]
        )
        c_units = c_gate.reshape(2 * half, rows, channels)
        gated = (c_units * conv_out).astype(bf16).reshape(2, half * rows, channels)
        far = flip(times(gated[1], out_matrix).astype(bf16), 1).astype(f32)
        near = times(gated[0], out_matrix) + far
        middle = stream + collect(near, None, odd)
        scale_ffn = rms_scale(middle)
        normed_ffn = spread((middle * scale_ffn * ffn_scale).astype(bf16), odd)
        pairs = [times(piece, pair_matrix) for piece in normed_ffn]
        hidden = [
            (jax.nn.silu(piece[:, :ffn_columns]) * piece[:, ffn_columns:]).astype(bf16)
            for piece in pairs
        ]
        far = flip(times(hidden[1], down_matrix).astype(bf16), 1).astype(f32)
        near = times(hidden[0], down_matrix) + far
        result = middle + collect(near, None, odd)
        outputs.append(result.astype(bf16))
        saved.append(
            (stream, normed, projected, extended, conv_out, gated, middle, scale_ffn, normed_ffn, pairs, hidden)
        )
        stream = result.astype(bf16).astype(f32)

    mine = lax.dynamic_index_in_dim(cotangent[:, 0], x_index, 0, False)
    theirs = lax.dynamic_index_in_dim(cotangent[:, 0], 1 - x_index, 0, False)
    upstream = mine.astype(f32)
    grad_units = spread_replicated(mine, theirs)
    stream_grads = [None, None]
    small_grads = [None, None]
    matrix_grads = [None, None]

    def over_z(value):
        return lax.psum_scatter(value, "fsdp", scatter_dimension=0, tiled=True)

    for block in (1, 0):
        in_matrix, out_matrix, pair_matrix, down_matrix = weights[block]
        mixer_scale, ffn_scale = whole[block, 0], whole[block, 1]
        taps = taps_all[block]
        (stream, normed, projected, extended, conv_out, gated, middle, scale_ffn, normed_ffn, pairs, hidden) = saved[block]
        down_grad = over_z(row_products(jnp.concatenate(hidden, 0), jnp.concatenate(grad_units, 0)))
        grad_pairs = []
        for piece, grad in zip(pairs, grad_units):
            gate_value, up_value = piece[:, :ffn_columns], piece[:, ffn_columns:]
            grad_hidden = times_transposed(grad, down_matrix)
            sigmoid_gate = jax.nn.sigmoid(gate_value)
            grad_gate = (
                grad_hidden * up_value * sigmoid_gate * (1.0 + gate_value * (1.0 - sigmoid_gate))
            ).astype(bf16)
            grad_up = (grad_hidden * gate_value * sigmoid_gate).astype(bf16)
            grad_pairs.append(jnp.concatenate([grad_gate, grad_up], 1))
        far = flip(times_transposed(grad_pairs[1], pair_matrix).astype(bf16), 1).astype(f32)
        near = times_transposed(grad_pairs[0], pair_matrix) + far
        grad_normed_ffn = collect(near, None, odd)
        pair_grad = over_z(
            row_products(jnp.concatenate(normed_ffn, 0), jnp.concatenate(grad_pairs, 0))
        )
        ffn_gain_part = jnp.sum(grad_normed_ffn * middle * scale_ffn, 0)
        weighted_ffn = ffn_scale * grad_normed_ffn
        grad_middle = (
            upstream
            + scale_ffn * weighted_ffn
            - middle * scale_ffn**3 * jnp.mean(weighted_ffn * middle, -1, keepdims=True)
        )
        mixer_grad = spread(grad_middle.astype(bf16), odd)
        grad_gated = jnp.concatenate(
            [times_transposed(piece, out_matrix) for piece in mixer_grad], 0
        ).reshape(2 * half, rows, channels)
        b_gate = projected[:, :channels].reshape(2 * half, rows, channels)
        c_gate = projected[:, channels : 2 * channels].reshape(2 * half, rows, channels)
        x_value = projected[:, 2 * channels :].reshape(2 * half, rows, channels)
        grad_cgate = grad_gated * conv_out
        grad_conv = grad_gated * c_gate
        later = pick_units(after_pick, grad_conv[:, :2])
        grad_extended = jnp.concatenate([grad_conv, later], 1)
        grad_input = (
            taps[0] * grad_extended[:, 2:]
            + taps[1] * grad_extended[:, 1:-1]
            + taps[2] * grad_extended[:, :-2]
        )
        taps_part = jnp.stack(
            [jnp.sum(grad_conv * extended[:, tap : tap + rows], (0, 1)) for tap in range(3)], 0
        )
        grad_projected = (
            jnp.concatenate([grad_input * x_value, grad_cgate, grad_input * b_gate], 2)
            .astype(bf16)
            .reshape(2, half * rows, in_columns)
        )
        far = flip(times_transposed(grad_projected[1], in_matrix).astype(bf16), 1).astype(f32)
        near = times_transposed(grad_projected[0], in_matrix) + far
        grad_normed = collect(near, None, odd)
        in_grad = row_products(
            jnp.concatenate(normed, 0), grad_projected.reshape(2 * half * rows, in_columns)
        )
        out_grad = row_products(
            gated.reshape(2 * half * rows, channels), jnp.concatenate(mixer_grad, 0)
        )
        mixer_sum = over_z(jnp.concatenate([in_grad, out_grad.reshape(width, -1)], 1))
        scale_mix = rms_scale(stream)
        mixer_gain_part = jnp.sum(grad_normed * stream * scale_mix, 0)
        weighted_mix = mixer_scale * grad_normed
        grad_stream = (
            grad_middle
            + scale_mix * weighted_mix
            - stream * scale_mix**3 * jnp.mean(weighted_mix * stream, -1, keepdims=True)
        )
        stream_grads[block] = grad_stream
        own_mask = (jnp.arange(count) == share)[None, None, :, None]
        taps_placed = jnp.where(own_mask, taps_part.reshape(3, shards, 1, part), 0.0)
        small_grads[block] = jnp.concatenate(
            [mixer_gain_part[None], ffn_gain_part[None], taps_placed.reshape(3, width)], 0
        )
        matrix_grads[block] = (down_grad, pair_grad, mixer_sum)
        if block == 1:
            sent = grad_stream.astype(bf16)
            upstream = sent.astype(f32)
            grad_units = spread(sent, odd)

    section_count = lax.axis_size("section")

    def to_owners(value, block):
        over = [
            ((1 - block) * seq_count + seq, block * seq_count + seq) for seq in range(seq_count)
        ]
        units_held = jnp.stack([value, lax.ppermute(value, PLANE, over)], 0)
        step = 1
        inside = chip_bits()[1:] + [1]
        for bits in inside:
            pairs = [
                (block * seq_count + seq, block * seq_count + (seq ^ bits))
                for seq in range(seq_count)
            ]
            units_held = jnp.concatenate([units_held, lax.ppermute(units_held, PLANE, pairs)], 0)
        return units_held

    def both_owners(index):
        first = to_owners(matrix_grads[0][index], 0)
        second = to_owners(matrix_grads[1][index], 1)
        return jnp.where(first_plane, first, second)

    relative = [0, seq_count]
    for bits in chip_bits()[1:] + [1]:
        relative = relative + [unit | bits for unit in relative]
    position = {unit: place for place, unit in enumerate(relative)}
    order = jnp.stack([jnp.int32(0)] * 0 + [jnp.int32(position[unit]) for unit in range(count)])
    absolute = order[jnp.arange(count) ^ share]

    def in_order(value):
        return jnp.take(value, absolute, axis=0)

    def columns_of(value, blocks):
        piece = value.reshape(count, shard_rows, blocks, shards, -1)
        return piece.transpose(1, 2, 3, 0, 4).reshape(shard_rows, -1).astype(f32)

    down_grad = in_order(both_owners(0)).reshape(-1, width).astype(f32)
    pair_grad = in_order(both_owners(1))
    gate_grad = columns_of(pair_grad[..., :ffn_columns], 1)
    up_grad = columns_of(pair_grad[..., ffn_columns:], 1)
    mixer_sum = in_order(both_owners(2))
    in_grad = columns_of(mixer_sum[..., :in_columns], 3)
    out_grad = mixer_sum[..., in_columns:].reshape(shard_rows, width).astype(f32)

    smalls = lax.psum(jnp.stack(small_grads), ("section", "seq", "fsdp"))
    smalls = lax.dynamic_slice(
        smalls, (x_index, 0, lax.axis_index("fsdp") * shard_rows), (1, 5, shard_rows)
    )[0]

    def by_slot(values, dtype):
        kept = jnp.where(first_plane, values[0], values[1]).astype(dtype)
        sent = jnp.where(first_plane, values[1], values[0]).astype(bf16)
        other = flip(sent, seq_count).astype(dtype)
        return jnp.stack(
            [jnp.where(first_plane, kept, other), jnp.where(first_plane, other, kept)], 0
        )

    return (
        by_slot(outputs, bf16)[None, :, None],
        by_slot(stream_grads, f32)[None, :, None],
        in_grad[None],
        smalls[2:].T[None],
        out_grad[None],
        gate_grad[None],
        up_grad[None],
        down_grad[None],
        smalls[0][None],
        smalls[1][None],
    )


def solution(mesh):
    placed = (
        P(None, "fsdp", "seq", None),
        P("section", "fsdp", None),
        P("section", "fsdp", None),
        P("section", "fsdp", None),
        P("section", "fsdp", None),
        P("section", "fsdp", None),
        P("section", "fsdp", None),
        P("section", "fsdp"),
        P("section", "fsdp"),
        P(None, "fsdp", "seq", None),
    )
    return jax.shard_map(
        body,
        mesh=mesh,
        in_specs=placed,
        out_specs=(
            P("section", None, "fsdp", "seq", None),
            P("section", None, "fsdp", "seq", None),
            P("section", "fsdp", None),
            P("section", "fsdp", None),
            P("section", "fsdp", None),
            P("section", "fsdp", None),
            P("section", "fsdp", None),
            P("section", "fsdp", None),
            P("section", "fsdp"),
            P("section", "fsdp"),
        ),
        check_vma=False,
    )
```

time: 3640 us -> 1610 us (0.44)
  waiting for transfers between devices: 2970 us -> 668 us
  local copies, waits for them, and re-layouts: 26.2 us -> 268 us
  matrix products: 445 us -> 249 us
  other arithmetic: 69.5 us -> 215 us
  starting transfers between devices: 24 us -> 108 us
    reduce_scatter x4 -> x2, waiting for transfers between devices: 1260 us -> 0.02 us  [over_z(): return lax.psum_scatter(value, 'fsdp', scatter_dimension=0, tiled=True)]
    all_gather x5 -> x6, waiting for transfers between devices: 1310 us -> 117 us  [the longest x2 74.2 us: body(): down = lax.all_gather(down_parts[block], 'fsdp', axis=0, tiled=True)]
    ppermute x10 -> x83, waiting for transfers between devices: 81.2 us -> 550 us  [the longest x51 338 us: flip(): lax.ppermute(value, PLANE, [(source, source ^ bits) for source in range(c...]
    psum x1 -> x0, waiting for transfers between devices: 322 us -> none  [body(): lax.psum(matrices[0].astype(jnp.bfloat16), 'seq').astype(jnp.float32)]
    unnamed x214 -> x461, local copies, waits for them, and re-layouts: 18.3 us -> 134 us
    dot_general x15 -> x16, matrix products: 186 us -> 95.9 us  [times_transposed(): lax.dot_general(left, matrix, (((1,), (1,)), ((), ())), preferred_element...]
    ppermute x10 -> x83, starting transfers between devices: 23 us -> 106 us  [the longest x51 46.4 us: flip(): lax.ppermute(value, PLANE, [(source, source ^ bits) for source in range(c...]
    dot_general x15 -> x16, matrix products: 158 us -> 80.1 us  [times(): return jnp.dot(left, matrix, preferred_element_type=jnp.float32)]
  transfers between devices with their start and end apart: 21 -> 95, of which waited for: 18 -> 53; matrix products, arithmetic and copies ran while one was open for 6% -> 32% of each run, Pallas kernels for 0% -> 0%
where the time goes in v1:
time: 1610 us; the launch traced here: 1600 us
  waiting for transfers between devices  668 us (41%)
  local copies, waits for them, and re-layouts  268 us (17%)
  matrix products  249 us (15%)
  other arithmetic  215 us (13%)
  starting transfers between devices  108 us (7%)
  blocking collectives  71.2 us (4%)
  between operations  17.7 us (1%)
    ppermute x51, waiting for transfers between devices, flip(): lax.ppermute(value, PLANE, [(source, source ^ bits) for source in range(c...  338 us
    unnamed x461, local copies, waits for them, and re-layouts  134 us
    ppermute x14, waiting for transfers between devices, flip_by_core(): return lax.ppermute(value, PLANE, pairs)  123 us
    dot_general x16, matrix products, times_transposed(): lax.dot_general(left, matrix, (((1,), (1,)), ((), ())), preferred_element...  95.9 us
    dot_general x16, matrix products, times(): return jnp.dot(left, matrix, preferred_element_type=jnp.float32)  80.1 us
    all_gather x2, waiting for transfers between devices, body(): down = lax.all_gather(down_parts[block], 'fsdp', axis=0, tiled=True)  74.2 us
    dot_general x8, matrix products, row_products(): lax.dot_general(left, right, (((0,), (0,)), ((), ())), preferred_element_...  73.2 us
    ppermute x6, waiting for transfers between devices, to_owners(): units_held = jnp.stack([value, lax.ppermute(value, PLANE, over)], 0)  58.6 us
  transfers between devices with their start and end apart: 95, of which 53 were waited for; matrix products, arithmetic and copies ran while one was open for 32% of the time, Pallas kernels for 0%

profile of v1, /device:TPU:0, one launch (start us, length us, event | category | flops | bytes accessed | tf_op | source)
XLA Modules:
  0.0 1597.6 jit_solution(6366856290375755836)
XLA Ops:
  26.8 11.5 collective-permute-done.1
  52.5 31.4 %all-gather.1 = bf16[8,5,384]{2,1,0:T(8,128)(2,1)S(1)} all-gather(bf16[1,5,384]{2,1,0:T(8,128)(2,1)S(1)} %maximum_bitcast_fusion.4), channel_id=2, replica_groups=mesh['section'=2,'seq'=4,'fsdp'=4] {'section','fsdp'}, dimensions={0}, use_global_device_ids=true | all-gather | bytes 34560 | tf_op jit(solution)/shard_map/all_gather | solution.py:148
  129.6 28.7 %collective-permute-done.10 = bf16[384,1728]{0,1:T(8,128)(2,1)} collective-permute-done((bf16[384,1728]{0,1:T(8,128)(2,1)}, bf16[384,1728]{0,1:T(8,128)(2,1)}, u32[]{:S(2)}, u32[]{:S(2)}) %collective-permute-start.10) | collective-permute-done | bytes 1327136 | tf_op jit(solution)/shard_map/ppermute | solution.py:12
  185.2 15.3 collective-permute-done.5
  207.0 15.4 collective-permute-done.7
  250.7 11.1 all-gather.11.cloned.1.call-done
  275.8 42.0 %all-gather.13.cloned.1.call-done = bf16[864,1536]{1,0:T(8,128)(2,1)} async-done(((bf16[216,1536]{1,0:T(8,128)(2,1)}), bf16[864,1536]{1,0:T(8,128)(2,1)}) %all-gather.13.cloned.1.call-update) | async-done | bytes 2654224 | tf_op jit(solution)/shard_map/all_gather | solution.py:191
  354.6 16.1 %collective-permute-done.15 = bf16[256,1536]{1,0:T(8,128)(2,1)S(1)} collective-permute-done((bf16[256,1536]{1,0:T(8,128)(2,1)S(1)}, bf16[256,1536]{1,0:T(8,128)(2,1)S(1)}, u32[]{:S(2)}, u32[]{:S(2)}) %collective-permute-start.15) | collective-permute-done | bytes 786464 | tf_op jit(solution)/shard_map/ppermute | solution.py:12
  375.4 15.8 collective-permute-done.17
  413.6 31.7 %all-gather.15.cloned.1.call-done = bf16[1536,768]{1,0:T(8,128)(2,1)} async-done(((bf16[384,768]{1,0:T(8,128)(2,1)}), bf16[1536,768]{1,0:T(8,128)(2,1)}) %all-gather.15.cloned.1.call-update) | async-done | bytes 2359312 | tf_op jit(solution)/shard_map/all_gather | solution.py:189
  496.2 15.9 collective-permute-done.23
  516.2 15.7 collective-permute-done.25
  537.4 15.2 collective-permute-done.27
  554.6 23.7 %collective-permute-done.34 = bf16[512,1536]{1,0:T(8,128)(2,1)} collective-permute-done((bf16[512,1536]{1,0:T(8,128)(2,1)}, bf16[512,1536]{1,0:T(8,128)(2,1)}, u32[]{:S(2)}, u32[]{:S(2)}) %collective-permute-start.34) | collective-permute-done | bytes 1572896 | tf_op jit(solution)/shard_map/ppermute | solution.py:12
  592.6 32.2 %all-gather.19.cloned.1.call-done = bf16[864,1536]{1,0:T(8,128)(2,1)} async-done(((bf16[216,1536]{1,0:T(8,128)(2,1)}), bf16[864,1536]{1,0:T(8,128)(2,1)}) %all-gather.19.cloned.1.call-update) | async-done | bytes 2654224 | tf_op jit(solution)/shard_map/all_gather | solution.py:191
  736.3 15.7 collective-permute-done.40
  802.6 20.9 %convolution_convert_fusion = bf16[1536,1728]{0,1:T(8,128)(2,1)} fusion(bf16[2048,1536]{1,0:T(8,128)(2,1)S(1)} %bitcast.473, bf16[1024,864]{0,1:T(8,128)(2,1)} %copy-done.179, bf16[1024,864]{0,1:T(8,128)(2,1)} %copy-done.178, bf16[1024,864]{0,1:T(8,128)(2,1)} %get-tuple-element.166, bf16[1024,864]{0,1:T(8,128)(2,1)S(1)} %copy-done.172), kind=kOutput, calls=%fused_computation.12 | convolution fusion | flops 10902601728 | bytes 18677760 | tf_op jit(solution)/shard_map/dot_general | solution.py:88
  854.9 17.4 %collective-permute-done.46 = bf16[256,1536]{1,0:T(8,128)(2,1)S(1)} collective-permute-done((bf16[256,1536]{1,0:T(8,128)(2,1)S(1)}, bf16[256,1536]{1,0:T(8,128)(2,1)S(1)}, u32[]{:S(2)}, u32[]{:S(2)}) %collective-permute-start.46) | collective-permute-done | bytes 786464 | tf_op jit(solution)/shard_map/ppermute | solution.py:12
  873.6 13.4 collective-permute-done.33
  891.1 15.8 collective-permute-done.48
  1021.0 11.0 collective-permute-done.54
  1041.0 20.7 %convolution_convert_fusion.1 = bf16[1536,1728]{0,1:T(8,128)(2,1)} fusion(bf16[2048,1536]{1,0:T(8,128)(2,1)S(1)} %bitcast.467, bf16[1024,864]{0,1:T(8,128)(2,1)} %copy-done.181, bf16[1024,864]{0,1:T(8,128)(2,1)} %copy-done.180, bf16[1024,864]{0,1:T(8,128)(2,1)} %copy-done.175, bf16[1024,864]{0,1:T(8,128)(2,1)S(1)} %copy-done.174), kind=kOutput, calls=%fused_computation.13 | convolution fusion | flops 10902601728 | bytes 18677760 | tf_op jit(solution)/shard_map/dot_general | solution.py:88
  1072.4 11.5 collective-permute-done.58
  1100.8 34.4 %collective-permute-done.80 = bf16[216,1536]{1,0:T(8,128)(2,1)S(1)} collective-permute-done((bf16[216,1536]{1,0:T(8,128)(2,1)}, bf16[216,1536]{1,0:T(8,128)(2,1)S(1)}, u32[]{:S(2)}, u32[]{:S(2)}) %collective-permute-start.80) | collective-permute-done | bytes 663584 | tf_op jit(solution)/shard_map/ppermute | solution.py:359
  1227.6 17.5 %collective-permute-done.78 = bf16[2,216,1536]{2,1,0:T(8,128)(2,1)} collective-permute-done((bf16[2,216,1536]{2,1,0:T(8,128)(2,1)}, bf16[2,216,1536]{2,1,0:T(8,128)(2,1)}, u32[]{:S(2)}, u32[]{:S(2)}) %collective-permute-start.78) | collective-permute-done | bytes 1327136 | tf_op jit(solution)/shard_map/ppermute | solution.py:367
  1274.1 24.2 %collective-permute-done.71 = bf16[384,1728]{0,1:T(8,128)(2,1)} collective-permute-done((bf16[384,1728]{0,1:T(8,128)(2,1)S(1)}, bf16[384,1728]{0,1:T(8,128)(2,1)}, u32[]{:S(2)}, u32[]{:S(2)}) %collective-permute-start.71) | collective-permute-done | bytes 1327136 | tf_op jit(solution)/shard_map/ppermute | solution.py:359
  1327.0 52.3 %collective-permute-done.63 = bf16[256,1536]{1,0:T(8,128)(2,1)} collective-permute-done((bf16[256,1536]{1,0:T(8,128)(2,1)}, bf16[256,1536]{1,0:T(8,128)(2,1)}, u32[]{:S(2)}, u32[]{:S(2)}) %collective-permute-start.63) | collective-permute-done | bytes 786464 | tf_op jit(solution)/shard_map/ppermute | solution.py:12
  1398.2 13.2 collective-permute-done.66
  1422.3 39.8 %psum.7 = f32[2,5,1536]{2,1,0:T(8,128)} all-reduce(f32[2,5,1536]{2,1,0:T(8,128)S(1)} %pad_maximum_fusion.34), channel_id=1, replica_groups=mesh['section'=2,'seq'=4,'fsdp'=4] {'section','seq','fsdp'}, use_global_device_ids=true, to_apply=%region_26.27 | all-reduce | flops 15360 | bytes 122880 | tf_op jit(solution)/shard_map/psum | solution.py:397
  1509.9 11.5 maximum_select_fusion
  1559.3 11.6 copy.230
  1578.9 11.6 copy.231
  (914 shorter events, 915.8 us)
Async XLA Ops:
  7.2 89.1 %all-gather.9.cloned.1.call-start = ((), (), s32[]{:S(2)}) async-start(), calls=%async_computation.6 | async-start | bytes 2949120 | tf_op jit(solution)/shard_map/all_gather | solution.py:189
  39.4 222.5 %all-gather.11.cloned.1.call-start = ((), (), s32[]{:S(2)}) async-start(), calls=%async_computation.7 | async-start | bytes 6635520 | tf_op jit(solution)/shard_map/all_gather | solution.py:190
  52.5 46.8 %collective-permute-start.2 = (bf16[1024,1536]{1,0:T(8,128)(2,1)}, bf16[1024,1536]{1,0:T(8,128)(2,1)}, u32[]{:S(2)}, u32[]{:S(2)}) collective-permute-start(bf16[1024,1536]{1,0:T(8,128)(2,1)} %get-tuple-element.158), channel_id=1, source_target_pairs={{0,4},{4,0},{8,12},{12,8},{16,20},{20,16},{24,28},{28,24},{1,5},{5... | collective-permute-start | bytes 9437192 | tf_op jit(solution)/shard_map/ppermute | solution.py:12
  161.4 156.3 %all-gather.13.cloned.1.call-start = ((), (), s32[]{:S(2)}) async-start(), calls=%async_computation.8 | async-start | bytes 3317760 | tf_op jit(solution)/shard_map/all_gather | solution.py:191
  250.7 194.6 %all-gather.15.cloned.1.call-start = ((), (), s32[]{:S(2)}) async-start(), calls=%async_computation.9 | async-start | bytes 2949120 | tf_op jit(solution)/shard_map/all_gather | solution.py:189
  396.9 185.0 %all-gather.17.cloned.1.call-start = ((), (), s32[]{:S(2)}) async-start(), calls=%async_computation.10 | async-start | bytes 6635520 | tf_op jit(solution)/shard_map/all_gather | solution.py:190
  471.4 153.4 %all-gather.19.cloned.1.call-start = ((), (), s32[]{:S(2)}) async-start(), calls=%async_computation.11 | async-start | bytes 3317760 | tf_op jit(solution)/shard_map/all_gather | solution.py:191
  554.6 531.3 %reduce-scatter.25.cloned.1.call-start = ((), (), s32[]{:S(2)}) async-start(), calls=%async_computation.17 | async-start | bytes 6881280
  581.8 43.0 %collective-permute-start.35 = (bf16[1024,1536]{1,0:T(8,128)(2,1)}, bf16[1024,1536]{1,0:T(8,128)(2,1)}, u32[]{:S(2)}, u32[]{:S(2)}) collective-permute-start(bf16[1024,1536]{1,0:T(8,128)(2,1)} %pad_maximum_fusion.6), channel_id=1, source_target_pairs={{0,4},{4,0},{8,12},{12,8},{16,20},{20,16},{24,28},{28,24},{1,5},{5... | collective-permute-start | bytes 9437192 | tf_op jit(solution)/shard_map/ppermute | solution.py:12
  831.4 260.5 %reduce-scatter.17.cloned.1.call-start = ((), (), s32[]{:S(2)}) async-start(), calls=%async_computation.13 | async-start | bytes 3317760 | tf_op jit(solution)/shard_map/reduce_scatter | solution.py:268
  935.5 206.8 %reduce-scatter.21.cloned.1.call-start = ((), (), s32[]{:S(2)}) async-start(), calls=%async_computation.15 | async-start | bytes 2949120
  973.3 177.4 %reduce-scatter.15.cloned.1.call-start = ((), (), s32[]{:S(2)}) async-start(), calls=%async_computation.12 | async-start | bytes 3317760 | tf_op jit(solution)/shard_map/reduce_scatter | solution.py:268
  1007.2 254.2 %reduce-scatter.23.cloned.1.call-start = ((), (), s32[]{:S(2)}) async-start(), calls=%async_computation.16 | async-start | bytes 6881280
  1069.8 235.6 %reduce-scatter.19.cloned.1.call-start = ((), (), s32[]{:S(2)}) async-start(), calls=%async_computation.14 | async-start | bytes 2949120
  1085.8 71.6 %collective-permute-start.59 = (bf16[1024,1536]{1,0:T(8,128)(2,1)}, bf16[1024,1536]{1,0:T(8,128)(2,1)}, u32[]{:S(2)}, u32[]{:S(2)}) collective-permute-start(bf16[1024,1536]{1,0:T(8,128)(2,1)} %pad_maximum_fusion.9), channel_id=1, source_target_pairs={{0,4},{4,0},{8,12},{12,8},{16,20},{20,16},{24,28},{28,24},{1,5},{5... | collective-permute-start | bytes 9437192 | tf_op jit(solution)/shard_map/ppermute | solution.py:12
  1088.5 49.7 %collective-permute-start.74 = (bf16[384,1728]{0,1:T(8,128)(2,1)S(1)}, bf16[384,1728]{0,1:T(8,128)(2,1)S(1)}, u32[]{:S(2)}, u32[]{:S(2)}) collective-permute-start(bf16[384,1728]{0,1:T(8,128)(2,1)S(1)} %copy.240), channel_id=1, source_target_pairs={{0,16},{4,20},{8,24},{12,28},{1,17},{5,21},{9,25},{13,29},{2,18},{... | collective-permute-start | bytes 3981320 | tf_op jit(solution)/shard_map/ppermute | solution.py:359
  1091.9 43.3 %collective-permute-start.80 = (bf16[216,1536]{1,0:T(8,128)(2,1)}, bf16[216,1536]{1,0:T(8,128)(2,1)S(1)}, u32[]{:S(2)}, u32[]{:S(2)}) collective-permute-start(bf16[216,1536]{1,0:T(8,128)(2,1)} %reduce-scatter.17.cloned.1.call-done), channel_id=1, source_target_pairs={{0,16},{4,20},{8,24},{12,28},{1,17},{5,21},{9,25},{13,29},{2,18},{... | collective-permute-start | bytes 1990664 | tf_op jit(solution)/shard_map/ppermute | solution.py:359
  1136.5 82.8 %collective-permute-start.81 = (bf16[2,216,1536]{2,1,0:T(8,128)(2,1)}, bf16[2,216,1536]{2,1,0:T(8,128)(2,1)}, u32[]{:S(2)}, u32[]{:S(2)}) collective-permute-start(bf16[2,216,1536]{2,1,0:T(8,128)(2,1)} %pad_maximum_fusion.31), channel_id=1, source_target_pairs={{16,24},{20,28},{24,16},{28,20},{17,25},{21,29},{25,17},{29,21},{1... | collective-permute-start | bytes 3981320 | tf_op jit(solution)/shard_map/ppermute | solution.py:367
  1140.2 110.1 %collective-permute-start.75 = (bf16[2,384,1728]{1,2,0:T(8,128)(2,1)}, bf16[2,384,1728]{1,2,0:T(8,128)(2,1)}, u32[]{:S(2)}, u32[]{:S(2)}) collective-permute-start(bf16[2,384,1728]{1,2,0:T(8,128)(2,1)} %pad_maximum_fusion.11), channel_id=1, source_target_pairs={{16,24},{20,28},{24,16},{28,20},{17,25},{21,29},{25,17},{29,21},{1... | collective-permute-start | bytes 7962632 | tf_op jit(solution)/shard_map/ppermute | solution.py:367
  1143.7 71.5 %collective-permute-start.68 = (bf16[384,768]{0,1:T(8,128)(2,1)S(1)}, bf16[384,768]{0,1:T(8,128)(2,1)}, u32[]{:S(2)}, u32[]{:S(2)}) collective-permute-start(bf16[384,768]{0,1:T(8,128)(2,1)S(1)} %copy.236), channel_id=1, source_target_pairs={{0,16},{4,20},{8,24},{12,28},{1,17},{5,21},{9,25},{13,29},{2,18},{... | collective-permute-start | bytes 1769480 | tf_op jit(solution)/shard_map/ppermute | solution.py:359
  1150.8 59.2 %collective-permute-start.77 = (bf16[216,1536]{1,0:T(8,128)(2,1)}, bf16[216,1536]{1,0:T(8,128)(2,1)}, u32[]{:S(2)}, u32[]{:S(2)}) collective-permute-start(bf16[216,1536]{1,0:T(8,128)(2,1)} %reduce-scatter.15.cloned.1.call-done), channel_id=1, source_target_pairs={{16,0},{20,4},{24,8},{28,12},{17,1},{21,5},{25,9},{29,13},{18,2},{... | collective-permute-start | bytes 1990664 | tf_op jit(solution)/shard_map/ppermute | solution.py:359
  1186.7 80.6 %collective-permute-start.60 = (bf16[1024,1536]{1,0:T(8,128)(2,1)}, bf16[1024,1536]{1,0:T(8,128)(2,1)}, u32[]{:S(2)}, u32[]{:S(2)}) collective-permute-start(bf16[1024,1536]{1,0:T(8,128)(2,1)} %convolution_convert_fusion.2), channel_id=1, source_target_pairs={{0,4},{4,0},{8,12},{12,8},{16,20},{20,16},{24,28},{28,24},{1,5},{5... | collective-permute-start | bytes 9437192 | tf_op jit(solution)/shard_map/ppermute | solution.py:12
  1222.4 85.2 %collective-permute-start.82 = (bf16[4,216,1536]{2,1,0:T(8,128)(2,1)}, bf16[4,216,1536]{2,1,0:T(8,128)(2,1)}, u32[]{:S(2)}, u32[]{:S(2)}) collective-permute-start(bf16[4,216,1536]{2,1,0:T(8,128)(2,1)} %pad_maximum_fusion.13), channel_id=1, source_target_pairs={{16,20},{20,16},{24,28},{28,24},{17,21},{21,17},{25,29},{29,25},{1... | collective-permute-start | bytes 7962632 | tf_op jit(solution)/shard_map/ppermute | solution.py:367
  1248.4 60.9 %collective-permute-start.79 = (bf16[4,216,1536]{2,1,0:T(8,128)(2,1)}, bf16[4,216,1536]{2,1,0:T(8,128)(2,1)}, u32[]{:S(2)}, u32[]{:S(2)}) collective-permute-start(bf16[4,216,1536]{2,1,0:T(8,128)(2,1)} %pad_maximum_fusion.12), channel_id=1, source_target_pairs={{0,4},{4,0},{8,12},{12,8},{1,5},{5,1},{9,13},{13,9},{2,6},{6,2},{1... | collective-permute-start | bytes 7962632 | tf_op jit(solution)/shard_map/ppermute | solution.py:367
  1255.0 254.9 %collective-permute-start.76 = (bf16[4,384,1728]{1,2,0:T(8,128)(2,1)}, bf16[4,384,1728]{1,2,0:T(8,128)(2,1)}, u32[]{:S(2)}, u32[]{:S(2)}) collective-permute-start(bf16[4,384,1728]{1,2,0:T(8,128)(2,1)} %pad_maximum_fusion.1), channel_id=1, source_target_pairs={{16,20},{20,16},{24,28},{28,24},{17,21},{21,17},{25,29},{29,25},{1... | collective-permute-start | bytes 15925256 | tf_op jit(solution)/shard_map/ppermute | solution.py:367
  1301.4 88.5 %collective-permute-start.72 = (bf16[2,384,1728]{1,2,0:T(8,128)(2,1)}, bf16[2,384,1728]{1,2,0:T(8,128)(2,1)}, u32[]{:S(2)}, u32[]{:S(2)}) collective-permute-start(bf16[2,384,1728]{1,2,0:T(8,128)(2,1)} %pad_maximum_fusion.10), channel_id=1, source_target_pairs={{0,8},{4,12},{8,0},{12,4},{1,9},{5,13},{9,1},{13,5},{2,10},{6,14},... | collective-permute-start | bytes 7962632 | tf_op jit(solution)/shard_map/ppermute | solution.py:367
  1307.6 71.7 %collective-permute-start.63 = (bf16[256,1536]{1,0:T(8,128)(2,1)}, bf16[256,1536]{1,0:T(8,128)(2,1)}, u32[]{:S(2)}, u32[]{:S(2)}) collective-permute-start(bf16[256,1536]{1,0:T(8,128)(2,1)} %get-tuple-element.170), channel_id=1, source_target_pairs={{0,8},{4,12},{8,0},{12,4},{16,24},{20,28},{24,16},{28,20},{1,9},{5... | collective-permute-start | bytes 2359304 | tf_op jit(solution)/shard_map/ppermute | solution.py:12
  1309.2 72.7 %collective-permute-start.65 = (bf16[384,768]{0,1:T(8,128)(2,1)}, bf16[384,768]{0,1:T(8,128)(2,1)}, u32[]{:S(2)}, u32[]{:S(2)}) collective-permute-start(bf16[384,768]{0,1:T(8,128)(2,1)} %copy.234), channel_id=1, source_target_pairs={{16,0},{20,4},{24,8},{28,12},{17,1},{21,5},{25,9},{29,13},{18,2},{... | collective-permute-start | bytes 1769480 | tf_op jit(solution)/shard_map/ppermute | solution.py:359
  1324.9 143.8 %collective-permute-start.70 = (bf16[4,384,768]{1,2,0:T(8,128)(2,1)}, bf16[4,384,768]{1,2,0:T(8,128)(2,1)}, u32[]{:S(2)}, u32[]{:S(2)}) collective-permute-start(bf16[4,384,768]{1,2,0:T(8,128)(2,1)} %pad_maximum_fusion.19), channel_id=1, source_target_pairs={{16,20},{20,16},{24,28},{28,24},{17,21},{21,17},{25,29},{29,25},{1... | collective-permute-start | bytes 7077896 | tf_op jit(solution)/shard_map/ppermute | solution.py:367
  1389.9 75.0 %collective-permute-start.64 = (bf16[256,1536]{1,0:T(8,128)(2,1)}, bf16[256,1536]{1,0:T(8,128)(2,1)S(1)}, u32[]{:S(2)}, u32[]{:S(2)}) collective-permute-start(bf16[256,1536]{1,0:T(8,128)(2,1)} %get-tuple-element.129), channel_id=1, source_target_pairs={{0,16},{4,20},{8,24},{12,28},{16,0},{20,4},{24,8},{28,12},{1,17},{... | collective-permute-start | bytes 2359304 | tf_op jit(solution)/shard_map/ppermute | solution.py:12
  1396.3 113.5 %collective-permute-start.73 = (bf16[4,384,1728]{1,2,0:T(8,128)(2,1)}, bf16[4,384,1728]{1,2,0:T(8,128)(2,1)}, u32[]{:S(2)}, u32[]{:S(2)}) collective-permute-start(bf16[4,384,1728]{1,2,0:T(8,128)(2,1)} %pad_maximum_fusion), channel_id=1, source_target_pairs={{0,4},{4,0},{8,12},{12,8},{1,5},{5,1},{9,13},{13,9},{2,6},{6,2},{1... | collective-permute-start | bytes 15925256 | tf_op jit(solution)/shard_map/ppermute | solution.py:367
  1415.4 53.3 %collective-permute-start.67 = (bf16[4,384,768]{1,2,0:T(8,128)(2,1)}, bf16[4,384,768]{1,2,0:T(8,128)(2,1)}, u32[]{:S(2)}, u32[]{:S(2)}) collective-permute-start(bf16[4,384,768]{1,2,0:T(8,128)(2,1)} %pad_maximum_fusion.17), channel_id=1, source_target_pairs={{0,4},{4,0},{8,12},{12,8},{1,5},{5,1},{9,13},{13,9},{2,6},{6,2},{1... | collective-permute-start | bytes 7077896 | tf_op jit(solution)/shard_map/ppermute | solution.py:367
  (261 other events, 4211.0 us)
Sparse Core Ops, SparseCore 0:
  39.5 51.4 all-gather.8
  161.5 100.2 all-gather.10
  264.0 53.7 all-gather.12
  396.9 48.3 all-gather.14
  471.5 98.0 all-gather.16
  571.0 53.7 all-gather.18
  831.5 95.8 reduce-scatter.24
  935.7 51.4 reduce-scatter.16
  990.0 47.7 reduce-scatter.20
  1040.5 52.0 reduce-scatter.14
  1095.6 97.7 reduce-scatter.22
  1210.1 48.4 reduce-scatter.18

commit v2 on v1

v2 whole, which is shorter than its diff:
```python
import functools

import jax
import jax.numpy as jnp
from jax import lax
from jax.experimental import pallas as pl
from jax.experimental.layout import Layout, with_layout_constraint
from jax.experimental.pallas import tpu as pltpu
from jax.sharding import PartitionSpec as P

EPSILON = 1e-05
PLANE = ("section", "seq")
MESH = pl.DeviceIdType.MESH
VMEM_BYTES = 56 * 2**20
BYTES_PER_US = 3.5e6


def lasting(us):
    return pl.CostEstimate(flops=0, bytes_accessed=int(us * BYTES_PER_US), transcendentals=0)


def tie(*values):
    return lax.optimization_barrier(values)


def kernels_fit():
    return lax.axis_size("section") == 2 and lax.axis_size("seq") == 4


def peers():
    x, q = lax.axis_index("section"), lax.axis_index("seq")
    odd = q % 2
    y = (1 - q // 2) * 2 + odd
    core = {"section": x, "seq": (q // 2) * 2 + (1 - odd)}
    across = {"section": 1 - x, "seq": q}
    beside = {"section": x, "seq": y}
    corner = {"section": x + odd * (1 - 2 * x), "seq": y * (1 - odd) + q * odd}
    return odd, core, across, beside, corner


def greet(others):
    barrier = pltpu.get_barrier_semaphore()
    for other in others:
        pl.semaphore_signal(barrier, inc=1, device_id=other, device_id_type=MESH)
    pl.semaphore_wait(barrier, len(others))


def sum_stages(partial_ref, finish_rows, scratch, chunks):
    from_core, to_corner, from_corner, to_side, from_side, send, recv = scratch
    odd, core, across, beside, corner = peers()
    f32 = jnp.float32
    step = partial_ref.shape[2] // chunks

    def part(k):
        return pl.ds(k * step, step)

    def copy(slot, k, source, target, device):
        return pltpu.make_async_remote_copy(
            src_ref=source,
            dst_ref=target,
            send_sem=send.at[slot, k],
            recv_sem=recv.at[slot, k],
            device_id=device,
            device_id_type=MESH,
        )

    def core_sum(k):
        return copy(0, k, partial_ref.at[1, :, part(k)], from_core.at[:, part(k)], core)

    def corner_sum(k):
        return copy(1, k, to_corner.at[part(k)], from_corner.at[part(k)], corner)

    def across_sum(k):
        return copy(2, k, to_side.at[0, part(k)], from_side.at[0, part(k)], across)

    def beside_sum(k):
        return copy(3, k, to_side.at[1, part(k)], from_side.at[1, part(k)], beside)

    def pair_sum(unit, k):
        return partial_ref[0, unit, part(k)].astype(f32) + from_core[unit, part(k)].astype(f32)

    def sum_corner(k):
        core_sum(k).wait_recv()
        to_corner[part(k)] = pair_sum(3, k).astype(jnp.bfloat16)
        corner_sum(k).start()

    def sum_sides(k):
        corner_sum(k).wait_recv()
        extra = from_corner[part(k)].astype(f32)
        to_side[0, part(k)] = (pair_sum(1, k) + jnp.where(odd == 0, extra, 0.0)).astype(jnp.bfloat16)
        to_side[1, part(k)] = (pair_sum(2, k) + jnp.where(odd == 0, 0.0, extra)).astype(jnp.bfloat16)
        across_sum(k).start()
        beside_sum(k).start()

    def total_rows(k):
        across_sum(k).wait_recv()
        beside_sum(k).wait_recv()
        finish_rows(
            k,
            part(k),
            pair_sum(0, k) + from_side[0, part(k)].astype(f32) + from_side[1, part(k)].astype(f32),
        )

    stages = [lambda k: core_sum(k).start(), sum_corner, sum_sides, total_rows]
    return stages, [core_sum, corner_sum, across_sum, beside_sum]


def run_stages(stages, chunks):
    for tick in range(chunks + len(stages) - 1):
        for place, stage in enumerate(stages):
            if 0 <= tick - place < chunks:
                stage(tick - place)


def sum_scratch(units, rows, width, chunks):
    bf16 = jnp.bfloat16
    return [
        pltpu.VMEM((units, rows, width), bf16),
        pltpu.VMEM((rows, width), bf16),
        pltpu.VMEM((rows, width), bf16),
        pltpu.VMEM((2, rows, width), bf16),
        pltpu.VMEM((2, rows, width), bf16),
        pltpu.SemaphoreType.DMA((4, chunks)),
        pltpu.SemaphoreType.DMA((4, chunks)),
    ]


def exchange_kernel(
    finish, row_ins, shared_ins, row_outs, sum_outs, gather, carried, extra, chunks, partial_ref, *refs
):
    refs = list(refs)
    ins = [refs.pop(0) for _ in range(row_ins)]
    shared = [refs.pop(0) for _ in range(shared_ins)]
    carried_ref = refs.pop(0) if carried else None
    extra_ref, extra_middle = (refs.pop(0), refs.pop(0)) if extra else (None, None)
    outs = [refs.pop(0) for _ in range(row_outs)]
    sums = [refs.pop(0) for _ in range(sum_outs)]
    carried_out = refs.pop(0) if carried else None
    extra_out = refs.pop(0) if extra else None
    spread_ref = refs.pop(0) if gather else None
    sum_refs, (send, recv, carry_send, carry_recv), extra_refs = refs[:7], refs[7:11], refs[11:]
    odd, core, across, beside, corner = peers()
    greet([core, across, beside])
    f32 = jnp.float32
    step = partial_ref.shape[2] // chunks

    def part(k):
        return pl.ds(k * step, step)

    def copy(slot, k, source, target, device):
        return pltpu.make_async_remote_copy(
            src_ref=source,
            dst_ref=target,
            send_sem=send.at[slot, k],
            recv_sem=recv.at[slot, k],
            device_id=device,
            device_id_type=MESH,
        )

    def across_out(k):
        return copy(0, k, spread_ref.at[0, 0, part(k)], spread_ref.at[0, 1, part(k)], across)

    def beside_out(k):
        return copy(1, k, spread_ref.at[0, 0, part(k)], spread_ref.at[0, 2, part(k)], beside)

    def corner_out(k):
        return copy(2, k, spread_ref.at[0, 1 + odd, part(k)], spread_ref.at[0, 3, part(k)], corner)

    def core_out(k):
        return copy(3, k, spread_ref.at[0, :, part(k)], spread_ref.at[1, :, part(k)], core)

    def finish_rows(k, rows, total):
        values, added, sent = finish(
            total, *[ref[rows].astype(f32) for ref in ins], *[ref[...] for ref in shared]
        )
        for ref, value in zip(outs, values):
            ref[rows] = value.astype(ref.dtype)
        for ref, value in zip(sums, added):
            ref[...] = value if k == 0 else ref[...] + value
        if gather:
            spread_ref[0, 0, rows] = sent
            across_out(k).start()
            beside_out(k).start()

    def pass_corner(k):
        across_out(k).wait_recv()
        beside_out(k).wait_recv()
        corner_out(k).start()

    def pass_core(k):
        corner_out(k).wait_recv()
        core_out(k).start()

    def arrive(k):
        core_out(k).wait_recv()

    if carried:
        carry = pltpu.make_async_remote_copy(
            src_ref=carried_ref,
            dst_ref=carried_out,
            send_sem=carry_send,
            recv_sem=carry_recv,
            device_id=across,
            device_id_type=MESH,
        )
        carry.start()
    stages, copies = sum_stages(partial_ref, finish_rows, sum_refs, chunks)
    if gather:
        stages = stages + [pass_corner, pass_core, arrive]
        copies = copies + [across_out, beside_out, corner_out, core_out]
    if extra:

        def extra_rows(k, rows, total):
            extra_out[rows] = (extra_middle[rows] + total).astype(extra_out.dtype)

        later, more = sum_stages(extra_ref, extra_rows, extra_refs, chunks)
        stages = stages[:1] + [lambda k, a=a, b=b: (a(k), b(k)) for a, b in zip(stages[1:5], later)] + stages[5:]
        copies = copies + more
    run_stages(stages, chunks)
    if carried:
        carry.wait()
    for k in range(chunks):
        for one in copies:
            one(k).wait_send()


def exchange(
    finish,
    partial,
    row_ins,
    shared_ins,
    row_outs,
    sum_outs,
    gather,
    number,
    carried=None,
    extra=None,
    chunks=4,
):
    _, units, rows, width = partial.shape
    if not kernels_fit():
        return exchange_plainly(finish, partial, row_ins, shared_ins, row_outs, gather, carried, extra)
    bf16 = jnp.bfloat16
    shapes = [jax.ShapeDtypeStruct((rows, width), dtype) for dtype in row_outs]
    shapes += [jax.ShapeDtypeStruct((1, width), jnp.float32)] * sum_outs
    shapes += [] if carried is None else [jax.ShapeDtypeStruct(carried.shape, carried.dtype)]
    shapes += [] if extra is None else [jax.ShapeDtypeStruct((rows, width), bf16)]
    shapes += [jax.ShapeDtypeStruct(partial.shape, bf16)] * gather
    more = ([] if carried is None else [carried]) + list(extra or ())
    place = pl.BlockSpec(memory_space=pltpu.VMEM)
    result = pl.pallas_call(
        functools.partial(
            exchange_kernel,
            finish,
            len(row_ins),
            len(shared_ins),
            len(row_outs),
            sum_outs,
            gather,
            carried is not None,
            extra is not None,
            chunks,
        ),
        out_shape=shapes,
        in_specs=[place] * (1 + len(row_ins) + len(shared_ins) + len(more)),
        out_specs=[place] * len(shapes),
        scratch_shapes=sum_scratch(units, rows, width, chunks)
        + [pltpu.SemaphoreType.DMA((4, chunks))] * 2
        + [pltpu.SemaphoreType.DMA] * 2
        + ([] if extra is None else sum_scratch(units, rows, width, chunks)),
        compiler_params=pltpu.CompilerParams(
            collective_id=number, has_side_effects=True, vmem_limit_bytes=VMEM_BYTES
        ),
        cost_estimate=lasting(66 if gather else 38),
        name=("exchange_%d" % number),
    )(partial, *row_ins, *shared_ins, *more)
    result = list(result)
    rows_done = [result.pop(0) for _ in row_outs]
    sums = [result.pop(0) for _ in range(sum_outs)]
    carried = None if carried is None else result.pop(0)
    extra = None if extra is None else result.pop(0)
    return rows_done, sums, (result.pop(0) if gather else None), carried, extra


def plane_total(partial):
    near = partial[0].reshape(-1, partial.shape[3]).astype(jnp.float32)
    near = near + flip(partial[1].reshape(-1, partial.shape[3]), 1).astype(jnp.float32)
    return collect(near, (lax.axis_index("seq") % 2) == 1)


def exchange_plainly(finish, partial, row_ins, shared_ins, row_outs, gather, carried, extra):
    total = plane_total(partial)
    rows, sums, sent = finish(total, *[value.astype(jnp.float32) for value in row_ins], *shared_ins)
    rows = [value.astype(dtype) for value, dtype in zip(rows, row_outs)]
    if carried is not None:
        carried = flip(carried, lax.axis_size("seq"))
    if extra is not None:
        extra = (plane_total(extra[0]) + extra[1]).astype(jnp.bfloat16)
    if gather:
        odd = (lax.axis_index("seq") % 2) == 1
        sent = jnp.stack(spread(sent, odd)).reshape(partial.shape)
    return rows, sums, sent, carried, extra


def finish_middle(total, stream, gain):
    middle = stream + total
    return [middle], [], (middle * rms_scale(middle) * gain).astype(jnp.bfloat16)


def finish_block(total, middle, gain):
    result = (middle + total).astype(jnp.bfloat16)
    stream = result.astype(jnp.float32)
    return [result], [], (stream * rms_scale(stream) * gain).astype(jnp.bfloat16)


def finish_gradient(total, upstream, stream, gain):
    scale = rms_scale(stream)
    weighted = gain * total
    grad = (
        upstream
        + scale * weighted
        - stream * scale**3 * jnp.mean(weighted * stream, -1, keepdims=True)
    )
    added = jnp.sum(total * stream * scale, 0, keepdims=True)
    return [grad], [added], grad.astype(jnp.bfloat16)


LAST_CHUNKS = 4


def last_kernel(
    partial_ref,
    upstream_ref,
    stream_ref,
    gain_ref,
    smalls_ref,
    result_ref,
    product_ref,
    mixer_ref,
    pair0_ref,
    pair1_ref,
    down0_ref,
    down1_ref,
    grad_ref,
    crossed_ref,
    smalls_out,
    pair_out,
    down_out,
    mixer_out,
    *scratch,
):
    sum_refs, scratch = scratch[:7], scratch[7:]
    pair_both, down_both, mixer_both, from_z, grad_low, gain_sum = scratch[:6]
    small_sum, small_sent, small_side, small_z = scratch[6:10]
    local, z_send, z_recv, own_send, own_recv, small_send, small_recv, cross_send, cross_recv = scratch[10:]
    x, q, z = lax.axis_index("section"), lax.axis_index("seq"), lax.axis_index("fsdp")
    shards = lax.axis_size("fsdp")
    _, core, across, beside, _ = peers()
    f32, bf16 = jnp.float32, jnp.bfloat16
    others = [{"fsdp": (z + step) % shards} for step in range(1, shards)]
    greet([core, across, beside] + others)
    share = x * 4 + q
    share_across = (1 - x) * 4 + q
    beside_q = (1 - q // 2) * 2 + q % 2
    share_beside = x * 4 + beside_q
    share_corner = (1 - x) * 4 + beside_q

    def remote(source, target, send, recv, device):
        return pltpu.make_async_remote_copy(
            src_ref=source,
            dst_ref=target,
            send_sem=send,
            recv_sem=recv,
            device_id=device,
            device_id_type=MESH,
        )

    early = remote(result_ref, crossed_ref.at[1], cross_send.at[1], cross_recv.at[1], across)
    early.start()
    z_moves = []
    for step, device in enumerate(others):
        one = remote(
            product_ref.at[(z + step + 1) % shards],
            from_z.at[step],
            z_send.at[step],
            z_recv.at[step],
            device,
        )
        one.start()
        z_moves.append(one)
    loads = [
        pltpu.make_async_copy(pair0_ref, pair_both.at[0], local.at[0]),
        pltpu.make_async_copy(pair1_ref, pair_both.at[1], local.at[1]),
        pltpu.make_async_copy(down0_ref, down_both.at[0], local.at[2]),
        pltpu.make_async_copy(down1_ref, down_both.at[1], local.at[3]),
        pltpu.make_async_copy(product_ref.at[z], from_z.at[shards - 1], local.at[4]),
        pltpu.make_async_copy(mixer_ref, mixer_both.at[1], local.at[5]),
    ]
    for one in loads:
        one.start()

    class Owners:
        def __init__(self, place, both, out):
            self.out = out

            def move(slot, source, target, device):
                return remote(source, out.at[target], own_send.at[place, slot], own_recv.at[place, slot], device)

            self.cross = move(0, both.at[1 - x], share, across)
            self.side = move(1, both.at[x], share, beside)
            self.near = move(2, both.at[x], share, core)
            self.side_across = move(3, out.at[share_across], share_across, beside)
            self.near_across = move(4, out.at[share_across], share_across, core)
            self.near_beside = move(5, out.at[share_beside], share_beside, core)
            self.near_corner = move(6, out.at[share_corner], share_corner, core)
            self.keep = pltpu.make_async_copy(both.at[x], out.at[share], local.at[6 + place])

        def first(self):
            for one in (self.cross, self.side, self.near, self.keep):
                one.start()

        def second(self):
            self.cross.wait_recv()
            self.side_across.start()
            self.near_across.start()

        def third(self):
            self.side.wait_recv()
            self.near_beside.start()

        def fourth(self):
            self.side_across.wait_recv()
            self.near_corner.start()

        def end(self):
            for one in (self.near, self.near_across, self.near_beside, self.near_corner):
                one.wait_recv()
            for one in (
                self.cross,
                self.side,
                self.near,
                self.side_across,
                self.near_across,
                self.near_beside,
                self.near_corner,
            ):
                one.wait_send()
            self.keep.wait()

    pair = Owners(0, pair_both, pair_out)
    down = Owners(1, down_both, down_out)
    mixer = Owners(2, mixer_both, mixer_out)
    loads[0].wait()
    loads[1].wait()
    pair.first()
    loads[2].wait()
    loads[3].wait()
    down.first()

    def finish_rows(k, rows, total):
        (grad,), (added,), sent = finish_gradient(
            total, upstream_ref[rows].astype(f32), stream_ref[rows].astype(f32), gain_ref[...]
        )
        grad_ref[rows] = grad
        grad_low[rows] = sent
        gain_sum[...] = added if k == 0 else gain_sum[...] + added

    stages, copies = sum_stages(partial_ref, finish_rows, sum_refs, LAST_CHUNKS)
    run_stages(stages, LAST_CHUNKS)
    pair.second()
    cross = remote(grad_low, crossed_ref.at[0], cross_send.at[0], cross_recv.at[0], across)
    cross.start()
    down.second()

    for one in z_moves:
        one.wait_recv()
    loads[4].wait()
    loads[5].wait()
    total = from_z[0].astype(f32)
    for step in range(1, shards):
        total = total + from_z[step].astype(f32)
    mixer_both[0] = total.astype(bf16)
    mixer.first()
    pair.third()
    down.third()

    small_rows = smalls_ref.shape[3]
    small_sum[...] = smalls_ref[...]
    for shard in range(shards):
        small_sum[0, shard, 0:1] += gain_sum[:, shard * small_rows : (shard + 1) * small_rows]
    for step, device in enumerate((core, across, beside)):
        small_sent[step] = small_sum[...]
        one = remote(small_sent.at[step], small_side.at[step], small_send.at[step], small_recv.at[step], device)
        one.start()
        one.wait()
        small_sum[...] += small_side[step]
    small_moves = []
    for step, device in enumerate(others):
        one = remote(
            small_sum.at[x, (z + step + 1) % shards],
            small_z.at[step],
            small_send.at[3 + step],
            small_recv.at[3 + step],
            device,
        )
        one.start()
        small_moves.append(one)
    small_total = small_sum[x, z]
    for step, one in enumerate(small_moves):
        one.wait()
        small_total = small_total + small_z[step]
    smalls_out[...] = small_total

    mixer.second()
    mixer.third()
    pair.fourth()
    down.fourth()
    mixer.fourth()
    for owners in (pair, down, mixer):
        owners.end()
    cross.wait()
    early.wait()
    for one in z_moves:
        one.wait_send()
    for k in range(LAST_CHUNKS):
        for one in copies:
            one(k).wait_send()


def last_exchange(partial, upstream, stream, gain, smalls, result, product, mixer, pairs, downs):
    _, units, rows, width = partial.shape
    shards, shard_rows, mixer_columns = product.shape
    bf16, f32 = jnp.bfloat16, jnp.float32
    count = 2 * units
    vmem = pl.BlockSpec(memory_space=pltpu.VMEM)
    anywhere = pl.BlockSpec(memory_space=pl.ANY)
    return pl.pallas_call(
        last_kernel,
        out_shape=[
            jax.ShapeDtypeStruct((rows, width), f32),
            jax.ShapeDtypeStruct((2, rows, width), bf16),
            jax.ShapeDtypeStruct(smalls.shape[2:], f32),
            jax.ShapeDtypeStruct((count, *pairs[0].shape), bf16),
            jax.ShapeDtypeStruct((count, *downs[0].shape), bf16),
            jax.ShapeDtypeStruct((count, shard_rows, mixer_columns), bf16),
        ],
        in_specs=[vmem] * 6 + [anywhere] * 6,
        out_specs=[vmem] * 3 + [anywhere] * 3,
        scratch_shapes=sum_scratch(units, rows, width, LAST_CHUNKS)
        + [
            pltpu.VMEM((2, *pairs[0].shape), bf16),
            pltpu.VMEM((2, *downs[0].shape), bf16),
            pltpu.VMEM((2, shard_rows, mixer_columns), bf16),
            pltpu.VMEM(product.shape, bf16),
            pltpu.VMEM((rows, width), bf16),
            pltpu.VMEM((1, width), f32),
            pltpu.VMEM(smalls.shape, f32),
            pltpu.VMEM((3, *smalls.shape), f32),
            pltpu.VMEM((3, *smalls.shape), f32),
            pltpu.VMEM((shards - 1, *smalls.shape[2:]), f32),
            pltpu.SemaphoreType.DMA((9,)),
            pltpu.SemaphoreType.DMA((shards - 1,)),
            pltpu.SemaphoreType.DMA((shards - 1,)),
            pltpu.SemaphoreType.DMA((3, 7)),
            pltpu.SemaphoreType.DMA((3, 7)),
            pltpu.SemaphoreType.DMA((2 + shards,)),
            pltpu.SemaphoreType.DMA((2 + shards,)),
            pltpu.SemaphoreType.DMA((2,)),
            pltpu.SemaphoreType.DMA((2,)),
        ],
        compiler_params=pltpu.CompilerParams(
            collective_id=20, has_side_effects=True, vmem_limit_bytes=VMEM_BYTES
        ),
        cost_estimate=lasting(130),
        name="last_exchange",
    )(partial, upstream, stream, gain, smalls, result, product, mixer, *pairs, *downs)


def place_kernel(blocks, width, stack_ref, *outs):
    shards = lax.axis_size("fsdp")
    count = stack_ref.shape[0]
    part = width // shards // count
    for block in range(blocks):
        pieces = []
        for shard in range(shards):
            start = (block * shards + shard) * part
            pieces += [stack_ref[share, :, start : start + part] for share in range(count)]
        value = jnp.concatenate(pieces, 1).astype(jnp.float32)
        if len(outs) == 1:
            outs[0][:, block * width : (block + 1) * width] = value
        else:
            outs[block][...] = value


def place_columns(stack, blocks, width, together):
    count, rows, columns = stack.shape
    step = 48
    widths = [blocks * width] if together else [width] * blocks
    return pl.pallas_call(
        functools.partial(place_kernel, blocks, width),
        grid=(rows // step,),
        out_shape=[jax.ShapeDtypeStruct((rows, each), jnp.float32) for each in widths],
        in_specs=[pl.BlockSpec((count, step, columns), lambda i: (0, i, 0))],
        out_specs=[pl.BlockSpec((step, each), lambda i: (i, 0)) for each in widths],
        compiler_params=pltpu.CompilerParams(vmem_limit_bytes=VMEM_BYTES),
        cost_estimate=lasting(14),
        name="place_columns",
    )(stack)


def flip(value, bits):
    count = lax.axis_size("section") * lax.axis_size("seq")
    return lax.ppermute(value, PLANE, [(source, source ^ bits) for source in range(count)])


def flip_by_core(value, even_bits, odd_bits):
    count = lax.axis_size("section") * lax.axis_size("seq")
    pairs = [(source, source ^ (odd_bits if source & 1 else even_bits)) for source in range(count)]
    return lax.ppermute(value, PLANE, pairs)


def chip_bits():
    bits = [lax.axis_size("seq")]
    step = lax.axis_size("seq") // 2
    while step > 1:
        bits.append(step)
        step //= 2
    return bits


def half_units():
    units = [0]
    for bits in chip_bits():
        units = units + [unit | bits for unit in units]
    return units


def spread_chips(own, odd):
    bits = chip_bits()
    if len(bits) == 2:
        first = flip(own, bits[0])
        second = flip(own, bits[1])
        third = flip_by_core(jnp.where(odd, second, first), bits[1], bits[0])
        return jnp.concatenate([own, first, second, third], 0)
    held = own
    for step in bits:
        held = jnp.concatenate([held, flip(held, step)], 0)
    return held


def spread(own, odd):
    near = spread_chips(own, odd)
    return near, flip(near, 1)


def collect(near, odd):
    bits = chip_bits()
    if len(bits) == 2:
        rows = near.shape[0] // 4
        held = near
        third = flip_by_core(held[3 * rows :].astype(jnp.bfloat16), bits[1], bits[0]).astype(jnp.float32)
        first = held[rows : 2 * rows] + jnp.where(odd, 0.0, third)
        second = held[2 * rows : 3 * rows] + jnp.where(odd, third, 0.0)
        first = flip(first.astype(jnp.bfloat16), bits[0]).astype(jnp.float32)
        second = flip(second.astype(jnp.bfloat16), bits[1]).astype(jnp.float32)
        return held[:rows] + first + second
    held = near
    for step in reversed(bits):
        rows = held.shape[0] // 2
        held = held[:rows] + flip(held[rows:].astype(jnp.bfloat16), step).astype(jnp.float32)
    return held


def rms_scale(stream):
    return lax.rsqrt(jnp.mean(stream * stream, -1, keepdims=True) + EPSILON)


def times(left, matrix):
    return jnp.dot(left, matrix, preferred_element_type=jnp.float32)


def times_transposed(left, matrix):
    return lax.dot_general(
        left, matrix, (((1,), (1,)), ((), ())), preferred_element_type=jnp.float32
    )


def by_rows(value):
    return with_layout_constraint(value, Layout(major_to_minor=tuple(range(value.ndim))))


def row_products(left, right):
    return lax.dot_general(
        left, right, (((0,), (0,)), ((), ())), preferred_element_type=jnp.float32
    ).astype(jnp.bfloat16)


def normed_with(stream, gain):
    return (stream * rms_scale(stream) * gain).astype(jnp.bfloat16)


def pick_columns(matrix, share, width, count):
    shards = lax.axis_size("fsdp")
    part = width // shards // count
    return jnp.concatenate(
        [
            lax.dynamic_slice(
                matrix, (0, start + shard * (width // shards) + share * part), (matrix.shape[0], part)
            )
            for start in range(0, matrix.shape[1], width)
            for shard in range(shards)
        ],
        1,
    )


def pick_rows(matrix, share, count):
    part = matrix.shape[0] // count
    return lax.dynamic_slice(matrix, (share * part, 0), (part, matrix.shape[1]))


def spread_tokens(tokens_ref, out_ref, send, recv, local, chunks):
    x = lax.axis_index("section")
    _, core, _, beside, _ = peers()
    step_rows = tokens_ref.shape[1] // chunks

    def move(source, target, number, device):
        return pltpu.make_async_remote_copy(
            src_ref=source,
            dst_ref=target,
            send_sem=send.at[number],
            recv_sem=recv.at[number],
            device_id=device,
            device_id_type=MESH,
        )

    sides = []
    for k in range(chunks):
        part = pl.ds(k * step_rows, step_rows)
        first = move(tokens_ref.at[x, part], out_ref.at[0, 2, part], 2 * k, beside)
        second = move(tokens_ref.at[1 - x, part], out_ref.at[0, 3, part], 2 * k + 1, beside)
        first.start()
        second.start()
        sides.append((first, second))
    keep = [
        pltpu.make_async_copy(tokens_ref.at[x], out_ref.at[0, 0], local.at[0]),
        pltpu.make_async_copy(tokens_ref.at[1 - x], out_ref.at[0, 1], local.at[1]),
    ]
    for one in keep:
        one.start()
    for one in keep:
        one.wait()
    near = move(out_ref.at[0, 0:2], out_ref.at[1, 0:2], 2 * chunks, core)
    near.start()

    def end():
        overs = []
        for k, (first, second) in enumerate(sides):
            part = pl.ds(k * step_rows, step_rows)
            first.wait_recv()
            second.wait_recv()
            over = move(out_ref.at[0, 2:4, part], out_ref.at[1, 2:4, part], 2 * chunks + 1 + k, core)
            over.start()
            overs.append(over)
        near.wait()
        for one in overs:
            one.wait()
        for first, second in sides:
            first.wait_send()
            second.wait_send()

    return end


SPREAD_CHUNKS = 4
FFN_CHUNKS = 4
SPREAD_MOVES = 3 * SPREAD_CHUNKS + 1


def spread_kernel(tokens_ref, out_ref, local, send, recv):
    _, core, _, beside, _ = peers()
    greet([core, beside])
    spread_tokens(tokens_ref, out_ref, send, recv, local, SPREAD_CHUNKS)()


def spread_slots(tokens, number):
    x = lax.axis_index("section")
    slots, rows, width = tokens.shape
    if not kernels_fit():
        near = jnp.concatenate(
            [
                lax.dynamic_index_in_dim(tokens, x, 0, False),
                lax.dynamic_index_in_dim(tokens, 1 - x, 0, False),
            ],
            0,
        )
        for step in chip_bits()[1:]:
            near = jnp.concatenate([near, flip(near, step)], 0)
        return jnp.stack([near, flip(near, 1)]).reshape(2, -1, rows, width)
    place = pl.BlockSpec(memory_space=pltpu.VMEM)
    return pl.pallas_call(
        spread_kernel,
        out_shape=jax.ShapeDtypeStruct((2, 4, rows, width), tokens.dtype),
        in_specs=[place],
        out_specs=place,
        scratch_shapes=[
            pltpu.SemaphoreType.DMA((2,)),
            pltpu.SemaphoreType.DMA((SPREAD_MOVES,)),
            pltpu.SemaphoreType.DMA((SPREAD_MOVES,)),
        ],
        compiler_params=pltpu.CompilerParams(
            collective_id=number, has_side_effects=True, vmem_limit_bytes=VMEM_BYTES
        ),
        cost_estimate=lasting(42),
        name="spread_slots",
    )(tokens)


def start_kernel(
    small_ref, tokens_ref, sent_ref, small_out, tokens_out, ffn_out, local, small_send, small_recv, send, recv
):
    x, z = lax.axis_index("section"), lax.axis_index("fsdp")
    shards = lax.axis_size("fsdp")
    _, core, across, beside, _ = peers()
    others = [
        {"section": (x + step // shards) % 2, "fsdp": (z + step) % shards} for step in range(1, 2 * shards)
    ]
    greet([core, beside] + others)
    ffn_rows = sent_ref.shape[0] // FFN_CHUNKS
    crossing = []
    for k in range(FFN_CHUNKS):
        part = pl.ds(k * ffn_rows, ffn_rows)
        one = pltpu.make_async_remote_copy(
            src_ref=sent_ref.at[part],
            dst_ref=ffn_out.at[part],
            send_sem=send.at[SPREAD_MOVES + k],
            recv_sem=recv.at[SPREAD_MOVES + k],
            device_id=across,
            device_id_type=MESH,
        )
        one.start()
        crossing.append(one)
    smalls = []
    for step, device in enumerate(others):
        one = pltpu.make_async_remote_copy(
            src_ref=small_ref,
            dst_ref=small_out.at[x, z],
            send_sem=small_send.at[step],
            recv_sem=small_recv.at[step],
            device_id=device,
            device_id_type=MESH,
        )
        one.start()
        smalls.append(one)
    end = spread_tokens(tokens_ref, tokens_out, send, recv, local, SPREAD_CHUNKS)
    keep = pltpu.make_async_copy(small_ref, small_out.at[x, z], local.at[2])
    keep.start()
    end()
    for one in [keep] + smalls + crossing:
        one.wait()


def start(small, tokens, sent):
    shards = lax.axis_size("fsdp")
    if not kernels_fit():
        every = lax.all_gather(small, ("section", "fsdp"), axis=0).reshape(2, shards, *small.shape)
        return every, spread_slots(tokens, 0), flip(sent, lax.axis_size("seq"))
    _, rows, width = tokens.shape
    place = pl.BlockSpec(memory_space=pltpu.VMEM)
    anywhere = pl.BlockSpec(memory_space=pl.ANY)
    return pl.pallas_call(
        start_kernel,
        out_shape=[
            jax.ShapeDtypeStruct((2, shards, *small.shape), small.dtype),
            jax.ShapeDtypeStruct((2, 4, rows, width), tokens.dtype),
            jax.ShapeDtypeStruct(sent.shape, sent.dtype),
        ],
        in_specs=[place, place, anywhere],
        out_specs=[place, place, anywhere],
        scratch_shapes=[
            pltpu.SemaphoreType.DMA((3,)),
            pltpu.SemaphoreType.DMA((2 * shards - 1,)),
            pltpu.SemaphoreType.DMA((2 * shards - 1,)),
            pltpu.SemaphoreType.DMA((SPREAD_MOVES + FFN_CHUNKS,)),
            pltpu.SemaphoreType.DMA((SPREAD_MOVES + FFN_CHUNKS,)),
        ],
        compiler_params=pltpu.CompilerParams(
            collective_id=21, has_side_effects=True, vmem_limit_bytes=VMEM_BYTES
        ),
        cost_estimate=lasting(59),
        name="start",
    )(small, tokens, sent)


def body(
    tokens,
    in_weight,
    conv_kernel,
    out_weight,
    gate_weight,
    up_weight,
    down_weight,
    mixer_gain,
    ffn_gain,
    cotangent,
):
    bf16, f32 = jnp.bfloat16, jnp.float32
    x_index = lax.axis_index("section")
    q_index = lax.axis_index("seq")
    seq_count = lax.axis_size("seq")
    count = lax.axis_size("section") * seq_count
    shards = lax.axis_size("fsdp")
    share = x_index * seq_count + q_index
    first_plane = x_index == 0
    width = tokens.shape[3]
    rows = tokens.shape[2]
    hidden_width = gate_weight.shape[2]
    shard_rows = width // shards
    in_columns = 3 * width // count
    channels = width // count
    ffn_columns = hidden_width // count
    units = half_units()
    half = len(units)
    part = shard_rows // count

    other = share ^ seq_count

    def mixer_share(index):
        columns = pick_columns(in_weight[0], index, width, count)
        return jnp.concatenate(
            [columns, pick_rows(out_weight[0], index, count).reshape(shard_rows, -1)], 1
        )

    def ffn_share(index):
        return jnp.concatenate(
            [
                pick_columns(gate_weight[0], index, hidden_width, count),
                pick_columns(up_weight[0], index, hidden_width, count),
                pick_rows(down_weight[0], index, count).reshape(shard_rows, -1),
            ],
            1,
        )

    mixer_kept = mixer_share(share)
    mixer_sent = flip(mixer_share(other), seq_count)
    ffn_kept, ffn_sent = ffn_share(share), ffn_share(other)
    mixer_sent, ffn_kept, ffn_sent = tie(mixer_sent, ffn_kept, ffn_sent)
    mixer_parts = [
        jnp.where(first_plane, mixer_kept, mixer_sent),
        jnp.where(first_plane, mixer_sent, mixer_kept),
    ]
    small = jnp.concatenate(
        [
            mixer_gain.astype(f32),
            ffn_gain.astype(f32),
            conv_kernel[0].T.astype(f32),
            jnp.zeros((3, shard_rows), f32),
        ],
        0,
    )
    small, mixer_parts = tie(small, mixer_parts)
    small, entry, ffn_sent = start(small, tokens[:, 0], ffn_sent)
    ffn_parts = [
        jnp.where(first_plane, ffn_kept, ffn_sent),
        jnp.where(first_plane, ffn_sent, ffn_kept),
    ]
    small = small.transpose(0, 2, 1, 3)
    whole = small.reshape(2, 8, width)
    taps_all = lax.dynamic_slice(
        small[:, 2:5].reshape(2, 3, shards, count, part), (0, 0, 0, share, 0), (2, 3, shards, 1, part)
    ).reshape(2, 3, shards * part)

    def over_fsdp(value):
        return lax.all_gather(value, "fsdp", axis=0, tiled=True)

    pair_columns = 2 * ffn_columns

    def mixer_weights(value):
        mixer = over_fsdp(value)
        return mixer[:, :in_columns], mixer[:, in_columns:].reshape(-1, width)

    mixer_matrices = [mixer_weights(mixer_parts[0]), None]

    def ffn_weights(value):
        return value[:, :pair_columns], value[:, pair_columns:].reshape(-1, width)

    in_matrix, out_matrix, value = tie(*mixer_matrices[0], ffn_parts[0])
    mixer_matrices[0] = (in_matrix, out_matrix)
    ffn = over_fsdp(value)
    ffn_matrices = [None, None]

    ids = jnp.stack([share ^ unit ^ side for side in (0, 1) for unit in units])
    has_before = (ids % seq_count) > 0
    has_after = (ids % seq_count) < seq_count - 1
    before_pick = (ids[None, :] == (ids - 1)[:, None]) & has_before[:, None]
    after_pick = (ids[None, :] == (ids + 1)[:, None]) & has_after[:, None]

    def pick_units(mask, edge):
        return jnp.sum(jnp.where(mask[:, :, None, None], edge[None].astype(f32), 0.0), 1)

    def flat(value):
        return value.reshape(2 * half * rows, value.shape[-1])

    def in_units(value):
        return value.reshape(2, half, rows, value.shape[-1])

    def gain_row(block, kind):
        return whole[block, kind : kind + 1]

    stream = lax.dynamic_index_in_dim(tokens[:, 0], x_index, 0, False)
    normed = normed_with(entry.astype(f32), whole[0, 0])
    saved = []
    outputs = []
    for block in range(2):
        in_matrix, out_matrix = mixer_matrices[block]
        taps = taps_all[block]
        projected = times(flat(normed), in_matrix)
        b_gate = projected[:, :channels]
        c_gate = projected[:, channels : 2 * channels]
        x_value = projected[:, 2 * channels :]
        conv_input = (b_gate * x_value).astype(bf16).reshape(2 * half, rows, channels)
        earlier = pick_units(before_pick, conv_input[:, -2:])
        extended = jnp.concatenate([earlier, conv_input.astype(f32)], 1)
        conv_out = (
            taps[0] * extended[:, :-2] + taps[1] * extended[:, 1:-1] + taps[2] * extended[:, 2:]
        )
        gated = flat((c_gate.reshape(conv_out.shape) * conv_out).astype(bf16))
        partial = in_units(times(gated, out_matrix).astype(bf16))
        (middle,), _, normed_ffn, crossed_out, _ = exchange(
            finish_middle,
            partial,
            [stream],
            [gain_row(block, 1)],
            [f32],
            0,
            True,
            1 + 2 * block,
            carried=outputs[0] if block else None,
        )
        if block == 0:
            tokens_back, normed_ffn = tie(cotangent[:, 0], normed_ffn)
            grad_units, normed_ffn = tie(spread_slots(tokens_back, 22), normed_ffn)
            ffn, normed_ffn, value = tie(ffn, normed_ffn, mixer_parts[1])
            ffn_matrices[0] = ffn_weights(ffn)
            mixer = over_fsdp(value)
        pair_matrix, down_matrix = ffn_matrices[block]
        pairs = times(flat(normed_ffn), pair_matrix)
        hidden = (jax.nn.silu(pairs[:, :ffn_columns]) * pairs[:, ffn_columns:]).astype(bf16)
        partial = in_units(times(hidden, down_matrix).astype(bf16))
        if block == 0:
            partial, mixer, value = tie(partial, mixer, ffn_parts[1])
            mixer_matrices[1] = (mixer[:, :in_columns], mixer[:, in_columns:].reshape(-1, width))
            ffn_matrices[1] = ffn_weights(over_fsdp(value))
        saved.append((stream, normed, projected, extended, conv_out, gated, middle, normed_ffn, pairs, hidden))
        if block == 0:
            (stream,), _, normed, _, _ = exchange(
                finish_block, partial, [middle], [gain_row(1, 0)], [bf16], 0, True, 2
            )
            outputs.append(stream)
        else:
            last_sum = (partial, middle)

    upstream = lax.dynamic_index_in_dim(cotangent[:, 0], x_index, 0, False)
    stream_grads = [None, None]
    small_grads = [None, None]
    matrix_grads = [None, None]

    def over_z(value):
        return lax.psum_scatter(value, "fsdp", scatter_dimension=0, tiled=True)

    def product(left, right):
        return by_rows(row_products(left, right))

    def small_rows(mixer_gain_part, ffn_gain_part, taps_placed):
        return jnp.concatenate(
            [
                mixer_gain_part.reshape(1, width),
                ffn_gain_part.reshape(1, width),
                taps_placed,
                jnp.zeros((3, width), f32),
            ],
            0,
        )

    def small_values():
        return jnp.stack(small_grads).reshape(2, 8, shards, shard_rows).transpose(0, 2, 1, 3)

    def to_section(value, block):
        over = [((1 - block) * seq_count + seq, block * seq_count + seq) for seq in range(seq_count)]
        return lax.ppermute(value, PLANE, over)

    inside = chip_bits()[1:] + [1]
    relative = [0, seq_count]
    for bits in inside:
        relative = relative + [unit | bits for unit in relative]

    def to_owners(value, block):
        held = [value, to_section(value, block)]
        for bits in inside:
            over = [
                (block * seq_count + seq, block * seq_count + (seq ^ bits)) for seq in range(seq_count)
            ]
            held = held + [lax.ppermute(unit, PLANE, over) for unit in held]
        return held

    mixer_sum = jnp.zeros((), f32)
    for block in (1, 0):
        in_matrix, out_matrix = mixer_matrices[block]
        pair_matrix, down_matrix = ffn_matrices[block]
        taps = taps_all[block]
        (stream, normed, projected, extended, conv_out, gated, middle, normed_ffn, pairs, hidden) = saved[block]
        down_product, grad_units, mixer_sum = tie(
            product(hidden, flat(grad_units)), grad_units, mixer_sum
        )
        if block == 0:
            matrix_grads[1] = (down_grad, pair_grad, mixer_sum)
        down_grad = over_z(down_product)
        gate_value, up_value = pairs[:, :ffn_columns], pairs[:, ffn_columns:]
        grad_hidden = times_transposed(flat(grad_units), down_matrix)
        sigmoid_gate = jax.nn.sigmoid(gate_value)
        grad_gate = (
            grad_hidden * up_value * sigmoid_gate * (1.0 + gate_value * (1.0 - sigmoid_gate))
        ).astype(bf16)
        grad_up = (grad_hidden * gate_value * sigmoid_gate).astype(bf16)
        grad_pairs = jnp.concatenate([grad_gate, grad_up], 1)
        partial = in_units(times_transposed(grad_pairs, pair_matrix).astype(bf16))
        partial, pair_product, down_grad = tie(
            partial, product(flat(normed_ffn), grad_pairs), down_grad
        )
        pair_grad = over_z(pair_product)
        (grad_middle,), (ffn_gain_part,), mixer_grad, crossed_grad, result = exchange(
            finish_gradient,
            partial,
            [upstream, middle],
            [gain_row(block, 1)],
            [f32],
            1,
            True,
            8 - 2 * block,
            carried=None if block else upstream,
            extra=last_sum if block else None,
        )
        if block == 1:
            outputs.append(result)
        grad_gated = times_transposed(flat(mixer_grad), out_matrix).reshape(2 * half, rows, channels)
        b_gate = projected[:, :channels].reshape(2 * half, rows, channels)
        c_gate = projected[:, channels : 2 * channels].reshape(2 * half, rows, channels)
        x_value = projected[:, 2 * channels :].reshape(2 * half, rows, channels)
        grad_cgate = grad_gated * conv_out
        grad_conv = grad_gated * c_gate
        later = pick_units(after_pick, grad_conv[:, :2])
        grad_extended = jnp.concatenate([grad_conv, later], 1)
        grad_input = (
            taps[0] * grad_extended[:, 2:]
            + taps[1] * grad_extended[:, 1:-1]
            + taps[2] * grad_extended[:, :-2]
        )
        taps_part = jnp.stack(
            [jnp.sum(grad_conv * extended[:, tap : tap + rows], (0, 1)) for tap in range(3)], 0
        )
        grad_projected = flat(
            jnp.concatenate([grad_input * x_value, grad_cgate, grad_input * b_gate], 2).astype(bf16)
        )
        partial = in_units(times_transposed(grad_projected, in_matrix).astype(bf16))
        in_grad = row_products(flat(normed), grad_projected)
        out_grad = row_products(gated, flat(mixer_grad))
        partial, mixer_product, pair_grad = tie(
            partial, by_rows(jnp.concatenate([in_grad, out_grad.reshape(width, -1)], 1)), pair_grad
        )
        if block == 1 or not kernels_fit():
            mixer_sum = over_z(mixer_product)
        own_mask = (jnp.arange(count) == share)[None, None, :, None]
        taps_placed = jnp.where(own_mask, taps_part.reshape(3, shards, 1, part), 0.0).reshape(3, width)
        if block == 0 and kernels_fit():
            break
        (grad_stream,), (mixer_gain_part,), sent, _, _ = exchange(
            finish_gradient,
            partial,
            [grad_middle, stream],
            [gain_row(block, 0)],
            [f32],
            1,
            block == 1,
            9 - 2 * block,
        )
        stream_grads[block] = grad_stream
        small_grads[block] = small_rows(mixer_gain_part, ffn_gain_part, taps_placed)
        if block == 0:
            matrix_grads[0] = (down_grad, pair_grad, mixer_sum)
        if block == 1:
            upstream = sent[0, 0]
            grad_units = sent

    def in_order(index):
        second = to_owners(matrix_grads[1][index], 1)
        first = to_owners(matrix_grads[0][index], 0)
        ordered = jnp.zeros((count, *first[0].shape), bf16)
        for unit, one, two in zip(relative, first, second):
            ordered = lax.dynamic_update_index_in_dim(
                ordered, jnp.where(first_plane, one, two), share ^ unit, 0
            )
        return ordered

    def columns_of(value, blocks):
        piece = value.reshape(count, shard_rows, blocks, shards, -1)
        return piece.transpose(1, 2, 3, 0, 4).reshape(shard_rows, -1).astype(f32)

    if kernels_fit():
        small_grads[0] = small_rows(jnp.zeros((1, width), f32), ffn_gain_part, taps_placed)
        later = matrix_grads[1]
        stream_grads[0], crossed_last, smalls, pair_grad, down_grad, mixer_sum = last_exchange(
            partial,
            grad_middle,
            stream,
            gain_row(0, 0),
            small_values(),
            outputs[1],
            mixer_product.reshape(shards, shard_rows, -1),
            later[2],
            (pair_grad, later[1]),
            (down_grad, later[0]),
        )
        gate_grad, up_grad = place_columns(pair_grad, 2, hidden_width, False)
        (in_grad,) = place_columns(mixer_sum, 3, width, True)
    else:
        crossed_last = flip(jnp.stack([stream_grads[0].astype(bf16), outputs[1]]), seq_count)
        smalls = lax.psum(small_values(), ("section", "seq", "fsdp"))
        smalls = lax.dynamic_slice(
            smalls, (x_index, lax.axis_index("fsdp"), 0, 0), (1, 1, *smalls.shape[2:])
        )[0, 0]
        down_grad, pair_grad, mixer_sum = in_order(0), in_order(1), in_order(2)
        gate_grad = columns_of(pair_grad[..., :ffn_columns], 1)
        up_grad = columns_of(pair_grad[..., ffn_columns:], 1)
        in_grad = columns_of(mixer_sum[..., :in_columns], 3)
    down_grad = down_grad.reshape(-1, width).astype(f32)
    out_grad = mixer_sum[..., in_columns:].reshape(shard_rows, width).astype(f32)

    def by_slot(values, crossed, dtype):
        kept = jnp.where(first_plane, values[0], values[1]).astype(dtype)
        other = jnp.where(first_plane, crossed[0], crossed[1]).astype(dtype)
        return jnp.stack(
            [jnp.where(first_plane, kept, other), jnp.where(first_plane, other, kept)], 0
        )

    return (
        by_slot(outputs, (crossed_out, crossed_last[1]), bf16)[None, :, None],
        by_slot(stream_grads, (crossed_last[0], crossed_grad), f32)[None, :, None],
        in_grad[None],
        smalls[2:5].T[None],
        out_grad[None],
        gate_grad[None],
        up_grad[None],
        down_grad[None],
        smalls[0][None],
        smalls[1][None],
    )


def solution(mesh):
    placed = (
        P(None, "fsdp", "seq", None),
        P("section", "fsdp", None),
        P("section", "fsdp", None),
        P("section", "fsdp", None),
        P("section", "fsdp", None),
        P("section", "fsdp", None),
        P("section", "fsdp", None),
        P("section", "fsdp"),
        P("section", "fsdp"),
        P(None, "fsdp", "seq", None),
    )
    return jax.shard_map(
        body,
        mesh=mesh,
        in_specs=placed,
        out_specs=(
            P("section", None, "fsdp", "seq", None),
            P("section", None, "fsdp", "seq", None),
            P("section", "fsdp", None),
            P("section", "fsdp", None),
            P("section", "fsdp", None),
            P("section", "fsdp", None),
            P("section", "fsdp", None),
            P("section", "fsdp", None),
            P("section", "fsdp"),
            P("section", "fsdp"),
        ),
        check_vma=False,
    )
```

time: 1610 us -> 1210 us (0.75)
  Pallas kernels: 0 us -> 739 us
  waiting for transfers between devices: 668 us -> 42.9 us
  local copies, waits for them, and re-layouts: 268 us -> 99.1 us
  other arithmetic: 215 us -> 65.6 us
  starting transfers between devices: 108 us -> 3.86 us
  blocking collectives: 71.2 us -> 0 us
    pallas_call x0 -> x11, Pallas kernels: none -> 739 us  [the longest x6 451 us: exchange(): pl.pallas_call(functools.partial(exchange_kernel, finish, len(row_ins), l...]
    ppermute x51 -> x1, waiting for transfers between devices: 338 us -> 0.01 us  [flip(): lax.ppermute(value, PLANE, [(source, source ^ bits) for source in range(c...]
    ppermute x32 -> x0, waiting for transfers between devices: 213 us -> none  [the longest x14 123 us: flip_by_core(): return lax.ppermute(value, PLANE, pairs)]
    unnamed x461 -> x153, local copies, waits for them, and re-layouts: 134 us -> 12.6 us
    all_gather x6 -> x4, waiting for transfers between devices: 117 us -> 16.9 us  [over_fsdp(): return lax.all_gather(value, 'fsdp', axis=0, tiled=True)]
    ppermute x32 -> x0, starting transfers between devices: 60 us -> none  [the longest x12 26.1 us: to_owners(): lax.ppermute(units_held, PLANE, pairs)]
    concatenate x17 -> x2, other arithmetic: 44.9 us -> 0.75 us  [the longest x1 0.67 us: body(): jnp.concatenate([mixer_gain.astype(f32), ffn_gain.astype(f32), conv_kerne...]
    ppermute x51 -> x1, starting transfers between devices: 46.4 us -> 2.94 us  [flip(): lax.ppermute(value, PLANE, [(source, source ^ bits) for source in range(c...]
  transfers between devices with their start and end apart: 95 -> 10, of which waited for: 53 -> 4; matrix products, arithmetic and copies ran while one was open for 32% -> 25% of each run, Pallas kernels for 0% -> 46%
where the time goes in v2:
time: 1210 us; the launch traced here: 1200 us
  Pallas kernels  739 us (61%)
  matrix products  235 us (19%)
  local copies, waits for them, and re-layouts  99.1 us (8%)
  other arithmetic  65.6 us (5%)
  waiting for transfers between devices  42.9 us (4%)
  between operations  15.4 us (1%)
    pallas_call x6, Pallas kernels, exchange(): pl.pallas_call(functools.partial(exchange_kernel, finish, len(row_ins), l...  451 us
    pallas_call x1, Pallas kernels, last_exchange(): pl.pallas_call(last_kernel, out_shape=[jax.ShapeDtypeStruct((rows, width)...  168 us
    dot_general x8, matrix products, times_transposed(): lax.dot_general(left, matrix, (((1,), (1,)), ((), ())), preferred_element...  90 us
    dot_general x8, matrix products, times(): return jnp.dot(left, matrix, preferred_element_type=jnp.float32)  75.3 us
    dot_general x8, matrix products, row_products(): lax.dot_general(left, right, (((0,), (0,)), ((), ())), preferred_element_...  69.8 us
    pallas_call x1, Pallas kernels, start(): pl.pallas_call(start_kernel, out_shape=[jax.ShapeDtypeStruct((2, shards,...  55.2 us
    pallas_call x1, Pallas kernels, spread_slots(): pl.pallas_call(spread_kernel, out_shape=jax.ShapeDtypeStruct((2, 4, rows,...  42.5 us
    reduce_scatter x5, waiting for transfers between devices, over_z(): return lax.psum_scatter(value, 'fsdp', scatter_dimension=0, tiled=True)  25.9 us
  transfers between devices with their start and end apart: 10, of which 4 were waited for; matrix products, arithmetic and copies ran while one was open for 25% of the time, Pallas kernels for 46%

profile of v2, /device:TPU:0, one launch (start us, length us, event | category | flops | bytes accessed | tf_op | source)
XLA Modules:
  0.0 1200.9 jit_solution(2128091373208903094)
XLA Ops:
  41.5 55.2 %start.1 = (f32[2,4,8,384]{3,2,1,0:T(8,128)}, bf16[2,4,256,1536]{3,2,1,0:T(8,128)(2,1)}, bf16[384,2592]{1,0:T(8,128)(2,1)}) custom-call(f32[8,384]{1,0:T(8,128)} %maximum_maximum_fusion.small_ref, bf16[2,256,1536]{2,1,0:T(8,128)(2,1)} %bitcast.350, bf16[384,2592]{1,0:T(8,128)(2,1)} %concatenate.99.sent_ref), custom_call_target="tpu_custom_call" | custom-call | bytes 206500000 | tf_op jit(solution)/shard_map/start/pallas_call | solution.py:871
  134.4 65.1 %exchange_1.1 = (f32[256,1536]{1,0:T(8,128)}, bf16[2,4,256,1536]{3,2,1,0:T(8,128)(2,1)}) custom-call(bf16[2,4,256,1536]{3,2,1,0:T(8,128)(2,1)} %bitcast.316, bf16[256,1536]{1,0:T(8,128)(2,1)} %get-tuple-element.304.refs_0_.stream_ref, f32[1,1536]{1,0:T(1,128)} %get-tuple-element.283.refs_1_.refs_2_), custom_call_target="tpu_custom_call" | custom-call | bytes 231000000 | tf_op jit(solution)/shard_map/exchange_1/pallas_call | solution.py:251
  199.5 42.5 %spread_slots.1 = bf16[2,4,256,1536]{3,2,1,0:T(8,128)(2,1)} custom-call(bf16[2,256,1536]{2,1,0:T(8,128)(2,1)} %bitcast.351), custom_call_target="tpu_custom_call" | custom-call | bytes 147000000 | tf_op jit(solution)/shard_map/spread_slots/pallas_call | solution.py:801
  242.0 10.4 all-gather.7.cloned.1.call-done
  252.5 17.9 %fusion.7 = f32[2048,1728]{0,1:T(8,128)} fusion(bf16[2048,1536]{1,0:T(8,128)(2,1)} %bitcast.368, bf16[1536,2592]{1,0:T(8,128)(2,1)} %all-gather.7.cloned.1.call-done), kind=kOutput, calls=%fused_computation.30 | convolution fusion | flops 10871635968 | bytes 25952256 | tf_op jit(solution)/shard_map/dot_general | solution.py:679
  288.0 8.9 convolution_convert_fusion.4
  296.9 6.4 all-gather.9.cloned.1.call-done
  306.6 66.0 %exchange_2.1 = (bf16[256,1536]{1,0:T(8,128)(2,1)}, bf16[2,4,256,1536]{3,2,1,0:T(8,128)(2,1)}) custom-call(bf16[2,4,256,1536]{3,2,1,0:T(8,128)(2,1)} %bitcast.342, f32[256,1536]{1,0:T(8,128)} %get-tuple-element.95.refs_0_.refs_1_, f32[1,1536]{1,0:T(1,128)} %get-tuple-element.282.refs_1_.refs_2_), custom_call_target="tpu_custom_call" | custom-call | bytes 231000000 | tf_op jit(solution)/shard_map/exchange_2/pallas_call | solution.py:251
  389.4 79.2 %exchange_3.1 = (f32[256,1536]{1,0:T(8,128)}, bf16[256,1536]{1,0:T(8,128)(2,1)}, bf16[2,4,256,1536]{3,2,1,0:T(8,128)(2,1)}) custom-call(bf16[2,4,256,1536]{3,2,1,0:T(8,128)(2,1)} %bitcast.315, bf16[256,1536]{1,0:T(8,128)(2,1)} %get-tuple-element.96.refs_0_.refs_2_.refs_1_, f32[1,1536]{1,0:T(1,128)} %get-tuple-element.281.refs_1_.refs_2_, ...), custom_call_target="tpu_custom_call" | custom-call | bytes 231000000 | tf_op jit(solution)/shard_map/exchange_3/pallas_call | solution.py:251
  478.2 18.2 %fusion.4 = f32[2048,1728]{0,1:T(8,128)} fusion(bf16[2048,1536]{1,0:T(8,128)(2,1)} %bitcast.376, bf16[1536,2592]{1,0:T(8,128)(2,1)} %all-gather.11.cloned.1.call-done), kind=kOutput, calls=%fused_computation.27 | convolution fusion | flops 10871635968 | bytes 25952256 | tf_op jit(solution)/shard_map/dot_general | solution.py:679
  504.4 9.8 convolution_convert_fusion.11
  514.3 13.0 %multiply_convert_fusion.3 = (bf16[2048,864]{0,1:T(8,128)(2,1)S(1)}, bf16[2048,864]{0,1:T(8,128)(2,1)S(1)}) fusion(f32[2048,1728]{0,1:T(8,128)} %fusion.4, bf16[2048,1536]{1,0:T(8,128)(2,1)} %bitcast.344, bf16[864,1536]{1,0:T(8,128)(2,1)S(1)} %copy-done.37), kind=kOutput, calls=%fused_computation.20 | convolution fusion | flops 5458821120 | bytes 30179328 | tf_op jit(solution)/shard_map/dot_general | solution.py:683
  527.4 15.6 %convolution_convert_fusion.1 = bf16[2048,1536]{1,0:T(8,128)(2,1)} fusion(bf16[1536,2592]{1,0:T(8,128)(2,1)} %all-gather.11.cloned.1.call-done, bf16[2048,864]{0,1:T(8,128)(2,1)S(1)} %get-tuple-element.217, bf16[2048,864]{0,1:T(8,128)(2,1)S(1)} %get-tuple-element.216), kind=kOutput, calls=%fused_computation.6 | convolution fusion | flops 10888937472 | bytes 18874368 | tf_op jit(solution)/shard_map/dot_general | solution.py:683
  543.0 14.9 %convolution_convert_fusion.9 = bf16[1536,1728]{1,0:T(8,128)(2,1)} fusion(bf16[2048,1536]{1,0:T(8,128)(2,1)} %bitcast.377, bf16[2048,864]{0,1:T(8,128)(2,1)S(1)} %get-tuple-element.217, bf16[2048,864]{0,1:T(8,128)(2,1)S(1)} %get-tuple-element.216), kind=kOutput, calls=%fused_computation.14 | convolution fusion | flops 10888445952 | bytes 18677760 | tf_op jit(solution)/shard_map/dot_general | solution.py:693
  557.8 7.1 reduce-scatter.6.cloned.1.call-done.down1_ref
  566.5 11.1 convolution_convert_fusion.2
  577.6 93.6 %exchange_6.1 = (f32[256,1536]{1,0:T(8,128)}, f32[1,1536]{1,0:T(1,128)}, bf16[256,1536]{1,0:T(8,128)(2,1)}, bf16[2,4,256,1536]{3,2,1,0:T(8,128)(2,1)}) custom-call(bf16[2,4,256,1536]{3,2,1,0:T(8,128)(2,1)} %bitcast.325, bf16[256,1536]{1,0:T(8,128)(2,1)} %get-tuple-element.303.refs_0_, f32[256,1536]{1,0:T(8,128)} %get-tuple-element.105.refs_1_.refs_4_, ...), custom_call_target="tpu_custom_call" | custom-call | bytes 231000000 | tf_op jit(solution)/shard_map/exchange_6/pallas_call | solution.py:251
  679.3 6.9 multiply_reduce_fusion.2
  705.1 9.0 convolution_convert_fusion.7
  714.4 66.2 %exchange_7.1 = (f32[256,1536]{1,0:T(8,128)}, f32[1,1536]{1,0:T(1,128)}, bf16[2,4,256,1536]{3,2,1,0:T(8,128)(2,1)}) custom-call(bf16[2,4,256,1536]{3,2,1,0:T(8,128)(2,1)} %bitcast.333, f32[256,1536]{1,0:T(8,128)} %get-tuple-element.111.refs_0_, bf16[256,1536]{1,0:T(8,128)(2,1)} %get-tuple-element.96.refs_0_.refs_2_.refs_1_, ...), custom_call_target="tpu_custom_call" | custom-call | bytes 231000000 | tf_op jit(solution)/shard_map/exchange_7/pallas_call | solution.py:251
  780.5 9.8 convolution_convert_fusion.10
  790.4 14.1 %multiply_convert_fusion.1 = (bf16[2048,864]{0,1:T(8,128)(2,1)}, bf16[2048,864]{0,1:T(8,128)(2,1)}) fusion(f32[2048,1728]{0,1:T(8,128)} %fusion.7, bf16[2048,1536]{1,0:T(8,128)(2,1)} %bitcast.363, bf16[864,1536]{1,0:T(8,128)(2,1)S(1)} %copy-done.36), kind=kOutput, calls=%fused_computation.18 | convolution fusion | flops 5458821120 | bytes 30179328 | tf_op jit(solution)/shard_map/dot_general | solution.py:683
  804.8 17.3 %convolution_convert_fusion = bf16[2048,1536]{1,0:T(8,128)(2,1)} fusion(bf16[1536,2592]{1,0:T(8,128)(2,1)} %all-gather.7.cloned.1.call-done, bf16[2048,864]{0,1:T(8,128)(2,1)} %get-tuple-element.215, bf16[2048,864]{0,1:T(8,128)(2,1)} %get-tuple-element.214), kind=kOutput, calls=%fused_computation.5 | convolution fusion | flops 10888937472 | bytes 18874368 | tf_op jit(solution)/shard_map/dot_general | solution.py:683
  822.2 15.2 %convolution_convert_fusion.8 = bf16[1536,1728]{1,0:T(8,128)(2,1)} fusion(bf16[2048,1536]{1,0:T(8,128)(2,1)} %bitcast.369, bf16[2048,864]{0,1:T(8,128)(2,1)S(1)} %copy-done.67, bf16[2048,864]{0,1:T(8,128)(2,1)S(1)} %copy-done.66), kind=kOutput, calls=%fused_computation.13 | convolution fusion | flops 10888445952 | bytes 18677760 | tf_op jit(solution)/shard_map/dot_general | solution.py:693
  837.4 18.8 %reduce-scatter.12.cloned.1.call-done.down0_ref = bf16[216,1536]{1,0:T(8,128)(2,1)} async-done(((bf16[864,1536]{1,0:T(8,128)(2,1)}), bf16[216,1536]{1,0:T(8,128)(2,1)}) %reduce-scatter.12.cloned.1.call-update) | async-done | bytes 663568 | tf_op jit(solution)/shard_map/reduce_scatter | solution.py:1069
  858.9 80.7 %exchange_8.1 = (f32[256,1536]{1,0:T(8,128)}, f32[1,1536]{1,0:T(1,128)}, bf16[256,1536]{1,0:T(8,128)(2,1)}, bf16[2,4,256,1536]{3,2,1,0:T(8,128)(2,1)}) custom-call(bf16[2,4,256,1536]{3,2,1,0:T(8,128)(2,1)} %bitcast.331, bf16[256,1536]{1,0:T(8,128)(2,1)} %slice_bitcast_fusion.refs_0_.refs_3_, f32[256,1536]{1,0:T(8,128)} %get-tuple-element.95.refs_0_.refs_1_, ...), custom_call_target="tpu_custom_call" | custom-call | bytes 231000000 | tf_op jit(solution)/shard_map/exchange_8/pallas_call | solution.py:251
  939.6 6.7 multiply_reduce_fusion.5
  976.5 7.3 convolution_convert_fusion.6
  983.8 168.1 %last_exchange.1 = (f32[256,1536]{1,0:T(8,128)}, bf16[2,256,1536]{2,1,0:T(8,128)(2,1)}, f32[8,384]{1,0:T(8,128)}, bf16[8,384,1728]{2,1,0:T(8,128)(2,1)}, bf16[8,...) custom-call(bf16[2,4,256,1536]{3,2,1,0:T(8,128)(2,1)} %bitcast.332, f32[256,1536]{1,0:T(8,128)} %get-tuple-element.120.upstream_ref, ...), custom_call_target="tpu_custom_call" | custom-call | bytes 455000000 | tf_op jit(solution)/shard_map/last_exchange/pallas_call | solution.py:537
  1155.9 8.6 place_columns.2
  1167.2 8.1 bitcast_convert_fusion
  1175.3 13.7 %place_columns.3 = (f32[384,6912]{1,0:T(8,128)}, f32[384,6912]{1,0:T(8,128)}) custom-call(bf16[8,384,1728]{2,1,0:T(8,128)(2,1)} %get-tuple-element.136.stack_ref), custom_call_target="tpu_custom_call" | custom-call | bytes 49000000 | tf_op jit(solution)/shard_map/place_columns/pallas_call | solution.py:599
  (312 shorter events, 199.9 us)
Async XLA Ops:
  7.2 93.5 %all-gather.5.cloned.1.call-start = ((), (), s32[]{:S(2)}) async-start(), calls=%async_computation.5 | async-start | bytes 2949120 | tf_op jit(solution)/shard_map/all_gather | solution.py:974
  8.6 10.4 copy-start.64
  8.6 10.4 copy-start.65
  16.0 23.2 %collective-permute-start = (bf16[384,768]{1,0:T(8,128)(2,1)}, bf16[384,768]{1,0:T(8,128)(2,1)}, u32[]{:S(2)}, u32[]{:S(2)}) collective-permute-start(bf16[384,768]{1,0:T(8,128)(2,1)} %concatenate.97), channel_id=1, source_target_pairs={{0,16},{4,20},{8,24},{12,28},{16,0},{20,4},{24,8},{28,12},{1,17},{... | collective-permute-start | bytes 1769480 | tf_op jit(solution)/shard_map/ppermute | solution.py:613
  41.4 211.0 %all-gather.7.cloned.1.call-start = ((), (), s32[]{:S(2)}) async-start(), calls=%async_computation.6 | async-start | bytes 10321920 | tf_op jit(solution)/shard_map/all_gather | solution.py:974
  106.8 196.5 %all-gather.9.cloned.1.call-start = ((), (), s32[]{:S(2)}) async-start(), calls=%async_computation.7 | async-start | bytes 2949120 | tf_op jit(solution)/shard_map/all_gather | solution.py:974
  109.4 17.9 %copy-start.53 = (f32[192]{0:T(256)}, f32[192]{0:T(256)S(1)}, u32[]{:S(2)}) copy-start(f32[192]{0:T(256)S(1)} %mul.293) | copy-start | bytes 2308
  109.5 17.9 %copy-start.55 = (f32[192]{0:T(256)}, f32[192]{0:T(256)S(1)}, u32[]{:S(2)}) copy-start(f32[192]{0:T(256)S(1)} %mul.290) | copy-start | bytes 2308
  109.6 17.8 %copy-start.57 = (f32[192]{0:T(256)}, f32[192]{0:T(256)S(1)}, u32[]{:S(2)}) copy-start(f32[192]{0:T(256)S(1)} %mul.286) | copy-start | bytes 2308
  252.5 216.2 %all-gather.11.cloned.1.call-start = ((), (), s32[]{:S(2)}) async-start(), calls=%async_computation.8 | async-start | bytes 10321920 | tf_op jit(solution)/shard_map/all_gather | solution.py:974
  303.4 261.6 %reduce-scatter.6.cloned.1.call-start = ((), (), s32[]{:S(2)}) async-start(), calls=%async_computation.9 | async-start | bytes 3317760 | tf_op jit(solution)/shard_map/reduce_scatter | solution.py:1069
  305.1 67.5 %copy-start.3 = (bf16[1536,192]{1,0:T(8,128)(2,1)}, bf16[1536,192]{1,0:T(8,128)(2,1)S(1)}, u32[]{:S(2)}) copy-start(bf16[1536,192]{1,0:T(8,128)(2,1)S(1)} %slice.215) | copy-start | bytes 1769476
  306.6 66.0 %copy-start.48 = (bf16[1536,768]{1,0:T(8,128)(2,1)S(1)}, bf16[1536,768]{1,0:T(8,128)(2,1)}, u32[]{:S(2)}) copy-start(bf16[1536,768]{1,0:T(8,128)(2,1)} %all-gather.9.cloned.1.call-done) | copy-start | bytes 7077892
  504.4 9.9 copy-start.37
  514.3 199.8 %reduce-scatter.8.cloned.1.call-start = ((), (), s32[]{:S(2)}) async-start(), calls=%async_computation.10 | async-start | bytes 6881280 | tf_op jit(solution)/shard_map/reduce_scatter | solution.py:1069
  565.0 225.4 %reduce-scatter.10.cloned.1.call-start = ((), (), s32[]{:S(2)}) async-start(), calls=%async_computation.11 | async-start | bytes 2949120 | tf_op jit(solution)/shard_map/reduce_scatter | solution.py:1069
  577.6 93.6 %copy-start.20 = (bf16[8,24,8,256]{3,2,0,1:T(8,128)(2,1)S(1)}, bf16[8,24,8,256]{3,2,0,1:T(8,128)(2,1)}, u32[]{:S(2)}) copy-start(bf16[8,24,8,256]{3,2,0,1:T(8,128)(2,1)} %copy-done.19) | copy-start | bytes 2359300
  714.1 142.0 %reduce-scatter.12.cloned.1.call-start = ((), (), s32[]{:S(2)}) async-start(), calls=%async_computation.12 | async-start | bytes 3317760 | tf_op jit(solution)/shard_map/reduce_scatter | solution.py:1069
  714.3 66.2 %copy-start.25 = (bf16[2048,864]{0,1:T(8,128)(2,1)S(1)}, bf16[2048,864]{0,1:T(8,128)(2,1)}, u32[]{:S(2)}) copy-start(bf16[2048,864]{0,1:T(8,128)(2,1)} %copy-done.24) | copy-start | bytes 10616836
  780.5 9.9 copy-start.36
  804.5 179.3 %reduce-scatter.14.cloned.1.call-start = ((), (), s32[]{:S(2)}) async-start(), calls=%async_computation.13 | async-start | bytes 6881280 | tf_op jit(solution)/shard_map/reduce_scatter | solution.py:1069
  804.8 17.4 %copy-start.66 = (bf16[2048,864]{0,1:T(8,128)(2,1)S(1)}, bf16[2048,864]{0,1:T(8,128)(2,1)}, u32[]{:S(2)}) copy-start(bf16[2048,864]{0,1:T(8,128)(2,1)} %get-tuple-element.214) | copy-start | bytes 10616836
  804.8 17.3 %copy-start.67 = (bf16[2048,864]{0,1:T(8,128)(2,1)S(1)}, bf16[2048,864]{0,1:T(8,128)(2,1)}, u32[]{:S(2)}) copy-start(bf16[2048,864]{0,1:T(8,128)(2,1)} %get-tuple-element.215) | copy-start | bytes 10616836
  858.8 80.7 %copy-start.2 = (bf16[2048,192]{0,1:T(8,128)(2,1)S(1)}, bf16[2048,192]{0,1:T(8,128)(2,1)}, u32[]{:S(2)}) copy-start(bf16[2048,192]{0,1:T(8,128)(2,1)} %copy-done.1) | copy-start | bytes 2359300
  858.8 80.7 %copy-start.9 = (f32[2048,192]{0,1:T(8,128)S(1)}, f32[2048,192]{0,1:T(8,128)}, u32[]{:S(2)}) copy-start(f32[2048,192]{0,1:T(8,128)} %copy-done.8) | copy-start | bytes 4718596
  858.8 80.7 %copy-start.15 = (f32[8,256,192]{1,2,0:T(8,128)S(1)}, f32[8,256,192]{1,2,0:T(8,128)}, u32[]{:S(2)}) copy-start(f32[8,256,192]{1,2,0:T(8,128)} %copy-done.14) | copy-start | bytes 4718596
  858.8 80.7 %copy-start.29 = (f32[8,2,192]{1,2,0:T(8,128)S(1)}, f32[8,2,192]{1,2,0:T(8,128)}, u32[]{:S(2)}) copy-start(f32[8,2,192]{1,2,0:T(8,128)} %copy-done.28) | copy-start | bytes 36868
  858.8 80.7 %copy-start.39 = (bf16[192,1536]{1,0:T(8,128)(2,1)S(1)}, bf16[192,1536]{1,0:T(8,128)(2,1)}, u32[]{:S(2)}) copy-start(bf16[192,1536]{1,0:T(8,128)(2,1)} %reshape.817) | copy-start | bytes 1769476
  1175.3 13.8 %copy-start = (bf16[256,1536]{1,0:T(8,128)(2,1)S(1)}, bf16[256,1536]{1,0:T(8,128)(2,1)}, u32[]{:S(2)}) copy-start(bf16[256,1536]{1,0:T(8,128)(2,1)} %get-tuple-element.96.refs_0_.refs_2_.refs_1_) | copy-start | bytes 2359300
  1175.3 13.8 %copy-start.27 = (bf16[256,1536]{1,0:T(8,128)(2,1)S(1)}, bf16[256,1536]{1,0:T(8,128)(2,1)}, u32[]{:S(2)}) copy-start(bf16[256,1536]{1,0:T(8,128)(2,1)} %get-tuple-element.106.result_ref) | copy-start | bytes 2359300
  1175.3 13.8 %copy-start.45 = (bf16[2,256,1536]{2,1,0:T(8,128)(2,1)S(1)}, bf16[2,256,1536]{2,1,0:T(8,128)(2,1)}, u32[]{:S(2)}) copy-start(bf16[2,256,1536]{2,1,0:T(8,128)(2,1)} %get-tuple-element.130) | copy-start | bytes 4718596
  1175.3 13.8 %copy-start.46 = (bf16[256,1536]{1,0:T(8,128)(2,1)S(1)}, bf16[256,1536]{1,0:T(8,128)(2,1)}, u32[]{:S(2)}) copy-start(bf16[256,1536]{1,0:T(8,128)(2,1)} %get-tuple-element.107) | copy-start | bytes 2359300
  (50 other events, 197.1 us)
Sparse Core Ops, SparseCore 0:
  41.5 50.7 all-gather.4
  107.0 145.4 all-gather.6
  254.6 48.6 all-gather.8
  305.3 146.2 all-gather.10
  514.4 50.4 reduce-scatter.5
  567.7 97.7 reduce-scatter.7
  714.2 47.2 reduce-scatter.9
  804.7 51.4 reduce-scatter.11
  859.1 97.6 reduce-scatter.13

commit v3 on v2

v3 whole, which is shorter than its diff:
```python
import functools

import jax
import jax.numpy as jnp
from jax import lax
from jax.experimental import pallas as pl
from jax.experimental.layout import Layout, with_layout_constraint
from jax.experimental.pallas import tpu as pltpu
from jax.sharding import PartitionSpec as P

EPSILON = 1e-05
PLANE = ("section", "seq")
MESH = pl.DeviceIdType.MESH
VMEM_BYTES = 56 * 2**20
BYTES_PER_US = 3.5e6


def lasting(us):
    return pl.CostEstimate(flops=0, bytes_accessed=int(us * BYTES_PER_US), transcendentals=0)


def tie(*values):
    return lax.optimization_barrier(values)


def kernels_fit():
    return lax.axis_size("section") == 2 and lax.axis_size("seq") == 4


def peers():
    x, q = lax.axis_index("section"), lax.axis_index("seq")
    odd = q % 2
    y = (1 - q // 2) * 2 + odd
    core = {"section": x, "seq": (q // 2) * 2 + (1 - odd)}
    across = {"section": 1 - x, "seq": q}
    beside = {"section": x, "seq": y}
    corner = {"section": x + odd * (1 - 2 * x), "seq": y * (1 - odd) + q * odd}
    return odd, core, across, beside, corner


def greet(others):
    barrier = pltpu.get_barrier_semaphore()
    for other in others:
        pl.semaphore_signal(barrier, inc=1, device_id=other, device_id_type=MESH)
    pl.semaphore_wait(barrier, len(others))


def remote_copy(source, target, send, recv, device):
    return pltpu.make_async_remote_copy(
        src_ref=source,
        dst_ref=target,
        send_sem=send,
        recv_sem=recv,
        device_id=device,
        device_id_type=MESH,
    )


def other_shards():
    z, shards = lax.axis_index("fsdp"), lax.axis_size("fsdp")
    return [{"fsdp": (z + step) % shards} for step in range(1, shards)]


class ShardSum:
    def __init__(self, product_ref, from_z, send, recv, local):
        z, shards = lax.axis_index("fsdp"), lax.axis_size("fsdp")
        self.from_z = from_z
        self.moves = [
            remote_copy(
                product_ref.at[(z + step) % shards],
                from_z.at[step - 1],
                send.at[step - 1],
                recv.at[step - 1],
                {"fsdp": (z + step) % shards},
            )
            for step in range(1, shards)
        ]
        self.keep = pltpu.make_async_copy(product_ref.at[z], from_z.at[shards - 1], local)

    def start(self):
        for one in self.moves + [self.keep]:
            one.start()

    def total(self):
        for one in self.moves:
            one.wait_recv()
        self.keep.wait()
        value = self.from_z[0].astype(jnp.float32)
        for step in range(1, self.from_z.shape[0]):
            value = value + self.from_z[step].astype(jnp.float32)
        return value.astype(self.from_z.dtype)

    def end(self):
        for one in self.moves:
            one.wait_send()


def shard_sum_scratch(product):
    shards = product.shape[0]
    return [
        pltpu.VMEM(product.shape, product.dtype),
        pltpu.SemaphoreType.DMA((shards - 1,)),
        pltpu.SemaphoreType.DMA((shards - 1,)),
        pltpu.SemaphoreType.DMA,
    ]


def sum_stages(left_ref, matrix_ref, turned, finish_rows, scratch, chunks):
    partial_ref, from_core, to_corner, from_corner, to_side, from_side, send, recv = scratch
    odd, core, across, beside, corner = peers()
    f32 = jnp.float32
    units, step = left_ref.shape[1], left_ref.shape[2] // chunks

    def multiply(half, k):
        left = left_ref[half, :, part(k)].reshape(units * step, left_ref.shape[3])
        right = matrix_ref[:, : left.shape[1]] if turned else matrix_ref[...]
        value = lax.dot_general(
            left, right, (((1,), (1 if turned else 0,)), ((), ())), preferred_element_type=f32
        )
        partial_ref[half, :, part(k)] = value.astype(jnp.bfloat16).reshape(units, step, value.shape[1])

    def part(k):
        return pl.ds(k * step, step)

    def copy(slot, k, source, target, device):
        return pltpu.make_async_remote_copy(
            src_ref=source,
            dst_ref=target,
            send_sem=send.at[slot, k],
            recv_sem=recv.at[slot, k],
            device_id=device,
            device_id_type=MESH,
        )

    def core_sum(k):
        return copy(0, k, partial_ref.at[1, :, part(k)], from_core.at[:, part(k)], core)

    def corner_sum(k):
        return copy(1, k, to_corner.at[part(k)], from_corner.at[part(k)], corner)

    def across_sum(k):
        return copy(2, k, to_side.at[0, part(k)], from_side.at[0, part(k)], across)

    def beside_sum(k):
        return copy(3, k, to_side.at[1, part(k)], from_side.at[1, part(k)], beside)

    def pair_sum(unit, k):
        return partial_ref[0, unit, part(k)].astype(f32) + from_core[unit, part(k)].astype(f32)

    def send_core(k):
        multiply(1, k)
        core_sum(k).start()

    def sum_corner(k):
        multiply(0, k)
        core_sum(k).wait_recv()
        to_corner[part(k)] = pair_sum(3, k).astype(jnp.bfloat16)
        corner_sum(k).start()

    def sum_sides(k):
        corner_sum(k).wait_recv()
        extra = from_corner[part(k)].astype(f32)
        to_side[0, part(k)] = (pair_sum(1, k) + jnp.where(odd == 0, extra, 0.0)).astype(jnp.bfloat16)
        to_side[1, part(k)] = (pair_sum(2, k) + jnp.where(odd == 0, 0.0, extra)).astype(jnp.bfloat16)
        across_sum(k).start()
        beside_sum(k).start()

    def total_rows(k):
        across_sum(k).wait_recv()
        beside_sum(k).wait_recv()
        finish_rows(
            k,
            part(k),
            pair_sum(0, k) + from_side[0, part(k)].astype(f32) + from_side[1, part(k)].astype(f32),
        )

    stages = [send_core, sum_corner, sum_sides, total_rows]
    return stages, [core_sum, corner_sum, across_sum, beside_sum]


STAGE_LAG = 2


def ticks_of(stages, chunks):
    return chunks + STAGE_LAG * (len(stages) - 1)


def run_tick(stages, chunks, tick):
    for place, stage in enumerate(stages):
        if 0 <= tick - STAGE_LAG * place < chunks:
            stage(tick - STAGE_LAG * place)


def run_stages(stages, chunks):
    for tick in range(ticks_of(stages, chunks)):
        run_tick(stages, chunks, tick)


def sum_scratch(units, rows, width, chunks):
    bf16 = jnp.bfloat16
    return [
        pltpu.VMEM((2, units, rows, width), bf16),
        pltpu.VMEM((units, rows, width), bf16),
        pltpu.VMEM((rows, width), bf16),
        pltpu.VMEM((rows, width), bf16),
        pltpu.VMEM((2, rows, width), bf16),
        pltpu.VMEM((2, rows, width), bf16),
        pltpu.SemaphoreType.DMA((4, chunks)),
        pltpu.SemaphoreType.DMA((4, chunks)),
    ]


def exchange_kernel(
    finish, turned, row_ins, shared_ins, row_outs, sum_outs, gather, product, extra, chunks, *refs
):
    refs = list(refs)
    left_ref, matrix_ref = refs.pop(0), refs.pop(0)
    ins = [refs.pop(0) for _ in range(row_ins)]
    shared = [refs.pop(0) for _ in range(shared_ins)]
    product_ref = refs.pop(0) if product else None
    extra_left, extra_matrix, extra_middle = [refs.pop(0) for _ in range(3)] if extra else [None] * 3
    outs = [refs.pop(0) for _ in range(row_outs)]
    sums = [refs.pop(0) for _ in range(sum_outs)]
    product_out = refs.pop(0) if product else None
    extra_out = refs.pop(0) if extra else None
    spread_ref = refs.pop(0) if gather else None
    sum_refs, (send, recv), refs = refs[:8], refs[8:10], refs[10:]
    product_refs, extra_refs = (refs[:4], refs[4:]) if product else ([], refs)
    odd, core, across, beside, corner = peers()
    greet([core, across, beside] + (other_shards() if product else []))
    f32 = jnp.float32
    step = left_ref.shape[2] // chunks

    def part(k):
        return pl.ds(k * step, step)

    def copy(slot, k, source, target, device):
        return pltpu.make_async_remote_copy(
            src_ref=source,
            dst_ref=target,
            send_sem=send.at[slot, k],
            recv_sem=recv.at[slot, k],
            device_id=device,
            device_id_type=MESH,
        )

    def across_out(k):
        return copy(0, k, spread_ref.at[0, 0, part(k)], spread_ref.at[0, 1, part(k)], across)

    def beside_out(k):
        return copy(1, k, spread_ref.at[0, 0, part(k)], spread_ref.at[0, 2, part(k)], beside)

    def corner_out(k):
        return copy(2, k, spread_ref.at[0, 1 + odd, part(k)], spread_ref.at[0, 3, part(k)], corner)

    def core_out(k):
        return copy(3, k, spread_ref.at[0, :, part(k)], spread_ref.at[1, :, part(k)], core)

    def finish_rows(k, rows, total):
        values, added, sent = finish(
            total, *[ref[rows].astype(f32) for ref in ins], *[ref[...] for ref in shared]
        )
        for ref, value in zip(outs, values):
            ref[rows] = value.astype(ref.dtype)
        for ref, value in zip(sums, added):
            ref[...] = value if k == 0 else ref[...] + value
        if gather:
            spread_ref[0, 0, rows] = sent
            across_out(k).start()
            beside_out(k).start()

    def pass_corner(k):
        across_out(k).wait_recv()
        beside_out(k).wait_recv()
        corner_out(k).start()

    def pass_core(k):
        corner_out(k).wait_recv()
        core_out(k).start()

    def arrive(k):
        core_out(k).wait_recv()

    if product:
        shard_sum = ShardSum(product_ref, *product_refs)
        shard_sum.start()
    stages, copies = sum_stages(left_ref, matrix_ref, turned, finish_rows, sum_refs, chunks)
    if gather:
        stages = stages + [pass_corner, pass_core, arrive]
        copies = copies + [across_out, beside_out, corner_out, core_out]
    if extra:

        def extra_rows(k, rows, total):
            extra_out[rows] = (extra_middle[rows] + total).astype(extra_out.dtype)

        later, more = sum_stages(extra_left, extra_matrix, False, extra_rows, extra_refs, chunks)
        stages = stages[:1] + [lambda k, a=a, b=b: (a(k), b(k)) for a, b in zip(stages[1:5], later)] + stages[5:]
        copies = copies + more
    run_stages(stages, chunks)
    if product:
        product_out[...] = shard_sum.total()
        shard_sum.end()
    for k in range(chunks):
        for one in copies:
            one(k).wait_send()


def exchange(
    finish,
    left,
    matrix,
    turned,
    row_ins,
    shared_ins,
    row_outs,
    sum_outs,
    gather,
    number,
    product=None,
    extra=None,
    chunks=4,
):
    _, units, rows, _ = left.shape
    width = matrix.shape[0] if turned else matrix.shape[1]
    if not kernels_fit():
        return exchange_plainly(
            finish, left, matrix, turned, row_ins, shared_ins, row_outs, gather, product, extra
        )
    bf16 = jnp.bfloat16
    shapes = [jax.ShapeDtypeStruct((rows, width), dtype) for dtype in row_outs]
    shapes += [jax.ShapeDtypeStruct((1, width), jnp.float32)] * sum_outs
    shapes += [] if product is None else [jax.ShapeDtypeStruct(product.shape[1:], product.dtype)]
    shapes += [] if extra is None else [jax.ShapeDtypeStruct((rows, width), bf16)]
    shapes += [jax.ShapeDtypeStruct((2, units, rows, width), bf16)] * gather
    more = ([] if product is None else [product]) + list(extra or ())
    place = pl.BlockSpec(memory_space=pltpu.VMEM)
    result = pl.pallas_call(
        functools.partial(
            exchange_kernel,
            finish,
            turned,
            len(row_ins),
            len(shared_ins),
            len(row_outs),
            sum_outs,
            gather,
            product is not None,
            extra is not None,
            chunks,
        ),
        out_shape=shapes,
        in_specs=[place] * (2 + len(row_ins) + len(shared_ins))
        + ([] if product is None else [pl.BlockSpec(memory_space=pl.ANY)])
        + [place] * len(extra or ()),
        out_specs=[place] * len(shapes),
        scratch_shapes=sum_scratch(units, rows, width, chunks)
        + [pltpu.SemaphoreType.DMA((4, chunks))] * 2
        + ([] if product is None else shard_sum_scratch(product))
        + ([] if extra is None else sum_scratch(units, rows, width, chunks)),
        compiler_params=pltpu.CompilerParams(
            collective_id=number, has_side_effects=True, vmem_limit_bytes=VMEM_BYTES
        ),
        cost_estimate=lasting(66 if gather else 38),
        name=("exchange_%d" % number),
    )(left, matrix, *row_ins, *shared_ins, *more)
    result = list(result)
    rows_done = [result.pop(0) for _ in row_outs]
    sums = [result.pop(0) for _ in range(sum_outs)]
    product = None if product is None else result.pop(0)
    extra = None if extra is None else result.pop(0)
    return rows_done, sums, (result.pop(0) if gather else None), product, extra


def plane_total(left, matrix, turned):
    multiply = times_transposed if turned else times
    matrix = matrix[:, : left.shape[3]] if turned else matrix
    near, far = [multiply(half.reshape(-1, half.shape[2]), matrix).astype(jnp.bfloat16) for half in left]
    total = near.astype(jnp.float32) + flip(far, 1).astype(jnp.float32)
    return collect(total, (lax.axis_index("seq") % 2) == 1)


def exchange_plainly(finish, left, matrix, turned, row_ins, shared_ins, row_outs, gather, product, extra):
    total = plane_total(left, matrix, turned)
    rows, sums, sent = finish(total, *[value.astype(jnp.float32) for value in row_ins], *shared_ins)
    rows = [value.astype(dtype) for value, dtype in zip(rows, row_outs)]
    if product is not None:
        product = lax.psum_scatter(
            product.reshape(-1, product.shape[2]), "fsdp", scatter_dimension=0, tiled=True
        )
    if extra is not None:
        extra = (plane_total(extra[0], extra[1], False) + extra[2]).astype(jnp.bfloat16)
    if gather:
        odd = (lax.axis_index("seq") % 2) == 1
        sent = jnp.stack(spread(sent, odd)).reshape(*left.shape[:3], -1)
    return rows, sums, sent, product, extra


def finish_middle(total, stream, gain):
    middle = stream + total
    return [middle], [], (middle * rms_scale(middle) * gain).astype(jnp.bfloat16)


def finish_block(total, middle, gain):
    result = (middle + total).astype(jnp.bfloat16)
    stream = result.astype(jnp.float32)
    return [result], [], (stream * rms_scale(stream) * gain).astype(jnp.bfloat16)


def finish_gradient(total, upstream, stream, gain):
    scale = rms_scale(stream)
    weighted = gain * total
    grad = (
        upstream
        + scale * weighted
        - stream * scale**3 * jnp.mean(weighted * stream, -1, keepdims=True)
    )
    added = jnp.sum(total * stream * scale, 0, keepdims=True)
    return [grad], [added], grad.astype(jnp.bfloat16)


LAST_CHUNKS = 4
OWNER_CHUNKS = (6, 1, 1)


def last_kernel(
    left_ref,
    matrix_ref,
    upstream_ref,
    stream_ref,
    gain_ref,
    smalls_ref,
    later_ref,
    product_ref,
    down_product_ref,
    mixer_ref,
    down_ref,
    pair0_ref,
    pair1_ref,
    grad_ref,
    crossed_ref,
    smalls_out,
    pair_out,
    down_out,
    mixer_out,
    *scratch,
):
    sum_refs, scratch = scratch[:8], scratch[8:]
    pair_both, down_both, mixer_both, grad_low, gain_sum = scratch[:5]
    small_sum, small_sent, small_side, small_z = scratch[5:9]
    local, own_send, own_recv, small_send, small_recv, cross_send, cross_recv = scratch[9:16]
    mixer_sum = ShardSum(product_ref, *scratch[16:20])
    down_sum = ShardSum(down_product_ref, *scratch[20:])
    x, q, z = lax.axis_index("section"), lax.axis_index("seq"), lax.axis_index("fsdp")
    shards = lax.axis_size("fsdp")
    _, core, across, beside, _ = peers()
    f32, bf16 = jnp.float32, jnp.bfloat16
    others = other_shards()
    greet([core, across, beside] + others)
    share = x * 4 + q
    share_across = (1 - x) * 4 + q
    beside_q = (1 - q // 2) * 2 + q % 2
    share_beside = x * 4 + beside_q
    share_corner = (1 - x) * 4 + beside_q

    def remote(source, target, send, recv, device):
        return pltpu.make_async_remote_copy(
            src_ref=source,
            dst_ref=target,
            send_sem=send,
            recv_sem=recv,
            device_id=device,
            device_id_type=MESH,
        )

    mixer_sum.start()
    loads = [
        pltpu.make_async_copy(pair0_ref, pair_both.at[0], local.at[0]),
        pltpu.make_async_copy(pair1_ref, pair_both.at[1], local.at[1]),
        pltpu.make_async_copy(down_ref, down_both.at[1], local.at[2]),
        pltpu.make_async_copy(mixer_ref, mixer_both.at[1], local.at[3]),
    ]
    for one in loads:
        one.start()

    class Owners:
        def __init__(self, place, both, out):
            self.place, self.both, self.out = place, both, out
            self.step = both.shape[1] // OWNER_CHUNKS[place]
            self.chunks = range(OWNER_CHUNKS[place])

        def move(self, slot, k, source, target, device):
            part = pl.ds(k * self.step, self.step)
            place = self.place
            return remote(
                source.at[part],
                self.out.at[target, part],
                own_send.at[place, slot, k],
                own_recv.at[place, slot, k],
                device,
            )

        def cross(self, k):
            return self.move(0, k, self.both.at[1 - x], share, across)

        def side(self, k):
            return self.move(1, k, self.both.at[x], share, beside)

        def near(self, k):
            return self.move(2, k, self.both.at[x], share, core)

        def side_across(self, k):
            return self.move(3, k, self.out.at[share_across], share_across, beside)

        def near_across(self, k):
            return self.move(4, k, self.out.at[share_across], share_across, core)

        def near_beside(self, k):
            return self.move(5, k, self.out.at[share_beside], share_beside, core)

        def near_corner(self, k):
            return self.move(6, k, self.out.at[share_corner], share_corner, core)

        def keep(self):
            return pltpu.make_async_copy(self.both.at[x], self.out.at[share], local.at[4 + self.place])

        def first(self, k):
            self.cross(k).start()
            self.side(k).start()
            self.near(k).start()

        def second(self, k):
            self.cross(k).wait_recv()
            self.side_across(k).start()
            self.near_across(k).start()

        def third(self, k):
            self.side(k).wait_recv()
            self.near_beside(k).start()

        def fourth(self, k):
            self.side_across(k).wait_recv()
            self.near_corner(k).start()

        def end(self):
            for k in self.chunks:
                for one in (self.near, self.near_across, self.near_beside, self.near_corner):
                    one(k).wait_recv()
                for one in (
                    self.cross,
                    self.side,
                    self.near,
                    self.side_across,
                    self.near_across,
                    self.near_beside,
                    self.near_corner,
                ):
                    one(k).wait_send()
            self.keep().wait()

    pair = Owners(0, pair_both, pair_out)
    down = Owners(1, down_both, down_out)
    mixer = Owners(2, mixer_both, mixer_out)
    for one in loads[:2]:
        one.wait()
    pair.keep().start()

    def finish_rows(k, rows, total):
        (grad,), (added,), sent = finish_gradient(
            total, upstream_ref[rows].astype(f32), stream_ref[rows].astype(f32), gain_ref[...]
        )
        grad_ref[rows] = grad
        grad_low[rows] = sent
        gain_sum[...] = added if k == 0 else gain_sum[...] + added

    stages, copies = sum_stages(left_ref, matrix_ref, True, finish_rows, sum_refs, LAST_CHUNKS)
    pieces = [(pair, k) for k in pair.chunks]
    for tick in range(ticks_of(stages, LAST_CHUNKS)):
        run_tick(stages, LAST_CHUNKS, tick)
        for owners, k in pieces[tick : tick + 1]:
            owners.first(k)
        if tick == 1:
            down_sum.start()
    cross = remote(grad_low, crossed_ref.at[0], cross_send.at[0], cross_recv.at[0], across)
    cross.start()
    later = remote(later_ref, crossed_ref.at[1], cross_send.at[1], cross_recv.at[1], across)
    later.start()
    for owners, k in pieces[:2]:
        owners.second(k)

    mixer_both[0] = mixer_sum.total()
    loads[3].wait()
    mixer.keep().start()
    mixer.first(0)
    for owners, k in pieces[2:]:
        owners.second(k)
    for owners, k in pieces:
        owners.third(k)

    mixer.second(0)
    mixer.third(0)
    down_both[0] = down_sum.total()
    loads[2].wait()
    down.keep().start()
    down.first(0)
    small_rows = smalls_ref.shape[3]
    small_sum[...] = smalls_ref[...]
    for shard in range(shards):
        small_sum[0, shard, 0:1] += gain_sum[:, shard * small_rows : (shard + 1) * small_rows]
    for step, device in enumerate((core, across, beside)):
        small_sent[step] = small_sum[...]
        one = remote(small_sent.at[step], small_side.at[step], small_send.at[step], small_recv.at[step], device)
        one.start()
        one.wait()
        small_sum[...] += small_side[step]
    small_moves = []
    for step, device in enumerate(others):
        one = remote(
            small_sum.at[x, (z + step + 1) % shards],
            small_z.at[step],
            small_send.at[3 + step],
            small_recv.at[3 + step],
            device,
        )
        one.start()
        small_moves.append(one)
    small_total = small_sum[x, z]
    for step, one in enumerate(small_moves):
        one.wait()
        small_total = small_total + small_z[step]
    smalls_out[...] = small_total

    for owners, k in pieces:
        owners.fourth(k)
    down.second(0)
    down.third(0)
    mixer.fourth(0)
    down.fourth(0)
    for owners in (pair, down, mixer):
        owners.end()
    cross.wait()
    later.wait()
    mixer_sum.end()
    down_sum.end()
    for k in range(LAST_CHUNKS):
        for one in copies:
            one(k).wait_send()


def last_exchange(left, matrix, upstream, stream, gain, smalls, later, product, down_product, mixer, down, pairs):
    _, units, rows, _ = left.shape
    width = matrix.shape[0]
    shards, shard_rows, mixer_columns = product.shape
    bf16, f32 = jnp.bfloat16, jnp.float32
    count = 2 * units
    vmem = pl.BlockSpec(memory_space=pltpu.VMEM)
    anywhere = pl.BlockSpec(memory_space=pl.ANY)
    return pl.pallas_call(
        last_kernel,
        out_shape=[
            jax.ShapeDtypeStruct((rows, width), f32),
            jax.ShapeDtypeStruct((2, rows, width), bf16),
            jax.ShapeDtypeStruct(smalls.shape[2:], f32),
            jax.ShapeDtypeStruct((count, *pairs[0].shape), bf16),
            jax.ShapeDtypeStruct((count, *down.shape), bf16),
            jax.ShapeDtypeStruct((count, shard_rows, mixer_columns), bf16),
        ],
        in_specs=[vmem] * 7 + [anywhere] * 6,
        out_specs=[vmem] * 3 + [anywhere] * 3,
        scratch_shapes=sum_scratch(units, rows, width, LAST_CHUNKS)
        + [
            pltpu.VMEM((2, *pairs[0].shape), bf16),
            pltpu.VMEM((2, *down.shape), bf16),
            pltpu.VMEM((2, shard_rows, mixer_columns), bf16),
            pltpu.VMEM((rows, width), bf16),
            pltpu.VMEM((1, width), f32),
            pltpu.VMEM(smalls.shape, f32),
            pltpu.VMEM((3, *smalls.shape), f32),
            pltpu.VMEM((3, *smalls.shape), f32),
            pltpu.VMEM((shards - 1, *smalls.shape[2:]), f32),
            pltpu.SemaphoreType.DMA((7,)),
            pltpu.SemaphoreType.DMA((3, 7, max(OWNER_CHUNKS))),
            pltpu.SemaphoreType.DMA((3, 7, max(OWNER_CHUNKS))),
            pltpu.SemaphoreType.DMA((2 + shards,)),
            pltpu.SemaphoreType.DMA((2 + shards,)),
            pltpu.SemaphoreType.DMA((2,)),
            pltpu.SemaphoreType.DMA((2,)),
        ]
        + shard_sum_scratch(product)
        + shard_sum_scratch(down_product),
        compiler_params=pltpu.CompilerParams(
            collective_id=20, has_side_effects=True, vmem_limit_bytes=VMEM_BYTES
        ),
        cost_estimate=lasting(130),
        name="last_exchange",
    )(left, matrix, upstream, stream, gain, smalls, later, product, down_product, mixer, down, *pairs)


def place_kernel(blocks, width, stride, stack_ref, *outs):
    shards = lax.axis_size("fsdp")
    count = stack_ref.shape[0]
    part = width // shards // count
    for block in range(blocks):
        pieces = []
        for shard in range(shards):
            start = block * stride + shard * part
            pieces += [stack_ref[share, :, start : start + part] for share in range(count)]
        value = jnp.concatenate(pieces, 1).astype(jnp.float32)
        if len(outs) == 1:
            outs[0][:, block * width : (block + 1) * width] = value
        else:
            outs[block][...] = value


def place_columns(stack, blocks, width, stride, together):
    count, rows, columns = stack.shape
    step = 48
    widths = [blocks * width] if together else [width] * blocks
    return pl.pallas_call(
        functools.partial(place_kernel, blocks, width, stride),
        grid=(rows // step,),
        out_shape=[jax.ShapeDtypeStruct((rows, each), jnp.float32) for each in widths],
        in_specs=[pl.BlockSpec((count, step, columns), lambda i: (0, i, 0))],
        out_specs=[pl.BlockSpec((step, each), lambda i: (i, 0)) for each in widths],
        compiler_params=pltpu.CompilerParams(vmem_limit_bytes=VMEM_BYTES),
        cost_estimate=lasting(14),
        name="place_columns",
    )(stack)


def local_call(kernel, outs, scratch, us, name, *operands):
    place = pl.BlockSpec(memory_space=pltpu.VMEM)
    return pl.pallas_call(
        kernel,
        out_shape=[jax.ShapeDtypeStruct(shape, dtype) for shape, dtype in outs],
        in_specs=[place] * len(operands),
        out_specs=[place] * len(outs),
        scratch_shapes=[pltpu.VMEM(shape, dtype) for shape, dtype in scratch],
        compiler_params=pltpu.CompilerParams(vmem_limit_bytes=VMEM_BYTES),
        cost_estimate=lasting(us),
        name=name,
    )(*operands)


def unit_place(difference):
    return difference // 4 + (difference // 2 % 2) * 2 + (difference % 2) * 4


def unit_bits(place):
    return (place % 2) * 4 + (place // 2 % 2) * 2 + place // 4


def either(left, right):
    total = 0
    for bit in (1, 2, 4):
        one, two = left // bit % 2, right // bit % 2
        total = total + bit * (one + two - 2 * one * two)
    return total


def neighbour(place, step):
    share = lax.axis_index("section") * 4 + lax.axis_index("seq")
    device = either(share, unit_bits(place))
    seq = device % 4 + step
    inside = jnp.where((seq >= 0) & (seq < 4), 1.0, 0.0)
    seq = (seq + 4) % 4
    return unit_place(either(share, device // 4 * 4 + seq)), inside


def conv_parts(held_ref, place):
    f32 = jnp.float32
    before, inside = neighbour(place, -1)
    here = held_ref[place]
    rows = here.shape[0]
    edge = held_ref[before, rows - 2 : rows] * inside
    whole = jnp.concatenate([edge.astype(f32), here], 0)
    return whole[:rows], whole[1 : rows + 1], here


def mixer_forward_kernel(channels, normed_ref, matrix_ref, taps_ref, projected_ref, held_ref, gated_ref):
    f32, bf16 = jnp.float32, jnp.bfloat16

    def project(place, carry):
        value = jnp.dot(
            normed_ref[place], matrix_ref[:, : 3 * channels], preferred_element_type=f32
        )
        projected_ref[place] = value
        held_ref[place] = (value[:, :channels] * value[:, 2 * channels :]).astype(bf16).astype(f32)
        return carry

    lax.fori_loop(0, 8, project, 0)

    def convolve(place, carry):
        first, second, third = conv_parts(held_ref, place)
        value = taps_ref[0:1] * first + taps_ref[1:2] * second + taps_ref[2:3] * third
        gated_ref[place] = (projected_ref[place, :, channels : 2 * channels] * value).astype(bf16)
        return carry

    lax.fori_loop(0, 8, convolve, 0)


def mixer_forward(normed, matrix, taps):
    rows = normed.shape[2]
    channels = taps.shape[1]
    f32, bf16 = jnp.float32, jnp.bfloat16
    return local_call(
        functools.partial(mixer_forward_kernel, channels),
        [((8, rows, 3 * channels), f32), ((8, rows, channels), f32), ((8, rows, channels), bf16)],
        [],
        10,
        "mixer_forward",
        normed.reshape(8, rows, -1),
        matrix,
        taps,
    )


def mixer_backward_kernel(
    channels, grad_ref, matrix_ref, projected_ref, held_ref, taps_ref, out_ref, taps_out, conv_grad, gate_grad
):
    f32, bf16 = jnp.float32, jnp.bfloat16

    def to_gates(place, carry):
        grad = lax.dot_general(
            grad_ref[place], matrix_ref[...], (((1,), (1,)), ((), ())), preferred_element_type=f32
        )
        first, second, third = conv_parts(held_ref, place)
        value = taps_ref[0:1] * first + taps_ref[1:2] * second + taps_ref[2:3] * third
        back = grad * projected_ref[place, :, channels : 2 * channels]
        gate_grad[place] = grad * value
        conv_grad[place] = back
        added = [jnp.sum(back * shifted, 0, keepdims=True) for shifted in (first, second, third)]
        return carry + jnp.concatenate(added + [jnp.zeros((5, channels), f32)], 0)

    taps_out[...] = lax.fori_loop(0, 8, to_gates, jnp.zeros((8, channels), f32))

    def to_inputs(place, carry):
        after, inside = neighbour(place, 1)
        here = conv_grad[place]
        rows = here.shape[0]
        whole = jnp.concatenate([here, conv_grad[after, 0:2] * inside], 0)
        grad = (
            taps_ref[0:1] * whole[2:] + taps_ref[1:2] * whole[1 : rows + 1] + taps_ref[2:3] * here
        )
        out_ref[place] = jnp.concatenate(
            [
                grad * projected_ref[place, :, 2 * channels :],
                gate_grad[place],
                grad * projected_ref[place, :, :channels],
            ],
            1,
        ).astype(bf16)
        return carry

    lax.fori_loop(0, 8, to_inputs, 0)


def mixer_backward(grads, matrix, projected, held, taps):
    rows = grads.shape[2]
    channels = taps.shape[1]
    f32, bf16 = jnp.float32, jnp.bfloat16
    return local_call(
        functools.partial(mixer_backward_kernel, channels),
        [((8, rows, 3 * channels), bf16), ((8, channels), f32)],
        [((8, rows, channels), f32), ((8, rows, channels), f32)],
        12,
        "mixer_backward",
        grads.reshape(8, rows, -1),
        matrix,
        projected,
        held,
        taps,
    )


def ffn_forward_kernel(pad, normed_ref, matrix_ref, pairs_ref, hidden_ref):
    pairs = jnp.dot(normed_ref[...], matrix_ref[:, : 2 * pad], preferred_element_type=jnp.float32)
    pairs_ref[...] = pairs
    gate, up = pairs[:, :pad], pairs[:, pad:]
    hidden = gate * jax.nn.sigmoid(gate) * up
    hidden_ref[...] = hidden[:, : hidden_ref.shape[1]].astype(jnp.bfloat16)


def ffn_forward(normed, matrix, pad, columns):
    count, width = normed.shape
    step = 256
    return pl.pallas_call(
        functools.partial(ffn_forward_kernel, pad),
        grid=(count // step,),
        out_shape=[
            jax.ShapeDtypeStruct((count, 2 * pad), jnp.float32),
            jax.ShapeDtypeStruct((count, columns), jnp.bfloat16),
        ],
        in_specs=[
            pl.BlockSpec((step, width), lambda i: (i, 0)),
            pl.BlockSpec(matrix.shape, lambda i: (0, 0)),
        ],
        out_specs=[
            pl.BlockSpec((step, 2 * pad), lambda i: (i, 0)),
            pl.BlockSpec((step, columns), lambda i: (i, 0)),
        ],
        compiler_params=pltpu.CompilerParams(vmem_limit_bytes=VMEM_BYTES),
        cost_estimate=lasting(16),
        name="ffn_forward",
    )(normed, matrix)


def ffn_backward_kernel(pad, grad_ref, matrix_ref, pairs_ref, out_ref):
    grad = lax.dot_general(
        grad_ref[...], matrix_ref[...], (((1,), (1,)), ((), ())), preferred_element_type=jnp.float32
    )
    extra = pad - grad.shape[1]
    if extra:
        grad = jnp.concatenate([grad, jnp.zeros((grad.shape[0], extra), jnp.float32)], 1)
    gate, up = pairs_ref[:, :pad], pairs_ref[:, pad:]
    sigmoid = jax.nn.sigmoid(gate)
    out_ref[:, :pad] = (grad * up * sigmoid * (1.0 + gate * (1.0 - sigmoid))).astype(jnp.bfloat16)
    out_ref[:, pad:] = (grad * gate * sigmoid).astype(jnp.bfloat16)


def ffn_backward(grads, matrix, pairs, pad):
    count, width = grads.shape
    step = 256
    return pl.pallas_call(
        functools.partial(ffn_backward_kernel, pad),
        grid=(count // step,),
        out_shape=jax.ShapeDtypeStruct((count, 2 * pad), jnp.bfloat16),
        in_specs=[
            pl.BlockSpec((step, width), lambda i: (i, 0)),
            pl.BlockSpec(matrix.shape, lambda i: (0, 0)),
            pl.BlockSpec((step, 2 * pad), lambda i: (i, 0)),
        ],
        out_specs=pl.BlockSpec((step, 2 * pad), lambda i: (i, 0)),
        compiler_params=pltpu.CompilerParams(vmem_limit_bytes=VMEM_BYTES),
        cost_estimate=lasting(16),
        name="ffn_backward",
    )(grads, matrix, pairs)


def mixer_product_kernel(shards, normed_ref, projected_ref, gated_ref, grad_ref, out_ref):
    f32, bf16 = jnp.float32, jnp.bfloat16
    turned = (((0,), (0,)), ((), ()))
    columns = projected_ref.shape[1]
    width, channels = normed_ref.shape[1], gated_ref.shape[1]
    step = 256
    for start in range(0, width, step):
        out_ref[start : start + step, :columns] = lax.dot_general(
            normed_ref[:, start : start + step], projected_ref[...], turned, preferred_element_type=f32
        ).astype(bf16)
    value = lax.dot_general(gated_ref[...], grad_ref[...], turned, preferred_element_type=f32)
    part = channels // shards
    blocks = width // channels
    for shard in range(shards):
        for block in range(blocks):
            row = (shard * blocks + block) * part
            out_ref[row : row + part, columns:] = value[
                shard * part : (shard + 1) * part, block * channels : (block + 1) * channels
            ].astype(bf16)


def mixer_products(normed, projected_grad, gated, grad):
    width, columns, channels = normed.shape[1], projected_grad.shape[1], gated.shape[1]
    shards = lax.axis_size("fsdp")
    (value,) = local_call(
        functools.partial(mixer_product_kernel, shards),
        [((width, columns + channels), jnp.bfloat16)],
        [],
        14,
        "mixer_products",
        normed,
        projected_grad,
        gated,
        grad,
    )
    return value


def flip(value, bits):
    count = lax.axis_size("section") * lax.axis_size("seq")
    return lax.ppermute(value, PLANE, [(source, source ^ bits) for source in range(count)])


def flip_by_core(value, even_bits, odd_bits):
    count = lax.axis_size("section") * lax.axis_size("seq")
    pairs = [(source, source ^ (odd_bits if source & 1 else even_bits)) for source in range(count)]
    return lax.ppermute(value, PLANE, pairs)


def chip_bits():
    bits = [lax.axis_size("seq")]
    step = lax.axis_size("seq") // 2
    while step > 1:
        bits.append(step)
        step //= 2
    return bits


def half_units():
    units = [0]
    for bits in chip_bits():
        units = units + [unit | bits for unit in units]
    return units


def spread_chips(own, odd):
    bits = chip_bits()
    if len(bits) == 2:
        first = flip(own, bits[0])
        second = flip(own, bits[1])
        third = flip_by_core(jnp.where(odd, second, first), bits[1], bits[0])
        return jnp.concatenate([own, first, second, third], 0)
    held = own
    for step in bits:
        held = jnp.concatenate([held, flip(held, step)], 0)
    return held


def spread(own, odd):
    near = spread_chips(own, odd)
    return near, flip(near, 1)


def collect(near, odd):
    bits = chip_bits()
    if len(bits) == 2:
        rows = near.shape[0] // 4
        held = near
        third = flip_by_core(held[3 * rows :].astype(jnp.bfloat16), bits[1], bits[0]).astype(jnp.float32)
        first = held[rows : 2 * rows] + jnp.where(odd, 0.0, third)
        second = held[2 * rows : 3 * rows] + jnp.where(odd, third, 0.0)
        first = flip(first.astype(jnp.bfloat16), bits[0]).astype(jnp.float32)
        second = flip(second.astype(jnp.bfloat16), bits[1]).astype(jnp.float32)
        return held[:rows] + first + second
    held = near
    for step in reversed(bits):
        rows = held.shape[0] // 2
        held = held[:rows] + flip(held[rows:].astype(jnp.bfloat16), step).astype(jnp.float32)
    return held


def rms_scale(stream):
    return lax.rsqrt(jnp.mean(stream * stream, -1, keepdims=True) + EPSILON)


def times(left, matrix):
    return jnp.dot(left, matrix, preferred_element_type=jnp.float32)


def times_transposed(left, matrix):
    return lax.dot_general(
        left, matrix, (((1,), (1,)), ((), ())), preferred_element_type=jnp.float32
    )


def by_rows(value):
    return with_layout_constraint(value, Layout(major_to_minor=tuple(range(value.ndim))))


def row_products(left, right):
    return lax.dot_general(
        left, right, (((0,), (0,)), ((), ())), preferred_element_type=jnp.float32
    ).astype(jnp.bfloat16)


def normed_with(stream, gain):
    return (stream * rms_scale(stream) * gain).astype(jnp.bfloat16)


def pick_columns(matrix, share, width, count):
    shards = lax.axis_size("fsdp")
    part = width // shards // count
    return jnp.concatenate(
        [
            lax.dynamic_slice(
                matrix, (0, start + shard * (width // shards) + share * part), (matrix.shape[0], part)
            )
            for start in range(0, matrix.shape[1], width)
            for shard in range(shards)
        ],
        1,
    )


def pick_rows(matrix, share, count):
    part = matrix.shape[0] // count
    return lax.dynamic_slice(matrix, (share * part, 0), (part, matrix.shape[1]))


SPREAD_CHUNKS = 4
SPREAD_MOVES = 3 * SPREAD_CHUNKS + 1
FFN_CHUNKS = 2 * SPREAD_CHUNKS


class Spread:
    def __init__(self, rows_of, out_ref, send, recv):
        self.rows_of, self.out_ref, self.send, self.recv = rows_of, out_ref, send, recv
        _, self.core, _, self.beside, _ = peers()
        step = out_ref.shape[2] // SPREAD_CHUNKS
        self.parts = [pl.ds(k * step, step) for k in range(SPREAD_CHUNKS)]

    def side(self, k, slot):
        number = 2 * k + slot
        return remote_copy(
            self.rows_of(slot, self.parts[k]),
            self.out_ref.at[0, 2 + slot, self.parts[k]],
            self.send.at[number],
            self.recv.at[number],
            self.beside,
        )

    def over(self, k):
        number = 2 * SPREAD_CHUNKS + 1 + k
        part = self.parts[k]
        return remote_copy(
            self.out_ref.at[0, 2:4, part],
            self.out_ref.at[1, 2:4, part],
            self.send.at[number],
            self.recv.at[number],
            self.core,
        )

    def near(self):
        number = 2 * SPREAD_CHUNKS
        return remote_copy(
            self.out_ref.at[0, 0:2],
            self.out_ref.at[1, 0:2],
            self.send.at[number],
            self.recv.at[number],
            self.core,
        )

    def first(self, k):
        self.side(k, 0).start()
        self.side(k, 1).start()

    def second(self, k):
        self.side(k, 0).wait_recv()
        self.side(k, 1).wait_recv()
        self.over(k).start()

    def end(self):
        self.near().wait()
        for k in range(SPREAD_CHUNKS):
            self.over(k).wait()
            self.side(k, 0).wait_send()
            self.side(k, 1).wait_send()


def start_kernel(
    small_ref,
    tokens_ref,
    ffn_sent,
    small_out,
    normed_out,
    ffn_out,
    local,
    small_send,
    small_recv,
    spread_send,
    spread_recv,
    cross_send,
    cross_recv,
):
    x, z = lax.axis_index("section"), lax.axis_index("fsdp")
    shards = lax.axis_size("fsdp")
    _, core, across, beside, _ = peers()
    others = [
        {"section": (x + step // shards) % 2, "fsdp": (z + step) % shards} for step in range(1, 2 * shards)
    ]
    greet([core, beside] + others)
    smalls = [
        remote_copy(small_ref, small_out.at[x, z], small_send.at[step], small_recv.at[step], device)
        for step, device in enumerate(others)
    ]
    step = ffn_sent.shape[0] // FFN_CHUNKS
    crossing = []
    for k in range(FFN_CHUNKS):
        part = pl.ds(k * step, step)
        crossing.append(
            remote_copy(
                ffn_sent.at[part], ffn_out.at[part], cross_send.at[k], cross_recv.at[k], across
            )
        )
    keep = pltpu.make_async_copy(small_ref, small_out.at[x, z], local.at[0])
    normed = Spread(lambda slot, part: normed_out.at[0, slot, part], normed_out, spread_send, spread_recv)
    for one in smalls + [keep]:
        one.start()
    crossing[0].start()
    for one in smalls:
        one.wait_recv()
    keep.wait()
    gain = jnp.concatenate([small_out[0, shard, 0:1] for shard in range(shards)], 1)
    for k in range(SPREAD_CHUNKS):
        for slot, place in ((x, 0), (1 - x, 1)):
            part = normed.parts[k]
            normed_out[0, place, part] = normed_with(tokens_ref[slot, part].astype(jnp.float32), gain)
        normed.first(k)
        if k >= 1:
            crossing[k].start()
    normed.near().start()
    for k in range(SPREAD_CHUNKS):
        crossing[SPREAD_CHUNKS + k].start()
        normed.second(k)
    normed.end()
    for one in crossing:
        one.wait()
    for one in smalls:
        one.wait_send()


def start(small, tokens, ffn_sent):
    shards = lax.axis_size("fsdp")
    _, rows, width = tokens.shape
    f32, bf16 = jnp.float32, jnp.bfloat16
    if not kernels_fit():
        seq_count = lax.axis_size("seq")
        every = lax.all_gather(small, ("section", "fsdp"), axis=0).reshape(2, shards, *small.shape)
        gain = every[0, :, 0].reshape(width)
        return (
            every,
            normed_with(spread_plainly(tokens).astype(f32), gain),
            flip(ffn_sent, seq_count),
        )
    place = pl.BlockSpec(memory_space=pltpu.VMEM)
    anywhere = pl.BlockSpec(memory_space=pl.ANY)
    return pl.pallas_call(
        start_kernel,
        out_shape=[
            jax.ShapeDtypeStruct((2, shards, *small.shape), f32),
            jax.ShapeDtypeStruct((2, 4, rows, width), bf16),
            jax.ShapeDtypeStruct(ffn_sent.shape, bf16),
        ],
        in_specs=[place] * 2 + [anywhere],
        out_specs=[place] * 2 + [anywhere],
        scratch_shapes=[
            pltpu.SemaphoreType.DMA((1,)),
            pltpu.SemaphoreType.DMA((2 * shards - 1,)),
            pltpu.SemaphoreType.DMA((2 * shards - 1,)),
            pltpu.SemaphoreType.DMA((SPREAD_MOVES,)),
            pltpu.SemaphoreType.DMA((SPREAD_MOVES,)),
            pltpu.SemaphoreType.DMA((FFN_CHUNKS,)),
            pltpu.SemaphoreType.DMA((FFN_CHUNKS,)),
        ],
        compiler_params=pltpu.CompilerParams(
            collective_id=21, has_side_effects=True, vmem_limit_bytes=VMEM_BYTES
        ),
        cost_estimate=lasting(55),
        name="start",
    )(small, tokens, ffn_sent)


def spread_kernel(rows_ref, out_ref, local, send, recv):
    x = lax.axis_index("section")
    _, core, _, beside, _ = peers()
    greet([core, beside])
    keeps = [
        pltpu.make_async_copy(rows_ref.at[x], out_ref.at[0, 0], local.at[0]),
        pltpu.make_async_copy(rows_ref.at[1 - x], out_ref.at[0, 1], local.at[1]),
    ]
    for one in keeps:
        one.start()
    move = Spread(lambda slot, part: rows_ref.at[x if slot == 0 else 1 - x, part], out_ref, send, recv)
    for k in range(SPREAD_CHUNKS):
        move.first(k)
    for one in keeps:
        one.wait()
    move.near().start()
    for k in range(SPREAD_CHUNKS):
        move.second(k)
    move.end()


def spread_slots(tokens):
    _, rows, width = tokens.shape
    if not kernels_fit():
        return spread_plainly(tokens)
    place = pl.BlockSpec(memory_space=pltpu.VMEM)
    return pl.pallas_call(
        spread_kernel,
        out_shape=jax.ShapeDtypeStruct((2, 4, rows, width), tokens.dtype),
        in_specs=[place],
        out_specs=place,
        scratch_shapes=[
            pltpu.SemaphoreType.DMA((2,)),
            pltpu.SemaphoreType.DMA((SPREAD_MOVES,)),
            pltpu.SemaphoreType.DMA((SPREAD_MOVES,)),
        ],
        compiler_params=pltpu.CompilerParams(
            collective_id=22, has_side_effects=True, vmem_limit_bytes=VMEM_BYTES
        ),
        cost_estimate=lasting(42),
        name="spread_slots",
    )(tokens)


def spread_plainly(tokens):
    x = lax.axis_index("section")
    _, rows, width = tokens.shape
    near = jnp.concatenate(
        [lax.dynamic_index_in_dim(tokens, x, 0, False), lax.dynamic_index_in_dim(tokens, 1 - x, 0, False)], 0
    )
    for step in chip_bits()[1:]:
        near = jnp.concatenate([near, flip(near, step)], 0)
    return jnp.stack([near, flip(near, 1)]).reshape(2, -1, rows, width)


def body(
    tokens,
    in_weight,
    conv_kernel,
    out_weight,
    gate_weight,
    up_weight,
    down_weight,
    mixer_gain,
    ffn_gain,
    cotangent,
):
    bf16, f32 = jnp.bfloat16, jnp.float32
    x_index = lax.axis_index("section")
    q_index = lax.axis_index("seq")
    seq_count = lax.axis_size("seq")
    count = lax.axis_size("section") * seq_count
    shards = lax.axis_size("fsdp")
    share = x_index * seq_count + q_index
    first_plane = x_index == 0
    width = tokens.shape[3]
    rows = tokens.shape[2]
    hidden_width = gate_weight.shape[2]
    shard_rows = width // shards
    in_columns = 3 * width // count
    channels = width // count
    ffn_columns = hidden_width // count
    ffn_pad = -(-ffn_columns // 128) * 128
    units = half_units()
    half = len(units)
    part = shard_rows // count

    other = share ^ seq_count

    def in_share(index):
        return pick_columns(in_weight[0], index, width, count)

    def out_share(index):
        return pick_rows(out_weight[0], index, count)

    def ffn_share(index):
        nothing = jnp.zeros((shard_rows, ffn_pad - ffn_columns), bf16)
        return jnp.concatenate(
            [
                pick_columns(gate_weight[0], index, hidden_width, count),
                nothing,
                pick_columns(up_weight[0], index, hidden_width, count),
                nothing,
                pick_rows(down_weight[0], index, count).reshape(shard_rows, -1),
            ],
            1,
        )

    small = jnp.concatenate(
        [
            mixer_gain.astype(f32),
            ffn_gain.astype(f32),
            conv_kernel[0].T.astype(f32),
            jnp.zeros((3, shard_rows), f32),
        ],
        0,
    )
    def over_fsdp(value):
        return lax.all_gather(value, "fsdp", axis=0, tiled=True)

    def pack_rows(value):
        return value.reshape(part, count, channels).transpose(1, 0, 2).reshape(shard_rows, channels)

    def unpack_rows(value):
        return value.reshape(-1, count, part, channels).transpose(0, 2, 1, 3).reshape(-1, width)

    def mixer_share(index):
        return jnp.concatenate([in_share(index), pack_rows(out_share(index))], 1)

    def over_mixers(value):
        value = over_fsdp(value)
        return value[:, :in_columns], unpack_rows(value[:, in_columns:])

    mixer_own = over_mixers(mixer_share(share))
    mixer_sent = flip(mixer_share(other), seq_count)
    mixer_sent, ffn_kept, ffn_sent = tie(mixer_sent, ffn_share(share), ffn_share(other))
    small, mixer_sent = tie(small, mixer_sent)
    small, normed, ffn_sent = start(small, tokens[:, 0], ffn_sent)
    mixer_across = over_mixers(mixer_sent)
    mixer_matrices = [
        [jnp.where(first_plane == kept, own, across) for own, across in zip(mixer_own, mixer_across)]
        for kept in (True, False)
    ]
    ffn_parts = [
        jnp.where(first_plane, ffn_kept, ffn_sent),
        jnp.where(first_plane, ffn_sent, ffn_kept),
    ]
    small = small.transpose(0, 2, 1, 3)
    whole = small.reshape(2, 8, width)
    taps_all = lax.dynamic_slice(
        small[:, 2:5].reshape(2, 3, shards, count, part), (0, 0, 0, share, 0), (2, 3, shards, 1, part)
    ).reshape(2, 3, shards * part)

    pair_columns = 2 * ffn_pad
    *mixer_matrices[0], pair_part, down_part = tie(
        *mixer_matrices[0], ffn_parts[0][:, :pair_columns], ffn_parts[0][:, pair_columns:]
    )
    pair = over_fsdp(pair_part)
    ids = jnp.stack([share ^ unit ^ side for side in (0, 1) for unit in units])
    has_before = (ids % seq_count) > 0
    has_after = (ids % seq_count) < seq_count - 1
    before_pick = (ids[None, :] == (ids - 1)[:, None]) & has_before[:, None]
    after_pick = (ids[None, :] == (ids + 1)[:, None]) & has_after[:, None]

    def pick_units(mask, edge):
        return jnp.sum(jnp.where(mask[:, :, None, None], edge[None].astype(f32), 0.0), 1)

    def flat(value):
        return value.reshape(2 * half * rows, value.shape[-1])

    def in_units(value):
        return value.reshape(2, half, rows, value.shape[-1])

    def gain_row(block, kind):
        return whole[block, kind : kind + 1]

    stream = lax.dynamic_index_in_dim(tokens[:, 0], x_index, 0, False)
    saved = []
    outputs = []
    for block in range(2):
        in_matrix, out_matrix = mixer_matrices[block]
        taps = taps_all[block]
        if kernels_fit():
            projected, held, gated = mixer_forward(normed, in_matrix, taps)
            gated = flat(gated)
            if block == 1:
                gated, crossed_out = tie(gated, crossed_out)
        else:
            projected = times(flat(normed), in_matrix[:, :in_columns])
            b_gate = projected[:, :channels]
            c_gate = projected[:, channels : 2 * channels]
            x_value = projected[:, 2 * channels :]
            conv_input = (b_gate * x_value).astype(bf16).reshape(2 * half, rows, channels)
            earlier = pick_units(before_pick, conv_input[:, -2:])
            held = jnp.concatenate([earlier, conv_input.astype(f32)], 1)
            conv_out = taps[0] * held[:, :-2] + taps[1] * held[:, 1:-1] + taps[2] * held[:, 2:]
            gated = flat((c_gate.reshape(conv_out.shape) * conv_out).astype(bf16))
        (middle,), _, normed_ffn, _, _ = exchange(
            finish_middle,
            in_units(gated),
            out_matrix,
            False,
            [stream],
            [gain_row(block, 1)],
            [f32],
            0,
            True,
            1 + 2 * block,
        )
        if block == 0:
            pair, normed_ffn, value = tie(pair, normed_ffn, down_part.reshape(-1, width))
            down = over_fsdp(value)
            ffn_matrices = [(pair, down), None]
        pair_matrix, down_matrix = ffn_matrices[block]
        if kernels_fit():
            pairs, hidden = ffn_forward(flat(normed_ffn), pair_matrix, ffn_pad, ffn_columns)
        else:
            pairs = times(flat(normed_ffn), pair_matrix[:, :pair_columns])
            hidden = (jax.nn.silu(pairs[:, :ffn_pad]) * pairs[:, ffn_pad:]).astype(bf16)[:, :ffn_columns]
        if block == 0:
            hidden, grad_rows = tie(hidden, cotangent[:, 0])
            hidden, grad_units = tie(hidden, spread_slots(grad_rows))
            hidden, down, value = tie(hidden, down, ffn_parts[1])
            down_matrix = down
            ffn = over_fsdp(value)
            ffn_matrices = [(pair, down), (ffn, ffn[:, pair_columns:].reshape(-1, width))]
        saved.append((stream, normed, projected, held, gated, middle, normed_ffn, pairs, hidden))
        if block == 0:
            (stream,), _, normed, _, _ = exchange(
                finish_block,
                in_units(hidden),
                down_matrix,
                False,
                [middle],
                [gain_row(1, 0)],
                [bf16],
                0,
                True,
                2,
            )
            outputs.append(stream)
            crossed_out = flip(stream, seq_count)
        else:
            last_sum = (in_units(hidden), down_matrix, middle)

    upstream = lax.dynamic_index_in_dim(cotangent[:, 0], x_index, 0, False)
    stream_grads = [None, None]
    small_grads = [None, None]
    matrix_grads = [None, None]

    def over_z(value):
        return lax.psum_scatter(value, "fsdp", scatter_dimension=0, tiled=True)

    def product(left, right):
        return by_rows(row_products(left, right))

    def small_rows(mixer_gain_part, ffn_gain_part, taps_placed):
        return jnp.concatenate(
            [
                mixer_gain_part.reshape(1, width),
                ffn_gain_part.reshape(1, width),
                taps_placed,
                jnp.zeros((3, width), f32),
            ],
            0,
        )

    def small_values():
        return jnp.stack(small_grads).reshape(2, 8, shards, shard_rows).transpose(0, 2, 1, 3)

    def to_section(value, block):
        over = [((1 - block) * seq_count + seq, block * seq_count + seq) for seq in range(seq_count)]
        return lax.ppermute(value, PLANE, over)

    inside = chip_bits()[1:] + [1]
    relative = [0, seq_count]
    for bits in inside:
        relative = relative + [unit | bits for unit in relative]

    def to_owners(value, block):
        held = [value, to_section(value, block)]
        for bits in inside:
            over = [
                (block * seq_count + seq, block * seq_count + (seq ^ bits)) for seq in range(seq_count)
            ]
            held = held + [lax.ppermute(unit, PLANE, over) for unit in held]
        return held

    mixer_sum = jnp.zeros((), f32)
    for block in (1, 0):
        in_matrix, out_matrix = mixer_matrices[block]
        pair_matrix, down_matrix = ffn_matrices[block]
        taps = taps_all[block]
        (stream, normed, projected, held, gated, middle, normed_ffn, pairs, hidden) = saved[block]
        down_product, grad_units, mixer_sum = tie(
            product(hidden, flat(grad_units)), grad_units, mixer_sum
        )
        if block == 0:
            matrix_grads[1] = (down_grad, pair_grad, mixer_sum)
        down_product = down_product.reshape(shards, -1, width)
        if kernels_fit():
            grad_pairs = ffn_backward(flat(grad_units), down_matrix, pairs, ffn_pad)
            if block == 0:
                grad_pairs, crossed = tie(grad_pairs, crossed)
        else:
            gate_value, up_value = pairs[:, :ffn_pad], pairs[:, ffn_pad:]
            grad_hidden = times_transposed(flat(grad_units), down_matrix)
            grad_hidden = jnp.pad(grad_hidden, ((0, 0), (0, ffn_pad - ffn_columns)))
            sigmoid_gate = jax.nn.sigmoid(gate_value)
            grad_gate = grad_hidden * up_value * sigmoid_gate * (1.0 + gate_value * (1.0 - sigmoid_gate))
            grad_up = grad_hidden * gate_value * sigmoid_gate
            grad_pairs = jnp.concatenate([grad_gate, grad_up], 1).astype(bf16)
        grad_pairs, pair_product = tie(grad_pairs, product(flat(normed_ffn), grad_pairs))
        pair_grad = over_z(pair_product)
        (grad_middle,), (ffn_gain_part,), mixer_grad, _, _ = exchange(
            finish_gradient,
            in_units(grad_pairs),
            pair_matrix,
            True,
            [upstream, middle],
            [gain_row(block, 1)],
            [f32],
            1,
            True,
            8 - 2 * block,
        )
        if kernels_fit():
            grad_projected, taps_part = mixer_backward(mixer_grad, out_matrix, projected, held, taps)
            grad_projected, taps_part = flat(grad_projected), taps_part[:3]
            mixer_product = mixer_products(flat(normed), grad_projected, gated, flat(mixer_grad))
        else:
            grad_gated = times_transposed(flat(mixer_grad), out_matrix).reshape(2 * half, rows, channels)
            b_gate = projected[:, :channels].reshape(2 * half, rows, channels)
            c_gate = projected[:, channels : 2 * channels].reshape(2 * half, rows, channels)
            x_value = projected[:, 2 * channels :].reshape(2 * half, rows, channels)
            conv_out = taps[0] * held[:, :-2] + taps[1] * held[:, 1:-1] + taps[2] * held[:, 2:]
            grad_cgate = grad_gated * conv_out
            grad_conv = grad_gated * c_gate
            later = pick_units(after_pick, grad_conv[:, :2])
            grad_extended = jnp.concatenate([grad_conv, later], 1)
            grad_input = (
                taps[0] * grad_extended[:, 2:]
                + taps[1] * grad_extended[:, 1:-1]
                + taps[2] * grad_extended[:, :-2]
            )
            taps_part = jnp.stack(
                [jnp.sum(grad_conv * held[:, tap : tap + rows], (0, 1)) for tap in range(3)], 0
            )
            grad_projected = flat(
                jnp.concatenate([grad_input * x_value, grad_cgate, grad_input * b_gate], 2).astype(bf16)
            )
            in_grad = row_products(flat(normed), grad_projected)
            out_grad = row_products(gated, flat(mixer_grad)).reshape(shards, part, count, channels)
            out_grad = out_grad.transpose(0, 2, 1, 3).reshape(width, channels)
            mixer_product = jnp.concatenate([in_grad, out_grad], 1)
        grad_projected, mixer_product, pair_grad = tie(
            grad_projected, mixer_product, pair_grad
        )
        if block == 1 or not kernels_fit():
            mixer_sum = over_z(mixer_product)
        own_mask = (jnp.arange(count) == share)[None, None, :, None]
        taps_placed = jnp.where(own_mask, taps_part.reshape(3, shards, 1, part), 0.0).reshape(3, width)
        if block == 0 and kernels_fit():
            break
        (grad_stream,), (mixer_gain_part,), sent, down_grad, result = exchange(
            finish_gradient,
            in_units(grad_projected),
            in_matrix,
            True,
            [grad_middle, stream],
            [gain_row(block, 0)],
            [f32],
            1,
            block == 1,
            9 - 2 * block,
            product=down_product,
            extra=last_sum if block else None,
        )
        if block == 1:
            outputs.append(result)
        stream_grads[block] = grad_stream
        small_grads[block] = small_rows(mixer_gain_part, ffn_gain_part, taps_placed)
        if block == 0:
            matrix_grads[0] = (down_grad, pair_grad, mixer_sum)
        if block == 1:
            upstream = sent[0, 0]
            grad_units = sent
            crossed = flip(result, seq_count)

    def in_order(index):
        second = to_owners(matrix_grads[1][index], 1)
        first = to_owners(matrix_grads[0][index], 0)
        ordered = jnp.zeros((count, *first[0].shape), bf16)
        for unit, one, two in zip(relative, first, second):
            ordered = lax.dynamic_update_index_in_dim(
                ordered, jnp.where(first_plane, one, two), share ^ unit, 0
            )
        return ordered

    def columns_of(value, blocks):
        piece = value.reshape(count, shard_rows, blocks, shards, -1)
        return piece.transpose(1, 2, 3, 0, 4).reshape(shard_rows, -1).astype(f32)

    if kernels_fit():
        small_grads[0] = small_rows(jnp.zeros((1, width), f32), ffn_gain_part, taps_placed)
        later = matrix_grads[1]
        stream_grads[0], crossed_last, smalls, pair_grad, down_grad, mixer_sum = last_exchange(
            in_units(grad_projected),
            in_matrix,
            grad_middle,
            stream,
            gain_row(0, 0),
            small_values(),
            upstream,
            mixer_product.reshape(shards, shard_rows, -1),
            down_product,
            later[2],
            later[0],
            (pair_grad, later[1]),
        )
        gate_grad, up_grad = place_columns(pair_grad, 2, hidden_width, ffn_pad, False)
        (in_grad,) = place_columns(mixer_sum, 3, width, channels, True)
    else:
        crossed_last = flip(jnp.stack([grad.astype(bf16) for grad in stream_grads]), seq_count)
        smalls = lax.psum(small_values(), ("section", "seq", "fsdp"))
        smalls = lax.dynamic_slice(
            smalls, (x_index, lax.axis_index("fsdp"), 0, 0), (1, 1, *smalls.shape[2:])
        )[0, 0]
        down_grad, pair_grad, mixer_sum = in_order(0), in_order(1), in_order(2)
        gate_grad = columns_of(pair_grad[..., :ffn_columns], 1)
        up_grad = columns_of(pair_grad[..., ffn_pad : ffn_pad + ffn_columns], 1)
        in_grad = columns_of(mixer_sum[..., :in_columns], 3)
    down_grad = down_grad.reshape(-1, width).astype(f32)
    out_grad = unpack_rows(mixer_sum[..., in_columns:]).astype(f32)

    def by_slot(values, crossed, dtype):
        kept = jnp.where(first_plane, values[0], values[1]).astype(dtype)
        other = jnp.where(first_plane, crossed[0], crossed[1]).astype(dtype)
        return jnp.stack(
            [jnp.where(first_plane, kept, other), jnp.where(first_plane, other, kept)], 0
        )

    return (
        by_slot(outputs, (crossed_out, crossed), bf16)[None, :, None],
        by_slot(stream_grads, (crossed_last[0], crossed_last[1]), f32)[None, :, None],
        in_grad[None],
        smalls[2:5].T[None],
        out_grad[None],
        gate_grad[None],
        up_grad[None],
        down_grad[None],
        smalls[0][None],
        smalls[1][None],
    )


def solution(mesh):
    placed = (
        P(None, "fsdp", "seq", None),
        P("section", "fsdp", None),
        P("section", "fsdp", None),
        P("section", "fsdp", None),
        P("section", "fsdp", None),
        P("section", "fsdp", None),
        P("section", "fsdp", None),
        P("section", "fsdp"),
        P("section", "fsdp"),
        P(None, "fsdp", "seq", None),
    )
    return jax.shard_map(
        body,
        mesh=mesh,
        in_specs=placed,
        out_specs=(
            P("section", None, "fsdp", "seq", None),
            P("section", None, "fsdp", "seq", None),
            P("section", "fsdp", None),
            P("section", "fsdp", None),
            P("section", "fsdp", None),
            P("section", "fsdp", None),
            P("section", "fsdp", None),
            P("section", "fsdp", None),
            P("section", "fsdp"),
            P("section", "fsdp"),
        ),
        check_vma=False,
    )
```

time: 1210 us -> 1100 us (0.909)
  matrix products: 235 us -> 52 us
  Pallas kernels: 739 us -> 892 us
  other arithmetic: 65.6 us -> 22.8 us
  local copies, waits for them, and re-layouts: 99.1 us -> 58.8 us
    dot_general x16 -> x0, matrix products: 165 us -> none  [the longest x8 90 us: times_transposed(): lax.dot_general(left, matrix, (((1,), (1,)), ((), ())), preferred_element...]
    pallas_call x8 -> x18, Pallas kernels: 473 us -> 613 us  [the longest x6 439 us: exchange(): pl.pallas_call(functools.partial(exchange_kernel, finish, turned, len(row...]
    reduce_scatter x5 -> x3, waiting for transfers between devices: 25.9 us -> 2.6 us  [over_z(): return lax.psum_scatter(value, 'fsdp', scatter_dimension=0, tiled=True)]
    all_gather x4 -> x5, waiting for transfers between devices: 16.9 us -> 37.8 us  [over_fsdp(): return lax.all_gather(value, 'fsdp', axis=0, tiled=True)]
    convert_element_type x8 -> x1, other arithmetic: 19.7 us -> 0.41 us  [body(): out_grad = unpack_rows(mixer_sum[..., in_columns:]).astype(f32)]
    dot_general x8 -> x4, matrix products: 69.8 us -> 52 us  [row_products(): lax.dot_general(left, right, (((0,), (0,)), ((), ())), preferred_element_...]
    reshape x11 -> x4, local copies, waits for them, and re-layouts: 23.4 us -> 8.64 us  [the longest x1 6.12 us: body(): ffn[:, pair_columns:].reshape(-1, width)]
    pallas_call x1, Pallas kernels: 168 us -> 181 us  [last_exchange(): pl.pallas_call(last_kernel, out_shape=[jax.ShapeDtypeStruct((rows, width)...]
  transfers between devices with their start and end apart: 10 -> 11, of which waited for: 4 -> 4; matrix products, arithmetic and copies ran while one was open for 25% -> 4% of each run, Pallas kernels for 46% -> 60%
where the time goes in v3:
time: 1100 us; the launch traced here: 1090 us
  Pallas kernels  892 us (81%)
  local copies, waits for them, and re-layouts  58.8 us (5%)
  matrix products  52 us (5%)
  waiting for transfers between devices  42.3 us (4%)
  other arithmetic  22.8 us (2%)
  between operations  15.2 us (1%)
    pallas_call x6, Pallas kernels, exchange(): pl.pallas_call(functools.partial(exchange_kernel, finish, turned, len(row...  439 us
    pallas_call x1, Pallas kernels, last_exchange(): pl.pallas_call(last_kernel, out_shape=[jax.ShapeDtypeStruct((rows, width)...  181 us
    pallas_call x6, Pallas kernels, local_call(): pl.pallas_call(kernel, out_shape=[jax.ShapeDtypeStruct(shape, dtype) for...  82.6 us
    pallas_call x1, Pallas kernels, start(): pl.pallas_call(start_kernel, out_shape=[jax.ShapeDtypeStruct((2, shards,...  55.2 us
    dot_general x4, matrix products, row_products(): lax.dot_general(left, right, (((0,), (0,)), ((), ())), preferred_element_...  52 us
    pallas_call x1, Pallas kernels, spread_slots(): pl.pallas_call(spread_kernel, out_shape=jax.ShapeDtypeStruct((2, 4, rows,...  42.3 us
    all_gather x5, waiting for transfers between devices, over_fsdp(): return lax.all_gather(value, 'fsdp', axis=0, tiled=True)  37.8 us
    pallas_call x2, Pallas kernels, ffn_forward(): pl.pallas_call(functools.partial(ffn_forward_kernel, pad), grid=(count //...  36 us
  transfers between devices with their start and end apart: 11, of which 4 were waited for; matrix products, arithmetic and copies ran while one was open for 4% of the time, Pallas kernels for 60%

profile of v3, /device:TPU:0, one launch (start us, length us, event | category | flops | bytes accessed | tf_op | source)
XLA Modules:
  0.0 1089.3 jit_solution(12081815327235617465)
XLA Ops:
  23.2 5.3 dynamic-slice_bitcast_fusion.2
  28.4 4.1 concatenate.26.ffn_sent
  36.8 55.2 %start.1 = (f32[2,4,8,384]{3,2,1,0:T(8,128)}, bf16[2,4,256,1536]{3,2,1,0:T(8,128)(2,1)}, bf16[384,2656]{1,0:T(8,128)(2,1)}) custom-call(f32[8,384]{1,0:T(8,128)} %maximum_maximum_fusion.small_ref, bf16[2,256,1536]{2,1,0:T(8,128)(2,1)} %bitcast.239, bf16[384,2656]{1,0:T(8,128)(2,1)} %concatenate.26.ffn_sent), custom_call_target="tpu_custom_call" | custom-call | bytes 192500000 | tf_op jit(solution)/shard_map/start/pallas_call | solution.py:1225
  99.0 21.6 %all-gather.8.cloned.1.call-done = bf16[1536,768]{1,0:T(8,128)(2,1)} async-done(((bf16[384,768]{1,0:T(8,128)(2,1)}), bf16[1536,768]{1,0:T(8,128)(2,1)}) %all-gather.8.cloned.1.call-update) | async-done | bytes 2359312 | tf_op jit(solution)/shard_map/all_gather | solution.py:1369
  124.3 4.5 broadcast_select_fusion.2
  133.7 15.8 %mixer_forward.2 = (f32[8,256,576]{2,1,0:T(8,128)}, f32[8,256,192]{2,1,0:T(8,128)}, bf16[8,256,192]{2,1,0:T(8,128)(2,1)}) custom-call(bf16[8,256,1536]{2,1,0:T(8,128)(2,1)} %bitcast.203, bf16[1536,576]{1,0:T(8,128)(2,1)} %get-tuple-element.98.matrix_ref, f32[3,192]{1,0:T(4,128)} %squeeze.26.taps_ref), custom_call_target="tpu_custom_call" | custom-call | bytes 35000000 | tf_op jit(solution)/shard_map/mixer_forward/pallas_call | solution.py:732
  149.5 64.5 %exchange_1.1 = (f32[256,1536]{1,0:T(8,128)}, bf16[2,4,256,1536]{3,2,1,0:T(8,128)(2,1)}) custom-call(bf16[2,4,256,192]{3,2,1,0:T(8,128)(2,1)} %bitcast.233, bf16[192,1536]{1,0:T(8,128)(2,1)} %select_n.272.refs_1_.matrix_ref, bf16[256,1536]{1,0:T(8,128)(2,1)} %dynamic-slice_bitcast_fusion.1.refs_2_.stream_ref, f32[1,1536]{1,0:T(1,128)} %get-tuple-element.249.refs_3_.refs_4_), custom_call_target="tpu_custom_call" | custom-call | bytes 231000000 | tf_op jit(solution)/shard_map/exchange_1/pallas_call | solution.py:337
  214.0 16.2 %all-gather.10.cloned.1.call-done.matrix_ref.refs_1_ = bf16[1536,1792]{1,0:T(8,128)(2,1)} async-done(((bf16[384,1792]{1,0:T(8,128)(2,1)}), bf16[1536,1792]{1,0:T(8,128)(2,1)}) %all-gather.10.cloned.1.call-update) | async-done | bytes 5505040 | tf_op jit(solution)/shard_map/all_gather | solution.py:1369
  230.2 17.6 %ffn_forward.2 = (f32[2048,1792]{1,0:T(8,128)}, bf16[2048,864]{1,0:T(8,128)(2,1)}) custom-call(bf16[2048,1536]{1,0:T(8,128)(2,1)} %bitcast.225, bf16[1536,1792]{1,0:T(8,128)(2,1)} %all-gather.10.cloned.1.call-done.matrix_ref.refs_1_), custom_call_target="tpu_custom_call" | custom-call | bytes 56000000 | tf_op jit(solution)/shard_map/ffn_forward/pallas_call | solution.py:886
  247.8 42.3 %spread_slots.1 = bf16[2,4,256,1536]{3,2,1,0:T(8,128)(2,1)} custom-call(bf16[2,256,1536]{2,1,0:T(8,128)(2,1)} %bitcast.240), custom_call_target="tpu_custom_call" | custom-call | bytes 147000000 | tf_op jit(solution)/shard_map/spread_slots/pallas_call | solution.py:1277
  290.6 67.5 %exchange_2.1 = (bf16[256,1536]{1,0:T(8,128)(2,1)}, bf16[2,4,256,1536]{3,2,1,0:T(8,128)(2,1)}) custom-call(bf16[2,4,256,864]{3,2,1,0:T(8,128)(2,1)} %bitcast.238, bf16[864,1536]{1,0:T(8,128)(2,1)} %all-gather.12.cloned.1.call-done.refs_1_.matrix_ref, f32[256,1536]{1,0:T(8,128)} %get-tuple-element.113.refs_2_.refs_3_, ...), custom_call_target="tpu_custom_call" | custom-call | bytes 231000000 | tf_op jit(solution)/shard_map/exchange_2/pallas_call | solution.py:337
  361.4 15.2 %mixer_forward.3 = (f32[8,256,576]{2,1,0:T(8,128)}, f32[8,256,192]{2,1,0:T(8,128)}, bf16[8,256,192]{2,1,0:T(8,128)(2,1)}) custom-call(bf16[8,256,1536]{2,1,0:T(8,128)(2,1)} %bitcast.205, bf16[1536,576]{1,0:T(8,128)(2,1)} %get-tuple-element.214.matrix_ref.refs_1_, f32[3,192]{1,0:T(4,128)} %squeeze.60.taps_ref), custom_call_target="tpu_custom_call" | custom-call | bytes 35000000 | tf_op jit(solution)/shard_map/mixer_forward/pallas_call | solution.py:732
  378.3 63.3 %exchange_3.1 = (f32[256,1536]{1,0:T(8,128)}, bf16[2,4,256,1536]{3,2,1,0:T(8,128)(2,1)}) custom-call(bf16[2,4,256,192]{3,2,1,0:T(8,128)(2,1)} %bitcast.235, bf16[192,1536]{1,0:T(8,128)(2,1)} %select_n.284.refs_1_.matrix_ref, bf16[256,1536]{1,0:T(8,128)(2,1)} %get-tuple-element.114.refs_2_.refs_3_, f32[1,1536]{1,0:T(1,128)} %get-tuple-element.247.refs_3_.refs_4_), custom_call_target="tpu_custom_call" | custom-call | bytes 231000000 | tf_op jit(solution)/shard_map/exchange_3/pallas_call | solution.py:337
  441.7 18.5 %ffn_forward.3 = (f32[2048,1792]{1,0:T(8,128)}, bf16[2048,864]{1,0:T(8,128)(2,1)}) custom-call(bf16[2048,1536]{1,0:T(8,128)(2,1)} %bitcast.223, bf16[1536,2656]{1,0:T(8,128)(2,1)} %all-gather.14.cloned.1.call-done.matrix_ref.refs_1_), custom_call_target="tpu_custom_call" | custom-call | bytes 56000000 | tf_op jit(solution)/shard_map/ffn_forward/pallas_call | solution.py:886
  460.1 9.2 convolution_convert_fusion.3
  471.1 6.1 reshape.277.matrix_ref.refs_7_
  477.3 16.2 %ffn_backward.2 = bf16[2048,1792]{1,0:T(8,128)(2,1)} custom-call(bf16[2048,1536]{1,0:T(8,128)(2,1)} %bitcast.207, bf16[864,1536]{1,0:T(8,128)(2,1)} %reshape.277.matrix_ref.refs_7_, f32[2048,1792]{1,0:T(8,128)} %get-tuple-element.123.pairs_ref), custom_call_target="tpu_custom_call" | custom-call | bytes 56000000 | tf_op jit(solution)/shard_map/ffn_backward/pallas_call | solution.py:923
  493.5 17.1 %convolution_convert_fusion.1 = bf16[1536,1792]{1,0:T(8,128)(2,1)} fusion(bf16[2048,1536]{1,0:T(8,128)(2,1)} %bitcast.224, bf16[2048,1792]{1,0:T(8,128)(2,1)} %ffn_backward.2), kind=kOutput, calls=%fused_computation.1 | convolution fusion | flops 11277041664 | bytes 19136512 | tf_op jit(solution)/shard_map/dot_general | solution.py:1059
  513.0 74.9 %exchange_6.1 = (f32[256,1536]{1,0:T(8,128)}, f32[1,1536]{1,0:T(1,128)}, bf16[2,4,256,1536]{3,2,1,0:T(8,128)(2,1)}) custom-call(bf16[2,4,256,1792]{3,2,1,0:T(8,128)(2,1)} %bitcast.202, bf16[1536,2656]{1,0:T(8,128)(2,1)} %all-gather.14.cloned.1.call-done.matrix_ref.refs_1_, bf16[256,1536]{1,0:T(8,128)(2,1)} %dynamic-slice_bitcast_fusion.refs_2_, ...), custom_call_target="tpu_custom_call" | custom-call | bytes 231000000 | tf_op jit(solution)/shard_map/exchange_6/pallas_call | solution.py:337
  587.9 12.2 %mixer_backward.2 = (bf16[8,256,576]{2,1,0:T(8,128)(2,1)}, f32[8,192]{1,0:T(8,128)}) custom-call(bf16[8,256,1536]{2,1,0:T(8,128)(2,1)} %bitcast.213, bf16[192,1536]{1,0:T(8,128)(2,1)} %select_n.284.refs_1_.matrix_ref, f32[8,256,576]{2,1,0:T(8,128)} %get-tuple-element.127.projected_ref, f32[8,256,192]{2,1,0:T(8,128)} %get-tuple-element.128.held_ref, ...), custom_call_target="tpu_custom_call" | custom-call | bytes 42000000 | tf_op jit(solution)/shard_map/mixer_backward/pallas_call | solution.py:732
  600.1 13.5 %mixer_products.2 = bf16[1536,768]{1,0:T(8,128)(2,1)} custom-call(bf16[2048,1536]{1,0:T(8,128)(2,1)} %bitcast.206, bf16[2048,576]{1,0:T(8,128)(2,1)} %bitcast.217, bf16[2048,192]{1,0:T(8,128)(2,1)} %bitcast.236, bf16[2048,1536]{1,0:T(8,128)(2,1)} %bitcast.214), custom_call_target="tpu_custom_call" | custom-call | bytes 49000000 | tf_op jit(solution)/shard_map/mixer_products/pallas_call | solution.py:732
  613.8 95.5 %exchange_7.1 = (f32[256,1536]{1,0:T(8,128)}, f32[1,1536]{1,0:T(1,128)}, bf16[216,1536]{1,0:T(8,128)(2,1)}, bf16[256,1536]{1,0:T(8,128)(2,1)}, bf16[2,4,256,1536]{3,2,1,0:T(8,128)(2,1)}) custom-call(bf16[2,4,256,576]{3,2,1,0:T(8,128)(2,1)} %bitcast.218, bf16[1536,576]{1,0:T(8,128)(2,1)} %get-tuple-element.214.matrix_ref.refs_1_, ...), custom_call_target="tpu_custom_call" | custom-call | bytes 231000000 | tf_op jit(solution)/shard_map/exchange_7/pallas_call | solution.py:337
  710.0 9.1 convolution_convert_fusion.2
  719.1 16.3 %ffn_backward.3 = bf16[2048,1792]{1,0:T(8,128)(2,1)} custom-call(bf16[2048,1536]{1,0:T(8,128)(2,1)} %bitcast.221, bf16[864,1536]{1,0:T(8,128)(2,1)} %all-gather.12.cloned.1.call-done.refs_1_.matrix_ref, f32[2048,1792]{1,0:T(8,128)} %get-tuple-element.139.pairs_ref), custom_call_target="tpu_custom_call" | custom-call | bytes 56000000 | tf_op jit(solution)/shard_map/ffn_backward/pallas_call | solution.py:923
  735.5 16.6 %convolution_convert_fusion = bf16[1536,1792]{1,0:T(8,128)(2,1)} fusion(bf16[2048,1536]{1,0:T(8,128)(2,1)S(1)} %bitcast.228, bf16[2048,1792]{1,0:T(8,128)(2,1)} %ffn_backward.3), kind=kOutput, calls=%fused_computation | convolution fusion | flops 11277041664 | bytes 19136512 | tf_op jit(solution)/shard_map/dot_general | solution.py:1059
  755.1 73.0 %exchange_8.1 = (f32[256,1536]{1,0:T(8,128)}, f32[1,1536]{1,0:T(1,128)}, bf16[2,4,256,1536]{3,2,1,0:T(8,128)(2,1)}) custom-call(bf16[2,4,256,1792]{3,2,1,0:T(8,128)(2,1)} %bitcast.201, bf16[1536,1792]{1,0:T(8,128)(2,1)} %all-gather.10.cloned.1.call-done.matrix_ref.refs_1_, bf16[256,1536]{1,0:T(8,128)(2,1)} %slice_bitcast_fusion.refs_2_.later_ref, ...), custom_call_target="tpu_custom_call" | custom-call | bytes 231000000 | tf_op jit(solution)/shard_map/exchange_8/pallas_call | solution.py:337
  828.1 12.1 %mixer_backward.3 = (bf16[8,256,576]{2,1,0:T(8,128)(2,1)}, f32[8,192]{1,0:T(8,128)}) custom-call(bf16[8,256,1536]{2,1,0:T(8,128)(2,1)} %bitcast.211, bf16[192,1536]{1,0:T(8,128)(2,1)} %select_n.272.refs_1_.matrix_ref, f32[8,256,576]{2,1,0:T(8,128)} %get-tuple-element.144.projected_ref, f32[8,256,192]{2,1,0:T(8,128)} %get-tuple-element.145.held_ref, ...), custom_call_target="tpu_custom_call" | custom-call | bytes 42000000 | tf_op jit(solution)/shard_map/mixer_backward/pallas_call | solution.py:732
  841.2 13.7 %mixer_products.3 = bf16[1536,768]{1,0:T(8,128)(2,1)} custom-call(bf16[2048,1536]{1,0:T(8,128)(2,1)} %bitcast.204, bf16[2048,576]{1,0:T(8,128)(2,1)} %bitcast.215, bf16[2048,192]{1,0:T(8,128)(2,1)} %bitcast.234, bf16[2048,1536]{1,0:T(8,128)(2,1)} %bitcast.212), custom_call_target="tpu_custom_call" | custom-call | bytes 49000000 | tf_op jit(solution)/shard_map/mixer_products/pallas_call | solution.py:732
  859.7 181.5 %last_exchange.1 = (f32[256,1536]{1,0:T(8,128)}, bf16[2,256,1536]{2,1,0:T(8,128)(2,1)}, f32[8,384]{1,0:T(8,128)}, bf16[8,384,1792]{2,1,0:T(8,128)(2,1)}, bf16[8,...) custom-call(bf16[2,4,256,576]{3,2,1,0:T(8,128)(2,1)} %bitcast.216, bf16[1536,576]{1,0:T(8,128)(2,1)} %get-tuple-element.98.matrix_ref, ...), custom_call_target="tpu_custom_call" | custom-call | bytes 455000000 | tf_op jit(solution)/shard_map/last_exchange/pallas_call | solution.py:657
  1043.3 8.6 place_columns.2
  1052.4 14.8 %place_columns.3 = (f32[384,6912]{1,0:T(8,128)}, f32[384,6912]{1,0:T(8,128)}) custom-call(bf16[8,384,1792]{2,1,0:T(8,128)(2,1)} %get-tuple-element.166.stack_ref), custom_call_target="tpu_custom_call" | custom-call | bytes 49000000 | tf_op jit(solution)/shard_map/place_columns/pallas_call | solution.py:718
  1067.2 5.6 bitcast_convert_fusion
  (141 shorter events, 66.4 us)
Async XLA Ops:
  7.2 91.8 %all-gather.6.cloned.1.call-start = ((), (), s32[]{:S(2)}) async-start(), calls=%async_computation.3 | async-start | bytes 2949120 | tf_op jit(solution)/shard_map/all_gather | solution.py:1369
  14.5 106.1 %all-gather.8.cloned.1.call-start = ((), (), s32[]{:S(2)}) async-start(), calls=%async_computation.4 | async-start | bytes 2949120 | tf_op jit(solution)/shard_map/all_gather | solution.py:1369
  16.1 6.9 copy-start.13
  16.1 6.9 copy-start.14
  16.1 20.6 %collective-permute-start = (bf16[384,768]{1,0:T(8,128)(2,1)}, bf16[384,768]{1,0:T(8,128)(2,1)}, u32[]{:S(2)}, u32[]{:S(2)}) collective-permute-start(bf16[384,768]{1,0:T(8,128)(2,1)} %concatenate.24), channel_id=1, source_target_pairs={{0,16},{4,20},{8,24},{12,28},{16,0},{20,4},{24,8},{28,12},{1,17},{... | collective-permute-start | bytes 1769480 | tf_op jit(solution)/shard_map/ppermute | solution.py:979
  32.6 3.5 copy-start.11
  36.8 193.4 %all-gather.10.cloned.1.call-start = ((), (), s32[]{:S(2)}) async-start(), calls=%async_computation.5 | async-start | bytes 6881280 | tf_op jit(solution)/shard_map/all_gather | solution.py:1369
  95.3 1.3 copy-start
  124.3 4.8 copy-start.3
  124.3 5.7 copy-start.6
  128.8 161.3 %all-gather.12.cloned.1.call-start = ((), (), s32[]{:S(2)}) async-start(), calls=%async_computation.6 | async-start | bytes 3317760 | tf_op jit(solution)/shard_map/all_gather | solution.py:1369
  230.2 211.4 %all-gather.14.cloned.1.call-start = ((), (), s32[]{:S(2)}) async-start(), calls=%async_computation.7 | async-start | bytes 10321920 | tf_op jit(solution)/shard_map/all_gather | solution.py:1369
  290.2 323.5 %reduce-scatter.4.cloned.1.call-start = ((), (), s32[]{:S(2)}) async-start(), calls=%async_computation.8 | async-start | bytes 6881280 | tf_op jit(solution)/shard_map/reduce_scatter | solution.py:1502
  358.1 20.2 %collective-permute-start.1 = (bf16[256,1536]{1,0:T(8,128)(2,1)}, bf16[256,1536]{1,0:T(8,128)(2,1)S(1)}, u32[]{:S(2)}, u32[]{:S(2)}) collective-permute-start(bf16[256,1536]{1,0:T(8,128)(2,1)} %get-tuple-element.114.refs_2_.refs_3_), channel_id=1, source_target_pairs={{0,16},{4,20},{8,24},{12,28},{16,0},{20,4},{24,8},{28,12},{1,17},{... | collective-permute-start | bytes 2359304 | tf_op jit(solution)/shard_map/ppermute | solution.py:979
  378.3 81.8 %slice-start.1 = ((s8[6291456]{0:T(1024)(128)(4,1)}), s8[2097152]{0:T(1024)(128)(4,1)S(1)}, s32[]{:S(2)}) async-start(s8[6291456]{0:T(1024)(128)(4,1)} %bitcast.208), calls=%async_computation.12 | async-start | bytes 4194304
  441.6 18.5 %slice-start.2 = ((s8[6291456]{0:T(1024)(128)(4,1)}), s8[4194304]{0:T(1024)(128)(4,1)S(1)}, s32[]{:S(2)}) async-start(s8[6291456]{0:T(1024)(128)(4,1)} %bitcast.208), calls=%async_computation.13 | async-start | bytes 8388608
  469.4 1.8 slice-start
  510.6 1.4 copy-start.4
  510.6 208.5 %reduce-scatter.6.cloned.1.call-start = ((), (), s32[]{:S(2)}) async-start(), calls=%async_computation.9 | async-start | bytes 2949120 | tf_op jit(solution)/shard_map/reduce_scatter | solution.py:1502
  613.7 246.0 %reduce-scatter.8.cloned.1.call-start = ((), (), s32[]{:S(2)}) async-start(), calls=%async_computation.10 | async-start | bytes 6881280 | tf_op jit(solution)/shard_map/reduce_scatter | solution.py:1502
  613.7 96.3 %copy-start.2 = (bf16[2048,864]{1,0:T(8,128)(2,1)S(1)}, bf16[2048,864]{1,0:T(8,128)(2,1)}, u32[]{:S(2)}) copy-start(bf16[2048,864]{1,0:T(8,128)(2,1)} %get-tuple-element.111) | copy-start | bytes 10616836
  709.3 26.2 %collective-permute-start.2 = (bf16[256,1536]{1,0:T(8,128)(2,1)}, bf16[256,1536]{1,0:T(8,128)(2,1)}, u32[]{:S(2)}, u32[]{:S(2)}) collective-permute-start(bf16[256,1536]{1,0:T(8,128)(2,1)} %get-tuple-element.134), channel_id=1, source_target_pairs={{0,16},{4,20},{8,24},{12,28},{16,0},{20,4},{24,8},{28,12},{1,17},{... | collective-permute-start | bytes 2359304 | tf_op jit(solution)/shard_map/ppermute | solution.py:979
  710.0 25.4 %slice-start.3 = ((s8[6291456]{0:T(1024)(128)(4,1)}), s8[2097152]{0:T(1024)(128)(4,1)S(1)}, s32[]{:S(2)}) async-start(s8[6291456]{0:T(1024)(128)(4,1)} %bitcast.226), calls=%async_computation.14 | async-start | bytes 4194304
  719.1 16.4 %slice-start.4 = ((s8[6291456]{0:T(1024)(128)(4,1)}), s8[4194304]{0:T(1024)(128)(4,1)S(1)}, s32[]{:S(2)}) async-start(s8[6291456]{0:T(1024)(128)(4,1)} %bitcast.226), calls=%async_computation.15 | async-start | bytes 8388608
  841.1 13.8 %copy-start.8 = (f32[1,1536]{1,0:T(1,128)S(1)}, f32[1,1536]{1,0:T(1,128)}, u32[]{:S(2)}) copy-start(f32[1,1536]{1,0:T(1,128)} %get-tuple-element.153) | copy-start | bytes 18436
  841.1 13.8 %copy-start.9 = (f32[1,1536]{1,0:T(1,128)S(1)}, f32[1,1536]{1,0:T(1,128)}, u32[]{:S(2)}) copy-start(f32[1,1536]{1,0:T(1,128)} %get-tuple-element.152) | copy-start | bytes 18436
  841.1 13.8 %copy-start.10 = (f32[1,1536]{1,0:T(1,128)S(1)}, f32[1,1536]{1,0:T(1,128)}, u32[]{:S(2)}) copy-start(f32[1,1536]{1,0:T(1,128)} %get-tuple-element.150) | copy-start | bytes 18436
  841.1 14.5 %copy-start.1 = (bf16[256,1536]{1,0:T(8,128)(2,1)S(1)}, bf16[256,1536]{1,0:T(8,128)(2,1)}, u32[]{:S(2)}) copy-start(bf16[256,1536]{1,0:T(8,128)(2,1)} %get-tuple-element.114.refs_2_.refs_3_) | copy-start | bytes 2359300
  841.1 14.5 %copy-start.5 = (bf16[256,1536]{1,0:T(8,128)(2,1)S(1)}, bf16[256,1536]{1,0:T(8,128)(2,1)}, u32[]{:S(2)}) copy-start(bf16[256,1536]{1,0:T(8,128)(2,1)} %get-tuple-element.134) | copy-start | bytes 2359300
  1043.3 8.6 copy-start.7
  1052.4 14.8 %slice-start.5 = ((s8[5308416]{0:T(1024)(128)(4,1)}), s8[4194304]{0:T(1024)(128)(4,1)S(1)}, s32[]{:S(2)}) async-start(s8[5308416]{0:T(1024)(128)(4,1)} %bitcast.230), calls=%async_computation.16 | async-start | bytes 8388608
  1052.4 14.8 %slice-start.6 = ((s8[5308416]{0:T(1024)(128)(4,1)}), s8[1114112]{0:T(1024)(128)(4,1)S(1)}, s32[]{:S(2)}) async-start(s8[5308416]{0:T(1024)(128)(4,1)} %bitcast.230), calls=%async_computation.17 | async-start | bytes 2228224
  (1 other events, 0.7 us)
Sparse Core Ops, SparseCore 0:
  14.6 55.2 all-gather.5
  71.4 49.1 all-gather.7
  128.9 101.1 all-gather.9
  232.2 53.6 all-gather.11
  290.3 145.5 all-gather.13
  510.7 95.7 reduce-scatter.3
  613.8 87.0 reduce-scatter.5
  752.3 107.3 reduce-scatter.7

commit v4 on v3

--- a/solution.py
+++ b/solution.py
@@ -106,14 +106,32 @@
 
 
 def sum_stages(left_ref, matrix_ref, turned, finish_rows, scratch, chunks):
-    partial_ref, from_core, to_corner, from_corner, to_side, from_side, send, recv = scratch
+    left_held, matrix_held, partial_ref, from_core, to_corner, from_corner, to_side, from_side = scratch[:8]
+    send, recv, left_load, matrix_load = scratch[8:]
     odd, core, across, beside, corner = peers()
     f32 = jnp.float32
     units, step = left_ref.shape[1], left_ref.shape[2] // chunks
+    depth = left_ref.shape[3]
+
+    def load(half, k):
+        return pltpu.make_async_copy(
+            left_ref.at[half, :, part(k)], left_held.at[half, :, part(k)], left_load.at[half, k]
+        )
+
+    columns = matrix_held.shape[1]
+    source = matrix_ref if columns == matrix_ref.shape[1] else matrix_ref.at[:, pl.ds(0, columns)]
+    load_matrix = pltpu.make_async_copy(source, matrix_held, matrix_load)
+
+    def load_all():
+        load_matrix.start()
+        for k in range(chunks):
+            for half in (1, 0):
+                load(half, k).start()
 
     def multiply(half, k):
-        left = left_ref[half, :, part(k)].reshape(units * step, left_ref.shape[3])
-        right = matrix_ref[:, : left.shape[1]] if turned else matrix_ref[...]
+        load(half, k).wait()
+        left = left_held[half, :, part(k)].reshape(units * step, depth)
+        right = matrix_held[:, :depth] if turned else matrix_held[...]
         value = lax.dot_general(
             left, right, (((1,), (1 if turned else 0,)), ((), ())), preferred_element_type=f32
         )
@@ -148,6 +166,8 @@
         return partial_ref[0, unit, part(k)].astype(f32) + from_core[unit, part(k)].astype(f32)
 
     def send_core(k):
+        if k == 0:
+            load_matrix.wait()
         multiply(1, k)
         core_sum(k).start()
 
@@ -175,30 +195,32 @@
         )
 
     stages = [send_core, sum_corner, sum_sides, total_rows]
-    return stages, [core_sum, corner_sum, across_sum, beside_sum]
-
-
-STAGE_LAG = 2
-
-
-def ticks_of(stages, chunks):
-    return chunks + STAGE_LAG * (len(stages) - 1)
-
-
-def run_tick(stages, chunks, tick):
+    return stages, [core_sum, corner_sum, across_sum, beside_sum], load_all
+
+
+def ticks_of(stages, chunks, lag):
+    return chunks + lag * (len(stages) - 1)
+
+
+def run_tick(stages, chunks, lag, tick):
     for place, stage in enumerate(stages):
-        if 0 <= tick - STAGE_LAG * place < chunks:
-            stage(tick - STAGE_LAG * place)
-
-
-def run_stages(stages, chunks):
-    for tick in range(ticks_of(stages, chunks)):
-        run_tick(stages, chunks, tick)
-
-
-def sum_scratch(units, rows, width, chunks):
+        if 0 <= tick - lag * place < chunks:
+            stage(tick - lag * place)
+
+
+def run_stages(stages, chunks, lag):
+    for tick in range(ticks_of(stages, chunks, lag)):
+        run_tick(stages, chunks, lag, tick)
+
+
+def sum_scratch(left, matrix, turned, chunks):
     bf16 = jnp.bfloat16
+    _, units, rows, depth = left.shape
+    width = matrix.shape[0] if turned else matrix.shape[1]
+    columns = depth if turned and depth % 128 == 0 else matrix.shape[1]
     return [
+        pltpu.VMEM(left.shape, bf16),
+        pltpu.VMEM((matrix.shape[0], columns), bf16),
         pltpu.VMEM((2, units, rows, width), bf16),
         pltpu.VMEM((units, rows, width), bf16),
         pltpu.VMEM((rows, width), bf16),
@@ -207,7 +229,12 @@
         pltpu.VMEM((2, rows, width), bf16),
         pltpu.SemaphoreType.DMA((4, chunks)),
         pltpu.SemaphoreType.DMA((4, chunks)),
+        pltpu.SemaphoreType.DMA((2, chunks)),
+        pltpu.SemaphoreType.DMA,
     ]
+
+
+SUM_REFS = 12
 
 
 def exchange_kernel(
@@ -224,10 +251,10 @@
     product_out = refs.pop(0) if product else None
     extra_out = refs.pop(0) if extra else None
     spread_ref = refs.pop(0) if gather else None
-    sum_refs, (send, recv), refs = refs[:8], refs[8:10], refs[10:]
+    sum_refs, refs = refs[:SUM_REFS], refs[SUM_REFS:]
+    (send, recv), refs = refs[:2], refs[2:]
     product_refs, extra_refs = (refs[:4], refs[4:]) if product else ([], refs)
     odd, core, across, beside, corner = peers()
-    greet([core, across, beside] + (other_shards() if product else []))
     f32 = jnp.float32
     step = left_ref.shape[2] // chunks
 
@@ -281,10 +308,8 @@
     def arrive(k):
         core_out(k).wait_recv()
 
-    if product:
-        shard_sum = ShardSum(product_ref, *product_refs)
-        shard_sum.start()
-    stages, copies = sum_stages(left_ref, matrix_ref, turned, finish_rows, sum_refs, chunks)
+    stages, copies, load_all = sum_stages(left_ref, matrix_ref, turned, finish_rows, sum_refs, chunks)
+    load_all()
     if gather:
         stages = stages + [pass_corner, pass_core, arrive]
         copies = copies + [across_out, beside_out, corner_out, core_out]
@@ -293,10 +318,17 @@
         def extra_rows(k, rows, total):
             extra_out[rows] = (extra_middle[rows] + total).astype(extra_out.dtype)
 
-        later, more = sum_stages(extra_left, extra_matrix, False, extra_rows, extra_refs, chunks)
+        later, more, load_more = sum_stages(
+            extra_left, extra_matrix, False, extra_rows, extra_refs, chunks
+        )
+        load_more()
         stages = stages[:1] + [lambda k, a=a, b=b: (a(k), b(k)) for a, b in zip(stages[1:5], later)] + stages[5:]
         copies = copies + more
-    run_stages(stages, chunks)
+    greet([core, across, beside] + (other_shards() if product else []))
+    if product:
+        shard_sum = ShardSum(product_ref, *product_refs)
+        shard_sum.start()
+    run_stages(stages, chunks, 1 if left_ref.shape[3] > 1024 else 2)
     if product:
         product_out[...] = shard_sum.total()
         shard_sum.end()
@@ -333,7 +365,7 @@
     shapes += [] if extra is None else [jax.ShapeDtypeStruct((rows, width), bf16)]
     shapes += [jax.ShapeDtypeStruct((2, units, rows, width), bf16)] * gather
     more = ([] if product is None else [product]) + list(extra or ())
-    place = pl.BlockSpec(memory_space=pltpu.VMEM)
+    place, anywhere = pl.BlockSpec(memory_space=pltpu.VMEM), pl.BlockSpec(memory_space=pl.ANY)
     result = pl.pallas_call(
         functools.partial(
             exchange_kernel,
@@ -349,14 +381,15 @@
             chunks,
         ),
         out_shape=shapes,
-        in_specs=[place] * (2 + len(row_ins) + len(shared_ins))
-        + ([] if product is None else [pl.BlockSpec(memory_space=pl.ANY)])
-        + [place] * len(extra or ()),
+        in_specs=[anywhere] * 2
+        + [place] * (len(row_ins) + len(shared_ins))
+        + ([] if product is None else [anywhere])
+        + ([] if extra is None else [anywhere, anywhere, place]),
         out_specs=[place] * len(shapes),
-        scratch_shapes=sum_scratch(units, rows, width, chunks)
+        scratch_shapes=sum_scratch(left, matrix, turned, chunks)
         + [pltpu.SemaphoreType.DMA((4, chunks))] * 2
         + ([] if product is None else shard_sum_scratch(product))
-        + ([] if extra is None else sum_scratch(units, rows, width, chunks)),
+        + ([] if extra is None else sum_scratch(extra[0], extra[1], False, chunks)),
         compiler_params=pltpu.CompilerParams(
             collective_id=number, has_side_effects=True, vmem_limit_bytes=VMEM_BYTES
         ),
@@ -444,7 +477,7 @@
     mixer_out,
     *scratch,
 ):
-    sum_refs, scratch = scratch[:8], scratch[8:]
+    sum_refs, scratch = scratch[:SUM_REFS], scratch[SUM_REFS:]
     pair_both, down_both, mixer_both, grad_low, gain_sum = scratch[:5]
     small_sum, small_sent, small_side, small_z = scratch[5:9]
     local, own_send, own_recv, small_send, small_recv, cross_send, cross_recv = scratch[9:16]
@@ -455,7 +488,6 @@
     _, core, across, beside, _ = peers()
     f32, bf16 = jnp.float32, jnp.bfloat16
     others = other_shards()
-    greet([core, across, beside] + others)
     share = x * 4 + q
     share_across = (1 - x) * 4 + q
     beside_q = (1 - q // 2) * 2 + q % 2
@@ -471,16 +503,6 @@
             device_id=device,
             device_id_type=MESH,
         )
-
-    mixer_sum.start()
-    loads = [
-        pltpu.make_async_copy(pair0_ref, pair_both.at[0], local.at[0]),
-        pltpu.make_async_copy(pair1_ref, pair_both.at[1], local.at[1]),
-        pltpu.make_async_copy(down_ref, down_both.at[1], local.at[2]),
-        pltpu.make_async_copy(mixer_ref, mixer_both.at[1], local.at[3]),
-    ]
-    for one in loads:
-        one.start()
 
     class Owners:
         def __init__(self, place, both, out):
@@ -560,81 +582,93 @@
     pair = Owners(0, pair_both, pair_out)
     down = Owners(1, down_both, down_out)
     mixer = Owners(2, mixer_both, mixer_out)
+
+    def finish_rows(k, rows, total):
+        (grad,), (added,), sent = finish_gradient(
+            total, upstream_ref[rows].astype(f32), stream_ref[rows].astype(f32), gain_ref[...]
+        )
+        grad_ref[rows] = grad
+        grad_low[rows] = sent
+        gain_sum[...] = added if k == 0 else gain_sum[...] + added
+
+    stages, copies, load_all = sum_stages(left_ref, matrix_ref, True, finish_rows, sum_refs, LAST_CHUNKS)
+    load_all()
+    loads = [
+        pltpu.make_async_copy(pair0_ref, pair_both.at[0], local.at[0]),
+        pltpu.make_async_copy(pair1_ref, pair_both.at[1], local.at[1]),
+        pltpu.make_async_copy(down_ref, down_both.at[1], local.at[2]),
+        pltpu.make_async_copy(mixer_ref, mixer_both.at[1], local.at[3]),
+    ]
+    for one in loads:
+        one.start()
+    greet([core, across, beside] + others)
+    mixer_sum.start()
+    later = remote(later_ref, crossed_ref.at[1], cross_send.at[1], cross_recv.at[1], across)
+    later.start()
     for one in loads[:2]:
         one.wait()
     pair.keep().start()
-
-    def finish_rows(k, rows, total):
-        (grad,), (added,), sent = finish_gradient(
-            total, upstream_ref[rows].astype(f32), stream_ref[rows].astype(f32), gain_ref[...]
-        )
-        grad_ref[rows] = grad
-        grad_low[rows] = sent
-        gain_sum[...] = added if k == 0 else gain_sum[...] + added
-
-    stages, copies = sum_stages(left_ref, matrix_ref, True, finish_rows, sum_refs, LAST_CHUNKS)
-    pieces = [(pair, k) for k in pair.chunks]
-    for tick in range(ticks_of(stages, LAST_CHUNKS)):
-        run_tick(stages, LAST_CHUNKS, tick)
-        for owners, k in pieces[tick : tick + 1]:
-            owners.first(k)
+    for tick in range(ticks_of(stages, LAST_CHUNKS, 2)):
+        run_tick(stages, LAST_CHUNKS, 2, tick)
+        if tick in pair.chunks:
+            pair.first(tick)
         if tick == 1:
             down_sum.start()
-    cross = remote(grad_low, crossed_ref.at[0], cross_send.at[0], cross_recv.at[0], across)
-    cross.start()
-    later = remote(later_ref, crossed_ref.at[1], cross_send.at[1], cross_recv.at[1], across)
-    later.start()
-    for owners, k in pieces[:2]:
-        owners.second(k)
-
-    mixer_both[0] = mixer_sum.total()
-    loads[3].wait()
-    mixer.keep().start()
-    mixer.first(0)
-    for owners, k in pieces[2:]:
-        owners.second(k)
-    for owners, k in pieces:
-        owners.third(k)
-
-    mixer.second(0)
-    mixer.third(0)
-    down_both[0] = down_sum.total()
-    loads[2].wait()
-    down.keep().start()
-    down.first(0)
+
     small_rows = smalls_ref.shape[3]
     small_sum[...] = smalls_ref[...]
     for shard in range(shards):
         small_sum[0, shard, 0:1] += gain_sum[:, shard * small_rows : (shard + 1) * small_rows]
+
+    def small_move(step, device):
+        return remote(small_sent.at[step], small_side.at[step], small_send.at[step], small_recv.at[step], device)
+
     for step, device in enumerate((core, across, beside)):
         small_sent[step] = small_sum[...]
-        one = remote(small_sent.at[step], small_side.at[step], small_send.at[step], small_recv.at[step], device)
-        one.start()
-        one.wait()
+        small_move(step, device).start()
+        pair.second(step)
+        small_move(step, device).wait()
         small_sum[...] += small_side[step]
-    small_moves = []
-    for step, device in enumerate(others):
-        one = remote(
+    small_moves = [
+        remote(
             small_sum.at[x, (z + step + 1) % shards],
             small_z.at[step],
             small_send.at[3 + step],
             small_recv.at[3 + step],
             device,
         )
+        for step, device in enumerate(others)
+    ]
+    for one in small_moves:
         one.start()
-        small_moves.append(one)
+
+    mixer_both[0] = mixer_sum.total()
+    loads[3].wait()
+    mixer.keep().start()
+    mixer.first(0)
+    for k in pair.chunks[3:]:
+        pair.second(k)
+    mixer.second(0)
+    down_both[0] = down_sum.total()
+    loads[2].wait()
+    down.keep().start()
+    down.first(0)
+    cross = remote(grad_low, crossed_ref.at[0], cross_send.at[0], cross_recv.at[0], across)
+    cross.start()
+    for k in pair.chunks:
+        pair.third(k)
+    mixer.third(0)
+    down.second(0)
+    for k in pair.chunks:
+        pair.fourth(k)
+    mixer.fourth(0)
+    down.third(0)
+    down.fourth(0)
     small_total = small_sum[x, z]
     for step, one in enumerate(small_moves):
         one.wait()
         small_total = small_total + small_z[step]
     smalls_out[...] = small_total
-
-    for owners, k in pieces:
-        owners.fourth(k)
-    down.second(0)
-    down.third(0)
-    mixer.fourth(0)
-    down.fourth(0)
     for owners in (pair, down, mixer):
         owners.end()
     cross.wait()
@@ -664,9 +698,9 @@
             jax.ShapeDtypeStruct((count, *down.shape), bf16),
             jax.ShapeDtypeStruct((count, shard_rows, mixer_columns), bf16),
         ],
-        in_specs=[vmem] * 7 + [anywhere] * 6,
+        in_specs=[anywhere] * 2 + [vmem] * 5 + [anywhere] * 6,
         out_specs=[vmem] * 3 + [anywhere] * 3,
-        scratch_shapes=sum_scratch(units, rows, width, LAST_CHUNKS)
+        scratch_shapes=sum_scratch(left, matrix, True, LAST_CHUNKS)
         + [
             pltpu.VMEM((2, *pairs[0].shape), bf16),
             pltpu.VMEM((2, *down.shape), bf16),
@@ -711,6 +745,23 @@
             outs[block][...] = value
 
 
+def place_rows_kernel(stack_ref, out_ref):
+    channels = stack_ref.shape[2]
+    blocks = out_ref.shape[1] // channels
+    part = stack_ref.shape[1] // blocks
+    for share in range(stack_ref.shape[0]):
+        pieces = [stack_ref[share, block * part : (block + 1) * part] for block in range(blocks)]
+        out_ref[share * part : (share + 1) * part] = jnp.concatenate(pieces, 1).astype(jnp.float32)
+
+
+def place_rows(stack, width):
+    count, rows, _ = stack.shape
+    (value,) = local_call(
+        place_rows_kernel, [((rows, width), jnp.float32)], [], 5, "place_rows", stack
+    )
+    return value
+
+
 def place_columns(stack, blocks, width, stride, together):
     count, rows, columns = stack.shape
     step = 48
@@ -727,14 +778,15 @@
     )(stack)
 
 
-def local_call(kernel, outs, scratch, us, name, *operands):
+def local_call(kernel, outs, scratch, us, name, *operands, far=()):
     place = pl.BlockSpec(memory_space=pltpu.VMEM)
+    places = [pl.BlockSpec(memory_space=pl.ANY) if i in far else place for i in range(len(operands))]
     return pl.pallas_call(
         kernel,
         out_shape=[jax.ShapeDtypeStruct(shape, dtype) for shape, dtype in outs],
-        in_specs=[place] * len(operands),
+        in_specs=places,
         out_specs=[place] * len(outs),
-        scratch_shapes=[pltpu.VMEM(shape, dtype) for shape, dtype in scratch],
+        scratch_shapes=scratch,
         compiler_params=pltpu.CompilerParams(vmem_limit_bytes=VMEM_BYTES),
         cost_estimate=lasting(us),
         name=name,
@@ -776,10 +828,23 @@
     return whole[:rows], whole[1 : rows + 1], here
 
 
-def mixer_forward_kernel(channels, normed_ref, matrix_ref, taps_ref, projected_ref, held_ref, gated_ref):
+def load_units(source, target, sems):
+    def load(place):
+        return pltpu.make_async_copy(source.at[place], target.at[place], sems.at[place])
+
+    for place in range(8):
+        load(place).start()
+    return lambda place: load(place).wait()
+
+
+def mixer_forward_kernel(
+    channels, normed_far, matrix_ref, taps_ref, projected_ref, held_ref, gated_ref, normed_ref, sems
+):
     f32, bf16 = jnp.float32, jnp.bfloat16
+    wait_unit = load_units(normed_far, normed_ref, sems)
 
     def project(place, carry):
+        wait_unit(place)
         value = jnp.dot(
             normed_ref[place], matrix_ref[:, : 3 * channels], preferred_element_type=f32
         )
@@ -805,21 +870,39 @@
     return local_call(
         functools.partial(mixer_forward_kernel, channels),
         [((8, rows, 3 * channels), f32), ((8, rows, channels), f32), ((8, rows, channels), bf16)],
-        [],
+        [pltpu.VMEM((8, *normed.shape[2:]), bf16), pltpu.SemaphoreType.DMA((8,))],
         10,
         "mixer_forward",
         normed.reshape(8, rows, -1),
         matrix,
         taps,
+        far=(0,),
     )
 
 
 def mixer_backward_kernel(
-    channels, grad_ref, matrix_ref, projected_ref, held_ref, taps_ref, out_ref, taps_out, conv_grad, gate_grad
+    channels,
+    grad_far,
+    matrix_ref,
+    projected_far,
+    held_ref,
+    taps_ref,
+    out_ref,
+    taps_out,
+    conv_grad,
+    gate_grad,
+    grad_ref,
+    projected_ref,
+    grad_sems,
+    projected_sems,
 ):
     f32, bf16 = jnp.float32, jnp.bfloat16
+    wait_grad = load_units(grad_far, grad_ref, grad_sems)
+    wait_projected = load_units(projected_far, projected_ref, projected_sems)
 
     def to_gates(place, carry):
+        wait_grad(place)
+        wait_projected(place)
         grad = lax.dot_general(
             grad_ref[place], matrix_ref[...], (((1,), (1,)), ((), ())), preferred_element_type=f32
         )
@@ -861,7 +944,14 @@
     return local_call(
         functools.partial(mixer_backward_kernel, channels),
         [((8, rows, 3 * channels), bf16), ((8, channels), f32)],
-        [((8, rows, channels), f32), ((8, rows, channels), f32)],
+        [
+            pltpu.VMEM((8, rows, channels), f32),
+            pltpu.VMEM((8, rows, channels), f32),
+            pltpu.VMEM((8, *grads.shape[2:]), bf16),
+            pltpu.VMEM(projected.shape, f32),
+            pltpu.SemaphoreType.DMA((8,)),
+            pltpu.SemaphoreType.DMA((8,)),
+        ],
         12,
         "mixer_backward",
         grads.reshape(8, rows, -1),
@@ -869,6 +959,7 @@
         projected,
         held,
         taps,
+        far=(0, 2),
     )
 
 
@@ -936,22 +1027,34 @@
     )(grads, matrix, pairs)
 
 
-def mixer_product_kernel(shards, normed_ref, projected_ref, gated_ref, grad_ref, out_ref):
+def mixer_product_kernel(
+    shards, normed_far, projected_ref, gated_ref, grad_far, out_ref, normed_ref, grad_ref, sems
+):
     f32, bf16 = jnp.float32, jnp.bfloat16
+    blocks = normed_ref.shape[0]
+    step = normed_ref.shape[2]
+    loads = [
+        pltpu.make_async_copy(normed_far.at[:, pl.ds(i * step, step)], normed_ref.at[i], sems.at[i])
+        for i in range(blocks)
+    ]
+    loads.append(pltpu.make_async_copy(grad_far, grad_ref, sems.at[blocks]))
+    for one in loads:
+        one.start()
     turned = (((0,), (0,)), ((), ()))
     columns = projected_ref.shape[1]
-    width, channels = normed_ref.shape[1], gated_ref.shape[1]
-    step = 256
-    for start in range(0, width, step):
-        out_ref[start : start + step, :columns] = lax.dot_general(
-            normed_ref[:, start : start + step], projected_ref[...], turned, preferred_element_type=f32
+    width, channels = grad_ref.shape[1], gated_ref.shape[1]
+    for i in range(blocks):
+        loads[i].wait()
+        out_ref[i * step : (i + 1) * step, :columns] = lax.dot_general(
+            normed_ref[i], projected_ref[...], turned, preferred_element_type=f32
         ).astype(bf16)
+    loads[blocks].wait()
     value = lax.dot_general(gated_ref[...], grad_ref[...], turned, preferred_element_type=f32)
     part = channels // shards
-    blocks = width // channels
+    pieces = width // channels
     for shard in range(shards):
-        for block in range(blocks):
-            row = (shard * blocks + block) * part
+        for block in range(pieces):
+            row = (shard * pieces + block) * part
             out_ref[row : row + part, columns:] = value[
                 shard * part : (shard + 1) * part, block * channels : (block + 1) * channels
             ].astype(bf16)
@@ -960,16 +1063,22 @@
 def mixer_products(normed, projected_grad, gated, grad):
     width, columns, channels = normed.shape[1], projected_grad.shape[1], gated.shape[1]
     shards = lax.axis_size("fsdp")
+    blocks = width // 256
     (value,) = local_call(
         functools.partial(mixer_product_kernel, shards),
         [((width, columns + channels), jnp.bfloat16)],
-        [],
+        [
+            pltpu.VMEM((blocks, normed.shape[0], width // blocks), jnp.bfloat16),
+            pltpu.VMEM(grad.shape, jnp.bfloat16),
+            pltpu.SemaphoreType.DMA((blocks + 1,)),
+        ],
         14,
         "mixer_products",
         normed,
         projected_grad,
         gated,
         grad,
+        far=(0, 3),
     )
     return value
 
@@ -1402,10 +1511,10 @@
     ).reshape(2, 3, shards * part)
 
     pair_columns = 2 * ffn_pad
-    *mixer_matrices[0], pair_part, down_part = tie(
-        *mixer_matrices[0], ffn_parts[0][:, :pair_columns], ffn_parts[0][:, pair_columns:]
-    )
-    pair = over_fsdp(pair_part)
+    pair = over_fsdp(ffn_parts[0][:, :pair_columns])
+    normed, grad_rows = tie(normed, cotangent[:, 0])
+    normed, grad_units, down_part = tie(normed, spread_slots(grad_rows), ffn_parts[0][:, pair_columns:])
+    down = over_fsdp(down_part.reshape(-1, width))
     ids = jnp.stack([share ^ unit ^ side for side in (0, 1) for unit in units])
     has_before = (ids % seq_count) > 0
     has_after = (ids % seq_count) < seq_count - 1
@@ -1458,8 +1567,6 @@
             1 + 2 * block,
         )
         if block == 0:
-            pair, normed_ffn, value = tie(pair, normed_ffn, down_part.reshape(-1, width))
-            down = over_fsdp(value)
             ffn_matrices = [(pair, down), None]
         pair_matrix, down_matrix = ffn_matrices[block]
         if kernels_fit():
@@ -1468,12 +1575,11 @@
             pairs = times(flat(normed_ffn), pair_matrix[:, :pair_columns])
             hidden = (jax.nn.silu(pairs[:, :ffn_pad]) * pairs[:, ffn_pad:]).astype(bf16)[:, :ffn_columns]
         if block == 0:
-            hidden, grad_rows = tie(hidden, cotangent[:, 0])
-            hidden, grad_units = tie(hidden, spread_slots(grad_rows))
-            hidden, down, value = tie(hidden, down, ffn_parts[1])
+            hidden, down, pair_value, down_value = tie(
+                hidden, down, ffn_parts[1][:, :pair_columns], ffn_parts[1][:, pair_columns:].reshape(-1, width)
+            )
             down_matrix = down
-            ffn = over_fsdp(value)
-            ffn_matrices = [(pair, down), (ffn, ffn[:, pair_columns:].reshape(-1, width))]
+            ffn_matrices = [(pair, down), (over_fsdp(pair_value), over_fsdp(down_value))]
         saved.append((stream, normed, projected, held, gated, middle, normed_ffn, pairs, hidden))
         if block == 0:
             (stream,), _, normed, _, _ = exchange(
@@ -1681,7 +1787,10 @@
         up_grad = columns_of(pair_grad[..., ffn_pad : ffn_pad + ffn_columns], 1)
         in_grad = columns_of(mixer_sum[..., :in_columns], 3)
     down_grad = down_grad.reshape(-1, width).astype(f32)
-    out_grad = unpack_rows(mixer_sum[..., in_columns:]).astype(f32)
+    if kernels_fit():
+        out_grad = place_rows(mixer_sum[..., in_columns:], width)
+    else:
+        out_grad = unpack_rows(mixer_sum[..., in_columns:]).astype(f32)
 
     def by_slot(values, crossed, dtype):
         kept = jnp.where(first_plane, values[0], values[1]).astype(dtype)

time: 1100 us -> 1070 us (0.973)
  Pallas kernels: 892 us -> 873 us
    all_gather x5 -> x6, waiting for transfers between devices: 37.8 us -> 24.6 us  [over_fsdp(): return lax.all_gather(value, 'fsdp', axis=0, tiled=True)]
    pallas_call x6 -> x7, Pallas kernels: 82.6 us -> 77.3 us  [local_call(): pl.pallas_call(kernel, out_shape=[jax.ShapeDtypeStruct(shape, dtype) for...]
  transfers between devices with their start and end apart: 11 -> 12, of which waited for: 4 -> 3; matrix products, arithmetic and copies ran while one was open for 4% -> 7% of each run, Pallas kernels for 60% -> 62%
where the time goes in v4:
time: 1070 us; the launch traced here: 1060 us
  Pallas kernels  873 us (82%)
  local copies, waits for them, and re-layouts  55.9 us (5%)
  matrix products  52 us (5%)
  waiting for transfers between devices  34.9 us (3%)
  other arithmetic  18.7 us (2%)
  between operations  15 us (1%)
    pallas_call x6, Pallas kernels, exchange(): pl.pallas_call(functools.partial(exchange_kernel, finish, turned, len(row...  433 us
    pallas_call x1, Pallas kernels, last_exchange(): pl.pallas_call(last_kernel, out_shape=[jax.ShapeDtypeStruct((rows, width)...  174 us
    pallas_call x7, Pallas kernels, local_call(): pl.pallas_call(kernel, out_shape=[jax.ShapeDtypeStruct(shape, dtype) for...  77.3 us
    pallas_call x1, Pallas kernels, start(): pl.pallas_call(start_kernel, out_shape=[jax.ShapeDtypeStruct((2, shards,...  55.4 us
    dot_general x4, matrix products, row_products(): lax.dot_general(left, right, (((0,), (0,)), ((), ())), preferred_element_...  52 us
    pallas_call x1, Pallas kernels, spread_slots(): pl.pallas_call(spread_kernel, out_shape=jax.ShapeDtypeStruct((2, 4, rows,...  42.3 us
    pallas_call x2, Pallas kernels, ffn_forward(): pl.pallas_call(functools.partial(ffn_forward_kernel, pad), grid=(count //...  35.2 us
    pallas_call x2, Pallas kernels, ffn_backward(): pl.pallas_call(functools.partial(ffn_backward_kernel, pad), grid=(count /...  32.6 us
  transfers between devices with their start and end apart: 12, of which 3 were waited for; matrix products, arithmetic and copies ran while one was open for 7% of the time, Pallas kernels for 62%

profile of v4, /device:TPU:0, one launch (start us, length us, event | category | flops | bytes accessed | tf_op | source)
XLA Modules:
  0.0 1056.4 jit_solution(14894318130216837887)
XLA Ops:
  23.2 5.2 dynamic-slice_bitcast_fusion.2
  28.4 4.4 concatenate.25.ffn_sent
  32.8 3.8 concatenate.24
  37.3 55.4 %start.1 = (f32[2,4,8,384]{3,2,1,0:T(8,128)}, bf16[2,4,256,1536]{3,2,1,0:T(8,128)(2,1)}, bf16[384,2656]{1,0:T(8,128)(2,1)}) custom-call(f32[8,384]{1,0:T(8,128)} %maximum_maximum_fusion.small_ref, bf16[2,256,1536]{2,1,0:T(8,128)(2,1)} %bitcast.233, bf16[384,2656]{1,0:T(8,128)(2,1)} %concatenate.25.ffn_sent), custom_call_target="tpu_custom_call" | custom-call | bytes 192500000 | tf_op jit(solution)/shard_map/start/pallas_call | solution.py:1334
  98.4 42.3 %spread_slots.1 = bf16[2,4,256,1536]{3,2,1,0:T(8,128)(2,1)} custom-call(bf16[2,256,1536]{2,1,0:T(8,128)(2,1)} %bitcast.234), custom_call_target="tpu_custom_call" | custom-call | bytes 147000000 | tf_op jit(solution)/shard_map/spread_slots/pallas_call | solution.py:1386
  155.9 3.8 broadcast_select_fusion.2
  159.7 14.4 %mixer_forward.2 = (f32[8,256,576]{2,1,0:T(8,128)}, f32[8,256,192]{2,1,0:T(8,128)}, bf16[8,256,192]{2,1,0:T(8,128)(2,1)}) custom-call(bf16[8,256,1536]{2,1,0:T(8,128)(2,1)} %bitcast.198, bf16[1536,576]{1,0:T(8,128)(2,1)} %get-tuple-element.205.matrix_ref, f32[3,192]{1,0:T(4,128)} %squeeze.27.taps_ref), custom_call_target="tpu_custom_call" | custom-call | bytes 35000000 | tf_op jit(solution)/shard_map/mixer_forward/pallas_call | solution.py:784
  174.1 63.5 %exchange_1.1 = (f32[256,1536]{1,0:T(8,128)}, bf16[2,4,256,1536]{3,2,1,0:T(8,128)(2,1)}) custom-call(bf16[2,4,256,192]{3,2,1,0:T(8,128)(2,1)} %bitcast.227, bf16[192,1536]{1,0:T(8,128)(2,1)} %select_n.272.refs_1_.matrix_ref, bf16[256,1536]{1,0:T(8,128)(2,1)} %dynamic-slice_bitcast_fusion.1.refs_2_.stream_ref, f32[1,1536]{1,0:T(1,128)} %get-tuple-element.239.refs_3_.refs_4_), custom_call_target="tpu_custom_call" | custom-call | bytes 231000000 | tf_op jit(solution)/shard_map/exchange_1/pallas_call | solution.py:369
  237.6 17.5 %ffn_forward.2 = (f32[2048,1792]{1,0:T(8,128)}, bf16[2048,864]{1,0:T(8,128)(2,1)}) custom-call(bf16[2048,1536]{1,0:T(8,128)(2,1)} %bitcast.218, bf16[1536,1792]{1,0:T(8,128)(2,1)} %all-gather.11.cloned.1.call-done.matrix_ref.refs_1_), custom_call_target="tpu_custom_call" | custom-call | bytes 56000000 | tf_op jit(solution)/shard_map/ffn_forward/pallas_call | solution.py:977
  255.2 24.5 %all-gather.13.cloned.1.call-done.refs_1_.matrix_ref = bf16[864,1536]{1,0:T(8,128)(2,1)} async-done(((bf16[216,1536]{1,0:T(8,128)(2,1)}), bf16[864,1536]{1,0:T(8,128)(2,1)}) %all-gather.13.cloned.1.call-update) | async-done | bytes 2654224 | tf_op jit(solution)/shard_map/all_gather | solution.py:1478
  280.8 67.3 %exchange_2.1 = (bf16[256,1536]{1,0:T(8,128)(2,1)}, bf16[2,4,256,1536]{3,2,1,0:T(8,128)(2,1)}) custom-call(bf16[2,4,256,864]{3,2,1,0:T(8,128)(2,1)} %bitcast.232, bf16[864,1536]{1,0:T(8,128)(2,1)} %all-gather.13.cloned.1.call-done.refs_1_.matrix_ref, f32[256,1536]{1,0:T(8,128)} %get-tuple-element.102.refs_2_.refs_3_, ...), custom_call_target="tpu_custom_call" | custom-call | bytes 231000000 | tf_op jit(solution)/shard_map/exchange_2/pallas_call | solution.py:369
  352.0 14.4 %mixer_forward.3 = (f32[8,256,576]{2,1,0:T(8,128)}, f32[8,256,192]{2,1,0:T(8,128)}, bf16[8,256,192]{2,1,0:T(8,128)(2,1)}) custom-call(bf16[8,256,1536]{2,1,0:T(8,128)(2,1)} %bitcast.200, bf16[1536,576]{1,0:T(8,128)(2,1)} %get-tuple-element.204.matrix_ref.refs_1_, f32[3,192]{1,0:T(4,128)} %squeeze.60.taps_ref), custom_call_target="tpu_custom_call" | custom-call | bytes 35000000 | tf_op jit(solution)/shard_map/mixer_forward/pallas_call | solution.py:784
  369.1 64.1 %exchange_3.1 = (f32[256,1536]{1,0:T(8,128)}, bf16[2,4,256,1536]{3,2,1,0:T(8,128)(2,1)}) custom-call(bf16[2,4,256,192]{3,2,1,0:T(8,128)(2,1)} %bitcast.229, bf16[192,1536]{1,0:T(8,128)(2,1)} %select_n.281.refs_1_.matrix_ref, bf16[256,1536]{1,0:T(8,128)(2,1)} %get-tuple-element.103.refs_2_.refs_3_, f32[1,1536]{1,0:T(1,128)} %get-tuple-element.237.refs_3_.refs_4_), custom_call_target="tpu_custom_call" | custom-call | bytes 231000000 | tf_op jit(solution)/shard_map/exchange_3/pallas_call | solution.py:369
  433.2 17.6 %ffn_forward.3 = (f32[2048,1792]{1,0:T(8,128)}, bf16[2048,864]{1,0:T(8,128)(2,1)}) custom-call(bf16[2048,1536]{1,0:T(8,128)(2,1)} %bitcast.222, bf16[1536,1792]{1,0:T(8,128)(2,1)} %all-gather.15.cloned.1.call-done.matrix_ref.refs_1_), custom_call_target="tpu_custom_call" | custom-call | bytes 56000000 | tf_op jit(solution)/shard_map/ffn_forward/pallas_call | solution.py:977
  450.9 9.2 convolution_convert_fusion.3
  460.0 16.2 %ffn_backward.2 = bf16[2048,1792]{1,0:T(8,128)(2,1)} custom-call(bf16[2048,1536]{1,0:T(8,128)(2,1)} %bitcast.202, bf16[864,1536]{1,0:T(8,128)(2,1)} %all-gather.17.cloned.1.call-done.matrix_ref.refs_7_, f32[2048,1792]{1,0:T(8,128)} %get-tuple-element.113.pairs_ref), custom_call_target="tpu_custom_call" | custom-call | bytes 56000000 | tf_op jit(solution)/shard_map/ffn_backward/pallas_call | solution.py:1014
  476.2 17.1 %convolution_convert_fusion.1 = bf16[1536,1792]{1,0:T(8,128)(2,1)} fusion(bf16[2048,1536]{1,0:T(8,128)(2,1)} %bitcast.223, bf16[2048,1792]{1,0:T(8,128)(2,1)} %ffn_backward.2), kind=kOutput, calls=%fused_computation.1 | convolution fusion | flops 11277041664 | bytes 19136512 | tf_op jit(solution)/shard_map/dot_general | solution.py:1168
  495.7 71.9 %exchange_6.1 = (f32[256,1536]{1,0:T(8,128)}, f32[1,1536]{1,0:T(1,128)}, bf16[2,4,256,1536]{3,2,1,0:T(8,128)(2,1)}) custom-call(bf16[2,4,256,1792]{3,2,1,0:T(8,128)(2,1)} %bitcast.197, bf16[1536,1792]{1,0:T(8,128)(2,1)} %all-gather.15.cloned.1.call-done.matrix_ref.refs_1_, bf16[256,1536]{1,0:T(8,128)(2,1)} %dynamic-slice_bitcast_fusion.refs_2_, ...), custom_call_target="tpu_custom_call" | custom-call | bytes 231000000 | tf_op jit(solution)/shard_map/exchange_6/pallas_call | solution.py:369
  567.7 10.2 mixer_backward.2
  577.9 12.3 %mixer_products.2 = bf16[1536,768]{1,0:T(8,128)(2,1)} custom-call(bf16[2048,1536]{1,0:T(8,128)(2,1)} %bitcast.201, bf16[2048,576]{1,0:T(8,128)(2,1)} %bitcast.212, bf16[2048,192]{1,0:T(8,128)(2,1)} %bitcast.230, bf16[2048,1536]{1,0:T(8,128)(2,1)} %bitcast.209), custom_call_target="tpu_custom_call" | custom-call | bytes 49000000 | tf_op jit(solution)/shard_map/mixer_products/pallas_call | solution.py:784
  590.3 94.5 %exchange_7.1 = (f32[256,1536]{1,0:T(8,128)}, f32[1,1536]{1,0:T(1,128)}, bf16[216,1536]{1,0:T(8,128)(2,1)}, bf16[256,1536]{1,0:T(8,128)(2,1)}, bf16[2,4,256,1536]{3,2,1,0:T(8,128)(2,1)}) custom-call(bf16[2,4,256,576]{3,2,1,0:T(8,128)(2,1)} %bitcast.213, bf16[1536,576]{1,0:T(8,128)(2,1)} %get-tuple-element.204.matrix_ref.refs_1_, ...), custom_call_target="tpu_custom_call" | custom-call | bytes 231000000 | tf_op jit(solution)/shard_map/exchange_7/pallas_call | solution.py:369
  686.0 9.1 convolution_convert_fusion.2
  695.0 16.3 %ffn_backward.3 = bf16[2048,1792]{1,0:T(8,128)(2,1)} custom-call(bf16[2048,1536]{1,0:T(8,128)(2,1)} %bitcast.216, bf16[864,1536]{1,0:T(8,128)(2,1)} %all-gather.13.cloned.1.call-done.refs_1_.matrix_ref, f32[2048,1792]{1,0:T(8,128)} %get-tuple-element.129.pairs_ref), custom_call_target="tpu_custom_call" | custom-call | bytes 56000000 | tf_op jit(solution)/shard_map/ffn_backward/pallas_call | solution.py:1014
  711.4 16.6 %convolution_convert_fusion = bf16[1536,1792]{1,0:T(8,128)(2,1)} fusion(bf16[2048,1536]{1,0:T(8,128)(2,1)S(1)} %bitcast.221, bf16[2048,1792]{1,0:T(8,128)(2,1)} %ffn_backward.3), kind=kOutput, calls=%fused_computation | convolution fusion | flops 11277041664 | bytes 19136512 | tf_op jit(solution)/shard_map/dot_general | solution.py:1168
  731.0 71.6 %exchange_8.1 = (f32[256,1536]{1,0:T(8,128)}, f32[1,1536]{1,0:T(1,128)}, bf16[2,4,256,1536]{3,2,1,0:T(8,128)(2,1)}) custom-call(bf16[2,4,256,1792]{3,2,1,0:T(8,128)(2,1)} %bitcast.196, bf16[1536,1792]{1,0:T(8,128)(2,1)} %all-gather.11.cloned.1.call-done.matrix_ref.refs_1_, bf16[256,1536]{1,0:T(8,128)(2,1)} %slice_bitcast_fusion.refs_2_.later_ref, ...), custom_call_target="tpu_custom_call" | custom-call | bytes 231000000 | tf_op jit(solution)/shard_map/exchange_8/pallas_call | solution.py:369
  802.6 10.3 mixer_backward.3
  813.8 12.5 %mixer_products.3 = bf16[1536,768]{1,0:T(8,128)(2,1)} custom-call(bf16[2048,1536]{1,0:T(8,128)(2,1)} %bitcast.199, bf16[2048,576]{1,0:T(8,128)(2,1)} %bitcast.210, bf16[2048,192]{1,0:T(8,128)(2,1)} %bitcast.228, bf16[2048,1536]{1,0:T(8,128)(2,1)} %bitcast.207), custom_call_target="tpu_custom_call" | custom-call | bytes 49000000 | tf_op jit(solution)/shard_map/mixer_products/pallas_call | solution.py:784
  828.6 7.9 reduce-scatter.8.cloned.1.call-done.pair0_ref
  836.5 173.9 %last_exchange.1 = (f32[256,1536]{1,0:T(8,128)}, bf16[2,256,1536]{2,1,0:T(8,128)(2,1)}, f32[8,384]{1,0:T(8,128)}, bf16[8,384,1792]{2,1,0:T(8,128)(2,1)}, bf16[8,...) custom-call(bf16[2,4,256,576]{3,2,1,0:T(8,128)(2,1)} %bitcast.211, bf16[1536,576]{1,0:T(8,128)(2,1)} %get-tuple-element.205.matrix_ref, ...), custom_call_target="tpu_custom_call" | custom-call | bytes 455000000 | tf_op jit(solution)/shard_map/last_exchange/pallas_call | solution.py:691
  1010.4 8.6 place_columns.2
  1022.8 14.8 %place_columns.3 = (f32[384,6912]{1,0:T(8,128)}, f32[384,6912]{1,0:T(8,128)}) custom-call(bf16[8,384,1792]{2,1,0:T(8,128)(2,1)} %get-tuple-element.156.stack_ref), custom_call_target="tpu_custom_call" | custom-call | bytes 49000000 | tf_op jit(solution)/shard_map/place_columns/pallas_call | solution.py:769
  1037.6 5.6 bitcast_convert_fusion
  (154 shorter events, 64.6 us)
Async XLA Ops:
  7.2 143.0 %all-gather.7.cloned.1.call-start = ((), (), s32[]{:S(2)}) async-start(), calls=%async_computation.3 | async-start | bytes 2949120 | tf_op jit(solution)/shard_map/all_gather | solution.py:1478
  14.5 135.7 %all-gather.9.cloned.1.call-start = ((), (), s32[]{:S(2)}) async-start(), calls=%async_computation.4 | async-start | bytes 2949120 | tf_op jit(solution)/shard_map/all_gather | solution.py:1478
  16.1 6.9 copy-start.19
  16.1 6.9 copy-start.20
  16.1 21.1 %collective-permute-start = (bf16[384,768]{1,0:T(8,128)(2,1)}, bf16[384,768]{1,0:T(8,128)(2,1)}, u32[]{:S(2)}, u32[]{:S(2)}) collective-permute-start(bf16[384,768]{1,0:T(8,128)(2,1)} %concatenate.23), channel_id=1, source_target_pairs={{0,16},{4,20},{8,24},{12,28},{16,0},{20,4},{24,8},{28,12},{1,17},{... | collective-permute-start | bytes 1769480 | tf_op jit(solution)/shard_map/ppermute | solution.py:1088
  37.3 200.4 %all-gather.11.cloned.1.call-start = ((), (), s32[]{:S(2)}) async-start(), calls=%async_computation.5 | async-start | bytes 6881280 | tf_op jit(solution)/shard_map/all_gather | solution.py:1478
  37.3 55.4 %copy-start = (bf16[384,2656]{1,0:T(8,128)(2,1)S(1)}, bf16[384,2656]{1,0:T(8,128)(2,1)}, u32[]{:S(2)}) copy-start(bf16[384,2656]{1,0:T(8,128)(2,1)} %concatenate.24) | copy-start | bytes 6119428
  97.2 182.5 %all-gather.13.cloned.1.call-start = ((), (), s32[]{:S(2)}) async-start(), calls=%async_computation.6 | async-start | bytes 3317760 | tf_op jit(solution)/shard_map/all_gather | solution.py:1478
  142.9 290.3 %all-gather.15.cloned.1.call-start = ((), (), s32[]{:S(2)}) async-start(), calls=%async_computation.7 | async-start | bytes 6881280 | tf_op jit(solution)/shard_map/all_gather | solution.py:1478
  150.2 5.7 copy-start.5
  279.7 180.3 %all-gather.17.cloned.1.call-start = ((), (), s32[]{:S(2)}) async-start(), calls=%async_computation.8 | async-start | bytes 3317760 | tf_op jit(solution)/shard_map/all_gather | solution.py:1478
  280.3 309.9 %reduce-scatter.4.cloned.1.call-start = ((), (), s32[]{:S(2)}) async-start(), calls=%async_computation.9 | async-start | bytes 6881280 | tf_op jit(solution)/shard_map/reduce_scatter | solution.py:1608
  348.1 20.2 %collective-permute-start.1 = (bf16[256,1536]{1,0:T(8,128)(2,1)}, bf16[256,1536]{1,0:T(8,128)(2,1)S(1)}, u32[]{:S(2)}, u32[]{:S(2)}) collective-permute-start(bf16[256,1536]{1,0:T(8,128)(2,1)} %get-tuple-element.103.refs_2_.refs_3_), channel_id=1, source_target_pairs={{0,16},{4,20},{8,24},{12,28},{16,0},{20,4},{24,8},{28,12},{1,17},{... | collective-permute-start | bytes 2359304 | tf_op jit(solution)/shard_map/ppermute | solution.py:1088
  369.1 81.8 %slice-start = ((s8[6291456]{0:T(1024)(128)(4,1)}), s8[2097152]{0:T(1024)(128)(4,1)S(1)}, s32[]{:S(2)}) async-start(s8[6291456]{0:T(1024)(128)(4,1)} %bitcast.203), calls=%async_computation.12 | async-start | bytes 4194304
  433.2 17.7 %slice-start.1 = ((s8[6291456]{0:T(1024)(128)(4,1)}), s8[4194304]{0:T(1024)(128)(4,1)S(1)}, s32[]{:S(2)}) async-start(s8[6291456]{0:T(1024)(128)(4,1)} %bitcast.203), calls=%async_computation.13 | async-start | bytes 8388608
  493.4 201.7 %reduce-scatter.6.cloned.1.call-start = ((), (), s32[]{:S(2)}) async-start(), calls=%async_computation.10 | async-start | bytes 2949120 | tf_op jit(solution)/shard_map/reduce_scatter | solution.py:1608
  590.2 246.3 %reduce-scatter.8.cloned.1.call-start = ((), (), s32[]{:S(2)}) async-start(), calls=%async_computation.11 | async-start | bytes 6881280 | tf_op jit(solution)/shard_map/reduce_scatter | solution.py:1608
  590.3 95.7 %copy-start.3 = (bf16[2048,864]{1,0:T(8,128)(2,1)S(1)}, bf16[2048,864]{1,0:T(8,128)(2,1)}, u32[]{:S(2)}) copy-start(bf16[2048,864]{1,0:T(8,128)(2,1)} %get-tuple-element.100) | copy-start | bytes 10616836
  684.8 26.6 %collective-permute-start.2 = (bf16[256,1536]{1,0:T(8,128)(2,1)}, bf16[256,1536]{1,0:T(8,128)(2,1)S(1)}, u32[]{:S(2)}, u32[]{:S(2)}) collective-permute-start(bf16[256,1536]{1,0:T(8,128)(2,1)} %get-tuple-element.124), channel_id=1, source_target_pairs={{0,16},{4,20},{8,24},{12,28},{16,0},{20,4},{24,8},{28,12},{1,17},{... | collective-permute-start | bytes 2359304 | tf_op jit(solution)/shard_map/ppermute | solution.py:1088
  686.0 25.4 %slice-start.2 = ((s8[6291456]{0:T(1024)(128)(4,1)}), s8[2097152]{0:T(1024)(128)(4,1)S(1)}, s32[]{:S(2)}) async-start(s8[6291456]{0:T(1024)(128)(4,1)} %bitcast.219), calls=%async_computation.14 | async-start | bytes 4194304
  695.0 16.4 %slice-start.3 = ((s8[6291456]{0:T(1024)(128)(4,1)}), s8[4194304]{0:T(1024)(128)(4,1)S(1)}, s32[]{:S(2)}) async-start(s8[6291456]{0:T(1024)(128)(4,1)} %bitcast.219), calls=%async_computation.15 | async-start | bytes 8388608
  813.8 12.6 %copy-start.14 = (f32[1,1536]{1,0:T(1,128)S(1)}, f32[1,1536]{1,0:T(1,128)}, u32[]{:S(2)}) copy-start(f32[1,1536]{1,0:T(1,128)} %get-tuple-element.143) | copy-start | bytes 18436
  813.8 12.6 %copy-start.15 = (f32[1,1536]{1,0:T(1,128)S(1)}, f32[1,1536]{1,0:T(1,128)}, u32[]{:S(2)}) copy-start(f32[1,1536]{1,0:T(1,128)} %get-tuple-element.142) | copy-start | bytes 18436
  813.8 12.6 %copy-start.16 = (f32[1,1536]{1,0:T(1,128)S(1)}, f32[1,1536]{1,0:T(1,128)}, u32[]{:S(2)}) copy-start(f32[1,1536]{1,0:T(1,128)} %get-tuple-element.140) | copy-start | bytes 18436
  813.8 13.3 %copy-start.2 = (bf16[256,1536]{1,0:T(8,128)(2,1)S(1)}, bf16[256,1536]{1,0:T(8,128)(2,1)}, u32[]{:S(2)}) copy-start(bf16[256,1536]{1,0:T(8,128)(2,1)} %get-tuple-element.103.refs_2_.refs_3_) | copy-start | bytes 2359300
  813.8 13.3 %copy-start.10 = (bf16[256,1536]{1,0:T(8,128)(2,1)S(1)}, bf16[256,1536]{1,0:T(8,128)(2,1)}, u32[]{:S(2)}) copy-start(bf16[256,1536]{1,0:T(8,128)(2,1)} %copy-done.9) | copy-start | bytes 2359300
  813.8 13.3 %copy-start.11 = (bf16[256,1536]{1,0:T(8,128)(2,1)S(1)}, bf16[256,1536]{1,0:T(8,128)(2,1)}, u32[]{:S(2)}) copy-start(bf16[256,1536]{1,0:T(8,128)(2,1)} %get-tuple-element.124) | copy-start | bytes 2359300
  1022.8 14.8 %slice-start.4 = ((s8[5308416]{0:T(1024)(128)(4,1)}), s8[4194304]{0:T(1024)(128)(4,1)S(1)}, s32[]{:S(2)}) async-start(s8[5308416]{0:T(1024)(128)(4,1)} %bitcast.224), calls=%async_computation.16 | async-start | bytes 8388608
  1022.8 14.8 %slice-start.5 = ((s8[5308416]{0:T(1024)(128)(4,1)}), s8[1114112]{0:T(1024)(128)(4,1)S(1)}, s32[]{:S(2)}) async-start(s8[5308416]{0:T(1024)(128)(4,1)} %bitcast.224), calls=%async_computation.17 | async-start | bytes 2228224
  1037.6 9.5 copy-start.8
  1043.2 3.8 copy-start.6
  1043.2 3.8 copy-start.7
  (7 other events, 15.0 us)
Sparse Core Ops, SparseCore 0:
  14.6 55.1 all-gather.6
  71.4 49.1 all-gather.8
  122.8 101.1 all-gather.10
  226.0 53.6 all-gather.12
  281.7 101.2 all-gather.14
  385.0 53.7 all-gather.16
  493.5 95.6 reduce-scatter.3
  592.1 85.5 reduce-scatter.5
  728.2 108.2 reduce-scatter.7

commit v5 on v4

--- a/solution.py
+++ b/solution.py
@@ -328,7 +328,7 @@
     if product:
         shard_sum = ShardSum(product_ref, *product_refs)
         shard_sum.start()
-    run_stages(stages, chunks, 1 if left_ref.shape[3] > 1024 else 2)
+    run_stages(stages, chunks, 1 if extra or left_ref.shape[3] > 1024 else 2)
     if product:
         product_out[...] = shard_sum.total()
         shard_sum.end()
@@ -608,8 +608,8 @@
     for one in loads[:2]:
         one.wait()
     pair.keep().start()
-    for tick in range(ticks_of(stages, LAST_CHUNKS, 2)):
-        run_tick(stages, LAST_CHUNKS, 2, tick)
+    for tick in range(ticks_of(stages, LAST_CHUNKS, 1)):
+        run_tick(stages, LAST_CHUNKS, 1, tick)
         if tick in pair.chunks:
             pair.first(tick)
         if tick == 1:
@@ -745,26 +745,30 @@
             outs[block][...] = value
 
 
-def place_rows_kernel(stack_ref, out_ref):
-    channels = stack_ref.shape[2]
+def place_rows_kernel(first, stack_ref, out_ref):
+    channels = stack_ref.shape[2] - first
     blocks = out_ref.shape[1] // channels
     part = stack_ref.shape[1] // blocks
     for share in range(stack_ref.shape[0]):
-        pieces = [stack_ref[share, block * part : (block + 1) * part] for block in range(blocks)]
+        pieces = [stack_ref[share, block * part : (block + 1) * part, first:] for block in range(blocks)]
         out_ref[share * part : (share + 1) * part] = jnp.concatenate(pieces, 1).astype(jnp.float32)
 
 
-def place_rows(stack, width):
-    count, rows, _ = stack.shape
+def place_rows(stack, first, width):
     (value,) = local_call(
-        place_rows_kernel, [((rows, width), jnp.float32)], [], 5, "place_rows", stack
+        functools.partial(place_rows_kernel, first),
+        [((stack.shape[1], width), jnp.float32)],
+        [],
+        5,
+        "place_rows",
+        stack,
     )
     return value
 
 
 def place_columns(stack, blocks, width, stride, together):
     count, rows, columns = stack.shape
-    step = 48
+    step = 96 if rows % 96 == 0 else rows
     widths = [blocks * width] if together else [width] * blocks
     return pl.pallas_call(
         functools.partial(place_kernel, blocks, width, stride),
@@ -1648,9 +1652,11 @@
         pair_matrix, down_matrix = ffn_matrices[block]
         taps = taps_all[block]
         (stream, normed, projected, held, gated, middle, normed_ffn, pairs, hidden) = saved[block]
-        down_product, grad_units, mixer_sum = tie(
-            product(hidden, flat(grad_units)), grad_units, mixer_sum
-        )
+        down_product = product(hidden, flat(grad_units))
+        if block == 1:
+            down_product, grad_units = tie(down_product, grad_units)
+        else:
+            grad_units, mixer_sum = tie(grad_units, mixer_sum)
         if block == 0:
             matrix_grads[1] = (down_grad, pair_grad, mixer_sum)
         down_product = down_product.reshape(shards, -1, width)
@@ -1788,7 +1794,7 @@
         in_grad = columns_of(mixer_sum[..., :in_columns], 3)
     down_grad = down_grad.reshape(-1, width).astype(f32)
     if kernels_fit():
-        out_grad = place_rows(mixer_sum[..., in_columns:], width)
+        out_grad = place_rows(mixer_sum, in_columns, width)
     else:
         out_grad = unpack_rows(mixer_sum[..., in_columns:]).astype(f32)
 

time: 1070 us -> 1060 us (level)
  transfers between devices with their start and end apart: 12 -> 12, of which waited for: 3 -> 3; matrix products, arithmetic and copies ran while one was open for 7% -> 7% of each run, Pallas kernels for 62% -> 63%
where the time goes in v5:
time: 1060 us; the launch traced here: 1050 us
  Pallas kernels  873 us (82%)
  matrix products  52.9 us (5%)
  local copies, waits for them, and re-layouts  52.6 us (5%)
  waiting for transfers between devices  30 us (3%)
  other arithmetic  18.7 us (2%)
  between operations  15 us (1%)
    pallas_call x6, Pallas kernels, exchange(): pl.pallas_call(functools.partial(exchange_kernel, finish, turned, len(row...  433 us
    pallas_call x1, Pallas kernels, last_exchange(): pl.pallas_call(last_kernel, out_shape=[jax.ShapeDtypeStruct((rows, width)...  176 us
    pallas_call x7, Pallas kernels, local_call(): pl.pallas_call(kernel, out_shape=[jax.ShapeDtypeStruct(shape, dtype) for...  78.2 us
    pallas_call x1, Pallas kernels, start(): pl.pallas_call(start_kernel, out_shape=[jax.ShapeDtypeStruct((2, shards,...  55.4 us
    dot_general x4, matrix products, row_products(): lax.dot_general(left, right, (((0,), (0,)), ((), ())), preferred_element_...  52.9 us
    pallas_call x1, Pallas kernels, spread_slots(): pl.pallas_call(spread_kernel, out_shape=jax.ShapeDtypeStruct((2, 4, rows,...  42.3 us
    pallas_call x2, Pallas kernels, ffn_forward(): pl.pallas_call(functools.partial(ffn_forward_kernel, pad), grid=(count //...  35.2 us
    pallas_call x2, Pallas kernels, ffn_backward(): pl.pallas_call(functools.partial(ffn_backward_kernel, pad), grid=(count /...  32.6 us
  transfers between devices with their start and end apart: 12, of which 3 were waited for; matrix products, arithmetic and copies ran while one was open for 7% of the time, Pallas kernels for 63%

profile of v5, /device:TPU:0, one launch (start us, length us, event | category | flops | bytes accessed | tf_op | source)
XLA Modules:
  0.0 1048.9 jit_solution(11417653460399951578)
XLA Ops:
  23.2 5.2 dynamic-slice_bitcast_fusion.2
  28.4 4.4 concatenate.25.ffn_sent
  32.8 3.8 concatenate.24
  37.3 55.4 %start.1 = (f32[2,4,8,384]{3,2,1,0:T(8,128)}, bf16[2,4,256,1536]{3,2,1,0:T(8,128)(2,1)}, bf16[384,2656]{1,0:T(8,128)(2,1)}) custom-call(f32[8,384]{1,0:T(8,128)} %maximum_maximum_fusion.small_ref, bf16[2,256,1536]{2,1,0:T(8,128)(2,1)} %bitcast.233, bf16[384,2656]{1,0:T(8,128)(2,1)} %concatenate.25.ffn_sent), custom_call_target="tpu_custom_call" | custom-call | bytes 192500000 | tf_op jit(solution)/shard_map/start/pallas_call | solution.py:1338
  98.4 42.3 %spread_slots.1 = bf16[2,4,256,1536]{3,2,1,0:T(8,128)(2,1)} custom-call(bf16[2,256,1536]{2,1,0:T(8,128)(2,1)} %bitcast.234), custom_call_target="tpu_custom_call" | custom-call | bytes 147000000 | tf_op jit(solution)/shard_map/spread_slots/pallas_call | solution.py:1390
  155.9 3.8 broadcast_select_fusion.2
  159.7 14.4 %mixer_forward.2 = (f32[8,256,576]{2,1,0:T(8,128)}, f32[8,256,192]{2,1,0:T(8,128)}, bf16[8,256,192]{2,1,0:T(8,128)(2,1)}) custom-call(bf16[8,256,1536]{2,1,0:T(8,128)(2,1)} %bitcast.198, bf16[1536,576]{1,0:T(8,128)(2,1)} %get-tuple-element.203.matrix_ref, f32[3,192]{1,0:T(4,128)} %squeeze.27.taps_ref), custom_call_target="tpu_custom_call" | custom-call | bytes 35000000 | tf_op jit(solution)/shard_map/mixer_forward/pallas_call | solution.py:788
  174.1 63.5 %exchange_1.1 = (f32[256,1536]{1,0:T(8,128)}, bf16[2,4,256,1536]{3,2,1,0:T(8,128)(2,1)}) custom-call(bf16[2,4,256,192]{3,2,1,0:T(8,128)(2,1)} %bitcast.227, bf16[192,1536]{1,0:T(8,128)(2,1)} %select_n.272.refs_1_.matrix_ref, bf16[256,1536]{1,0:T(8,128)(2,1)} %dynamic-slice_bitcast_fusion.1.refs_2_.stream_ref, f32[1,1536]{1,0:T(1,128)} %get-tuple-element.237.refs_3_.refs_4_), custom_call_target="tpu_custom_call" | custom-call | bytes 231000000 | tf_op jit(solution)/shard_map/exchange_1/pallas_call | solution.py:369
  237.6 17.5 %ffn_forward.2 = (f32[2048,1792]{1,0:T(8,128)}, bf16[2048,864]{1,0:T(8,128)(2,1)}) custom-call(bf16[2048,1536]{1,0:T(8,128)(2,1)} %bitcast.218, bf16[1536,1792]{1,0:T(8,128)(2,1)} %all-gather.11.cloned.1.call-done.matrix_ref.refs_1_), custom_call_target="tpu_custom_call" | custom-call | bytes 56000000 | tf_op jit(solution)/shard_map/ffn_forward/pallas_call | solution.py:981
  255.2 24.5 %all-gather.13.cloned.1.call-done.refs_1_.matrix_ref = bf16[864,1536]{1,0:T(8,128)(2,1)} async-done(((bf16[216,1536]{1,0:T(8,128)(2,1)}), bf16[864,1536]{1,0:T(8,128)(2,1)}) %all-gather.13.cloned.1.call-update) | async-done | bytes 2654224 | tf_op jit(solution)/shard_map/all_gather | solution.py:1482
  280.8 67.3 %exchange_2.1 = (bf16[256,1536]{1,0:T(8,128)(2,1)}, bf16[2,4,256,1536]{3,2,1,0:T(8,128)(2,1)}) custom-call(bf16[2,4,256,864]{3,2,1,0:T(8,128)(2,1)} %bitcast.232, bf16[864,1536]{1,0:T(8,128)(2,1)} %all-gather.13.cloned.1.call-done.refs_1_.matrix_ref, f32[256,1536]{1,0:T(8,128)} %get-tuple-element.101.refs_2_.refs_3_, ...), custom_call_target="tpu_custom_call" | custom-call | bytes 231000000 | tf_op jit(solution)/shard_map/exchange_2/pallas_call | solution.py:369
  352.0 14.4 %mixer_forward.3 = (f32[8,256,576]{2,1,0:T(8,128)}, f32[8,256,192]{2,1,0:T(8,128)}, bf16[8,256,192]{2,1,0:T(8,128)(2,1)}) custom-call(bf16[8,256,1536]{2,1,0:T(8,128)(2,1)} %bitcast.200, bf16[1536,576]{1,0:T(8,128)(2,1)} %get-tuple-element.202.matrix_ref.refs_1_, f32[3,192]{1,0:T(4,128)} %squeeze.60.taps_ref), custom_call_target="tpu_custom_call" | custom-call | bytes 35000000 | tf_op jit(solution)/shard_map/mixer_forward/pallas_call | solution.py:788
  369.1 64.1 %exchange_3.1 = (f32[256,1536]{1,0:T(8,128)}, bf16[2,4,256,1536]{3,2,1,0:T(8,128)(2,1)}) custom-call(bf16[2,4,256,192]{3,2,1,0:T(8,128)(2,1)} %bitcast.229, bf16[192,1536]{1,0:T(8,128)(2,1)} %select_n.281.refs_1_.matrix_ref, bf16[256,1536]{1,0:T(8,128)(2,1)} %get-tuple-element.102.refs_2_.refs_3_, f32[1,1536]{1,0:T(1,128)} %get-tuple-element.235.refs_3_.refs_4_), custom_call_target="tpu_custom_call" | custom-call | bytes 231000000 | tf_op jit(solution)/shard_map/exchange_3/pallas_call | solution.py:369
  433.2 17.6 %ffn_forward.3 = (f32[2048,1792]{1,0:T(8,128)}, bf16[2048,864]{1,0:T(8,128)(2,1)}) custom-call(bf16[2048,1536]{1,0:T(8,128)(2,1)} %bitcast.222, bf16[1536,1792]{1,0:T(8,128)(2,1)} %all-gather.15.cloned.1.call-done.matrix_ref.refs_1_), custom_call_target="tpu_custom_call" | custom-call | bytes 56000000 | tf_op jit(solution)/shard_map/ffn_forward/pallas_call | solution.py:981
  450.8 9.2 convolution_convert_fusion.3
  460.0 16.2 %ffn_backward.2 = bf16[2048,1792]{1,0:T(8,128)(2,1)} custom-call(bf16[2048,1536]{1,0:T(8,128)(2,1)} %bitcast.202, bf16[864,1536]{1,0:T(8,128)(2,1)} %all-gather.17.cloned.1.call-done.matrix_ref.refs_7_, f32[2048,1792]{1,0:T(8,128)} %get-tuple-element.112.pairs_ref), custom_call_target="tpu_custom_call" | custom-call | bytes 56000000 | tf_op jit(solution)/shard_map/ffn_backward/pallas_call | solution.py:1018
  476.2 17.1 %convolution_convert_fusion.1 = bf16[1536,1792]{1,0:T(8,128)(2,1)} fusion(bf16[2048,1536]{1,0:T(8,128)(2,1)} %bitcast.223, bf16[2048,1792]{1,0:T(8,128)(2,1)} %ffn_backward.2), kind=kOutput, calls=%fused_computation.1 | convolution fusion | flops 11277041664 | bytes 19136512 | tf_op jit(solution)/shard_map/dot_general | solution.py:1172
  495.7 72.0 %exchange_6.1 = (f32[256,1536]{1,0:T(8,128)}, f32[1,1536]{1,0:T(1,128)}, bf16[2,4,256,1536]{3,2,1,0:T(8,128)(2,1)}) custom-call(bf16[2,4,256,1792]{3,2,1,0:T(8,128)(2,1)} %bitcast.197, bf16[1536,1792]{1,0:T(8,128)(2,1)} %all-gather.15.cloned.1.call-done.matrix_ref.refs_1_, bf16[256,1536]{1,0:T(8,128)(2,1)} %dynamic-slice_bitcast_fusion.refs_2_, ...), custom_call_target="tpu_custom_call" | custom-call | bytes 231000000 | tf_op jit(solution)/shard_map/exchange_6/pallas_call | solution.py:369
  567.6 10.2 mixer_backward.2
  577.9 12.3 %mixer_products.2 = bf16[1536,768]{1,0:T(8,128)(2,1)} custom-call(bf16[2048,1536]{1,0:T(8,128)(2,1)} %bitcast.201, bf16[2048,576]{1,0:T(8,128)(2,1)} %bitcast.212, bf16[2048,192]{1,0:T(8,128)(2,1)} %bitcast.230, bf16[2048,1536]{1,0:T(8,128)(2,1)} %bitcast.209), custom_call_target="tpu_custom_call" | custom-call | bytes 49000000 | tf_op jit(solution)/shard_map/mixer_products/pallas_call | solution.py:788
  590.3 94.1 %exchange_7.1 = (f32[256,1536]{1,0:T(8,128)}, f32[1,1536]{1,0:T(1,128)}, bf16[216,1536]{1,0:T(8,128)(2,1)}, bf16[256,1536]{1,0:T(8,128)(2,1)}, bf16[2,4,256,1536]{3,2,1,0:T(8,128)(2,1)}) custom-call(bf16[2,4,256,576]{3,2,1,0:T(8,128)(2,1)} %bitcast.213, bf16[1536,576]{1,0:T(8,128)(2,1)} %get-tuple-element.202.matrix_ref.refs_1_, ...), custom_call_target="tpu_custom_call" | custom-call | bytes 231000000 | tf_op jit(solution)/shard_map/exchange_7/pallas_call | solution.py:369
  685.7 16.3 %ffn_backward.3 = bf16[2048,1792]{1,0:T(8,128)(2,1)} custom-call(bf16[2048,1536]{1,0:T(8,128)(2,1)} %bitcast.215, bf16[864,1536]{1,0:T(8,128)(2,1)} %all-gather.13.cloned.1.call-done.refs_1_.matrix_ref, f32[2048,1792]{1,0:T(8,128)} %get-tuple-element.128.pairs_ref), custom_call_target="tpu_custom_call" | custom-call | bytes 56000000 | tf_op jit(solution)/shard_map/ffn_backward/pallas_call | solution.py:1018
  704.9 16.5 %convolution_convert_fusion = bf16[1536,1792]{1,0:T(8,128)(2,1)} fusion(bf16[2048,1536]{1,0:T(8,128)(2,1)S(1)} %bitcast.221, bf16[2048,1792]{1,0:T(8,128)(2,1)} %ffn_backward.3), kind=kOutput, calls=%fused_computation | convolution fusion | flops 11277041664 | bytes 19136512 | tf_op jit(solution)/shard_map/dot_general | solution.py:1172
  724.4 10.2 convolution_convert_fusion.2
  734.5 72.3 %exchange_8.1 = (f32[256,1536]{1,0:T(8,128)}, f32[1,1536]{1,0:T(1,128)}, bf16[2,4,256,1536]{3,2,1,0:T(8,128)(2,1)}) custom-call(bf16[2,4,256,1792]{3,2,1,0:T(8,128)(2,1)} %bitcast.196, bf16[1536,1792]{1,0:T(8,128)(2,1)} %all-gather.11.cloned.1.call-done.matrix_ref.refs_1_, bf16[256,1536]{1,0:T(8,128)(2,1)} %slice_bitcast_fusion.refs_2_.later_ref, ...), custom_call_target="tpu_custom_call" | custom-call | bytes 231000000 | tf_op jit(solution)/shard_map/exchange_8/pallas_call | solution.py:369
  806.8 10.4 mixer_backward.3
  818.2 12.5 %mixer_products.3 = bf16[1536,768]{1,0:T(8,128)(2,1)} custom-call(bf16[2048,1536]{1,0:T(8,128)(2,1)} %bitcast.199, bf16[2048,576]{1,0:T(8,128)(2,1)} %bitcast.210, bf16[2048,192]{1,0:T(8,128)(2,1)} %bitcast.228, bf16[2048,1536]{1,0:T(8,128)(2,1)} %bitcast.207), custom_call_target="tpu_custom_call" | custom-call | bytes 49000000 | tf_op jit(solution)/shard_map/mixer_products/pallas_call | solution.py:788
  832.9 175.9 %last_exchange.1 = (f32[256,1536]{1,0:T(8,128)}, bf16[2,256,1536]{2,1,0:T(8,128)(2,1)}, f32[8,384]{1,0:T(8,128)}, bf16[8,384,1792]{2,1,0:T(8,128)(2,1)}, bf16[8,...) custom-call(bf16[2,4,256,576]{3,2,1,0:T(8,128)(2,1)} %bitcast.211, bf16[1536,576]{1,0:T(8,128)(2,1)} %get-tuple-element.203.matrix_ref, ...), custom_call_target="tpu_custom_call" | custom-call | bytes 455000000 | tf_op jit(solution)/shard_map/last_exchange/pallas_call | solution.py:691
  1008.9 7.0 place_columns.2
  1015.8 4.0 place_rows.1
  1020.5 12.8 %place_columns.3 = (f32[384,6912]{1,0:T(8,128)}, f32[384,6912]{1,0:T(8,128)}) custom-call(bf16[8,384,1792]{2,1,0:T(8,128)(2,1)} %get-tuple-element.154.stack_ref), custom_call_target="tpu_custom_call" | custom-call | bytes 49000000 | tf_op jit(solution)/shard_map/place_columns/pallas_call | solution.py:773
  1033.3 5.6 bitcast_convert_fusion
  (151 shorter events, 61.1 us)
Async XLA Ops:
  7.2 143.0 %all-gather.7.cloned.1.call-start = ((), (), s32[]{:S(2)}) async-start(), calls=%async_computation.3 | async-start | bytes 2949120 | tf_op jit(solution)/shard_map/all_gather | solution.py:1482
  14.5 135.7 %all-gather.9.cloned.1.call-start = ((), (), s32[]{:S(2)}) async-start(), calls=%async_computation.4 | async-start | bytes 2949120 | tf_op jit(solution)/shard_map/all_gather | solution.py:1482
  16.1 6.9 copy-start.18
  16.1 6.9 copy-start.19
  16.1 21.1 %collective-permute-start = (bf16[384,768]{1,0:T(8,128)(2,1)}, bf16[384,768]{1,0:T(8,128)(2,1)}, u32[]{:S(2)}, u32[]{:S(2)}) collective-permute-start(bf16[384,768]{1,0:T(8,128)(2,1)} %concatenate.23), channel_id=1, source_target_pairs={{0,16},{4,20},{8,24},{12,28},{16,0},{20,4},{24,8},{28,12},{1,17},{... | collective-permute-start | bytes 1769480 | tf_op jit(solution)/shard_map/ppermute | solution.py:1092
  37.3 200.4 %all-gather.11.cloned.1.call-start = ((), (), s32[]{:S(2)}) async-start(), calls=%async_computation.5 | async-start | bytes 6881280 | tf_op jit(solution)/shard_map/all_gather | solution.py:1482
  37.3 55.4 %copy-start = (bf16[384,2656]{1,0:T(8,128)(2,1)S(1)}, bf16[384,2656]{1,0:T(8,128)(2,1)}, u32[]{:S(2)}) copy-start(bf16[384,2656]{1,0:T(8,128)(2,1)} %concatenate.24) | copy-start | bytes 6119428
  97.2 182.5 %all-gather.13.cloned.1.call-start = ((), (), s32[]{:S(2)}) async-start(), calls=%async_computation.6 | async-start | bytes 3317760 | tf_op jit(solution)/shard_map/all_gather | solution.py:1482
  142.9 290.3 %all-gather.15.cloned.1.call-start = ((), (), s32[]{:S(2)}) async-start(), calls=%async_computation.7 | async-start | bytes 6881280 | tf_op jit(solution)/shard_map/all_gather | solution.py:1482
  150.2 5.7 copy-start.4
  279.7 180.3 %all-gather.17.cloned.1.call-start = ((), (), s32[]{:S(2)}) async-start(), calls=%async_computation.8 | async-start | bytes 3317760 | tf_op jit(solution)/shard_map/all_gather | solution.py:1482
  280.3 309.9 %reduce-scatter.4.cloned.1.call-start = ((), (), s32[]{:S(2)}) async-start(), calls=%async_computation.9 | async-start | bytes 6881280 | tf_op jit(solution)/shard_map/reduce_scatter | solution.py:1612
  348.0 20.2 %collective-permute-start.1 = (bf16[256,1536]{1,0:T(8,128)(2,1)}, bf16[256,1536]{1,0:T(8,128)(2,1)S(1)}, u32[]{:S(2)}, u32[]{:S(2)}) collective-permute-start(bf16[256,1536]{1,0:T(8,128)(2,1)} %get-tuple-element.102.refs_2_.refs_3_), channel_id=1, source_target_pairs={{0,16},{4,20},{8,24},{12,28},{16,0},{20,4},{24,8},{28,12},{1,17},{... | collective-permute-start | bytes 2359304 | tf_op jit(solution)/shard_map/ppermute | solution.py:1092
  369.1 81.7 %slice-start = ((s8[6291456]{0:T(1024)(128)(4,1)}), s8[2097152]{0:T(1024)(128)(4,1)S(1)}, s32[]{:S(2)}) async-start(s8[6291456]{0:T(1024)(128)(4,1)} %bitcast.203), calls=%async_computation.12 | async-start | bytes 4194304
  433.2 17.6 %slice-start.1 = ((s8[6291456]{0:T(1024)(128)(4,1)}), s8[4194304]{0:T(1024)(128)(4,1)S(1)}, s32[]{:S(2)}) async-start(s8[6291456]{0:T(1024)(128)(4,1)} %bitcast.203), calls=%async_computation.13 | async-start | bytes 8388608
  493.4 192.3 %reduce-scatter.6.cloned.1.call-start = ((), (), s32[]{:S(2)}) async-start(), calls=%async_computation.10 | async-start | bytes 2949120 | tf_op jit(solution)/shard_map/reduce_scatter | solution.py:1612
  590.2 242.7 %reduce-scatter.8.cloned.1.call-start = ((), (), s32[]{:S(2)}) async-start(), calls=%async_computation.11 | async-start | bytes 6881280 | tf_op jit(solution)/shard_map/reduce_scatter | solution.py:1612
  590.3 114.7 %slice-start.2 = ((s8[6291456]{0:T(1024)(128)(4,1)}), s8[2097152]{0:T(1024)(128)(4,1)S(1)}, s32[]{:S(2)}) async-start(s8[6291456]{0:T(1024)(128)(4,1)} %bitcast.219), calls=%async_computation.14 | async-start | bytes 4194304
  684.4 20.5 %collective-permute-start.2 = (bf16[256,1536]{1,0:T(8,128)(2,1)}, bf16[256,1536]{1,0:T(8,128)(2,1)S(1)}, u32[]{:S(2)}, u32[]{:S(2)}) collective-permute-start(bf16[256,1536]{1,0:T(8,128)(2,1)} %get-tuple-element.123), channel_id=1, source_target_pairs={{0,16},{4,20},{8,24},{12,28},{16,0},{20,4},{24,8},{28,12},{1,17},{... | collective-permute-start | bytes 2359304 | tf_op jit(solution)/shard_map/ppermute | solution.py:1092
  685.7 19.2 %slice-start.3 = ((s8[6291456]{0:T(1024)(128)(4,1)}), s8[4194304]{0:T(1024)(128)(4,1)S(1)}, s32[]{:S(2)}) async-start(s8[6291456]{0:T(1024)(128)(4,1)} %bitcast.219), calls=%async_computation.15 | async-start | bytes 8388608
  818.2 12.6 %copy-start.13 = (f32[1,1536]{1,0:T(1,128)S(1)}, f32[1,1536]{1,0:T(1,128)}, u32[]{:S(2)}) copy-start(f32[1,1536]{1,0:T(1,128)} %get-tuple-element.142) | copy-start | bytes 18436
  818.2 12.6 %copy-start.14 = (f32[1,1536]{1,0:T(1,128)S(1)}, f32[1,1536]{1,0:T(1,128)}, u32[]{:S(2)}) copy-start(f32[1,1536]{1,0:T(1,128)} %get-tuple-element.141) | copy-start | bytes 18436
  818.2 12.6 %copy-start.15 = (f32[1,1536]{1,0:T(1,128)S(1)}, f32[1,1536]{1,0:T(1,128)}, u32[]{:S(2)}) copy-start(f32[1,1536]{1,0:T(1,128)} %get-tuple-element.139) | copy-start | bytes 18436
  818.2 13.3 %copy-start.2 = (bf16[256,1536]{1,0:T(8,128)(2,1)S(1)}, bf16[256,1536]{1,0:T(8,128)(2,1)}, u32[]{:S(2)}) copy-start(bf16[256,1536]{1,0:T(8,128)(2,1)} %get-tuple-element.102.refs_2_.refs_3_) | copy-start | bytes 2359300
  818.2 13.3 %copy-start.9 = (bf16[256,1536]{1,0:T(8,128)(2,1)S(1)}, bf16[256,1536]{1,0:T(8,128)(2,1)}, u32[]{:S(2)}) copy-start(bf16[256,1536]{1,0:T(8,128)(2,1)} %copy-done.8) | copy-start | bytes 2359300
  818.2 13.3 %copy-start.10 = (bf16[256,1536]{1,0:T(8,128)(2,1)S(1)}, bf16[256,1536]{1,0:T(8,128)(2,1)}, u32[]{:S(2)}) copy-start(bf16[256,1536]{1,0:T(8,128)(2,1)} %get-tuple-element.123) | copy-start | bytes 2359300
  1015.8 4.0 copy-start.12
  1020.4 12.8 %slice-start.4 = ((s8[5308416]{0:T(1024)(128)(4,1)}), s8[4194304]{0:T(1024)(128)(4,1)S(1)}, s32[]{:S(2)}) async-start(s8[5308416]{0:T(1024)(128)(4,1)} %bitcast.224), calls=%async_computation.16 | async-start | bytes 8388608
  1020.4 12.8 %slice-start.5 = ((s8[5308416]{0:T(1024)(128)(4,1)}), s8[1114112]{0:T(1024)(128)(4,1)S(1)}, s32[]{:S(2)}) async-start(s8[5308416]{0:T(1024)(128)(4,1)} %bitcast.224), calls=%async_computation.17 | async-start | bytes 2228224
  1033.3 6.3 copy-start.5
  1033.3 6.3 copy-start.6
  1033.3 6.2 copy-start.7
  (6 other events, 11.7 us)
Sparse Core Ops, SparseCore 0:
  14.6 55.1 all-gather.6
  71.4 49.1 all-gather.8
  122.8 101.1 all-gather.10
  226.0 53.6 all-gather.12
  281.7 101.2 all-gather.14
  385.0 53.7 all-gather.16
  493.5 95.6 reduce-scatter.3
  592.1 85.5 reduce-scatter.5
  721.5 107.3 reduce-scatter.7

commit v6 on v5

--- a/solution.py
+++ b/solution.py
@@ -977,7 +977,7 @@
 
 def ffn_forward(normed, matrix, pad, columns):
     count, width = normed.shape
-    step = 256
+    step = 512
     return pl.pallas_call(
         functools.partial(ffn_forward_kernel, pad),
         grid=(count // step,),
@@ -1014,7 +1014,7 @@
 
 def ffn_backward(grads, matrix, pairs, pad):
     count, width = grads.shape
-    step = 256
+    step = 512
     return pl.pallas_call(
         functools.partial(ffn_backward_kernel, pad),
         grid=(count // step,),

time: 1060 us -> 1060 us (level)
  no operation moved by 1% of the time
where the time goes in v6:
time: 1060 us; the launch traced here: 1050 us
  Pallas kernels  870 us (82%)
  matrix products  52.9 us (5%)
  local copies, waits for them, and re-layouts  52.6 us (5%)
  waiting for transfers between devices  31.3 us (3%)
  other arithmetic  18.7 us (2%)
  between operations  15 us (1%)
    pallas_call x6, Pallas kernels, exchange(): pl.pallas_call(functools.partial(exchange_kernel, finish, turned, len(row...  433 us
    pallas_call x1, Pallas kernels, last_exchange(): pl.pallas_call(last_kernel, out_shape=[jax.ShapeDtypeStruct((rows, width)...  176 us
    pallas_call x7, Pallas kernels, local_call(): pl.pallas_call(kernel, out_shape=[jax.ShapeDtypeStruct(shape, dtype) for...  78.2 us
    pallas_call x1, Pallas kernels, start(): pl.pallas_call(start_kernel, out_shape=[jax.ShapeDtypeStruct((2, shards,...  55.4 us
    dot_general x4, matrix products, row_products(): lax.dot_general(left, right, (((0,), (0,)), ((), ())), preferred_element_...  52.9 us
    pallas_call x1, Pallas kernels, spread_slots(): pl.pallas_call(spread_kernel, out_shape=jax.ShapeDtypeStruct((2, 4, rows,...  42.3 us
    pallas_call x2, Pallas kernels, ffn_forward(): pl.pallas_call(functools.partial(ffn_forward_kernel, pad), grid=(count //...  34.9 us
    pallas_call x2, Pallas kernels, ffn_backward(): pl.pallas_call(functools.partial(ffn_backward_kernel, pad), grid=(count /...  30 us
  transfers between devices with their start and end apart: 12, of which 3 were waited for; matrix products, arithmetic and copies ran while one was open for 7% of the time, Pallas kernels for 63%

profile of v6, /device:TPU:0, one launch (start us, length us, event | category | flops | bytes accessed | tf_op | source)
XLA Modules:
  0.0 1047.4 jit_solution(10471983086655520502)
XLA Ops:
  23.2 5.2 dynamic-slice_bitcast_fusion.2
  28.4 4.4 concatenate.25.ffn_sent
  37.3 55.4 %start.1 = (f32[2,4,8,384]{3,2,1,0:T(8,128)}, bf16[2,4,256,1536]{3,2,1,0:T(8,128)(2,1)}, bf16[384,2656]{1,0:T(8,128)(2,1)}) custom-call(f32[8,384]{1,0:T(8,128)} %maximum_maximum_fusion.small_ref, bf16[2,256,1536]{2,1,0:T(8,128)(2,1)} %bitcast.233, bf16[384,2656]{1,0:T(8,128)(2,1)} %concatenate.25.ffn_sent), custom_call_target="tpu_custom_call" | custom-call | bytes 192500000 | tf_op jit(solution)/shard_map/start/pallas_call | solution.py:1338
  98.4 42.3 %spread_slots.1 = bf16[2,4,256,1536]{3,2,1,0:T(8,128)(2,1)} custom-call(bf16[2,256,1536]{2,1,0:T(8,128)(2,1)} %bitcast.234), custom_call_target="tpu_custom_call" | custom-call | bytes 147000000 | tf_op jit(solution)/shard_map/spread_slots/pallas_call | solution.py:1390
  155.9 3.8 broadcast_select_fusion.2
  159.7 14.4 %mixer_forward.2 = (f32[8,256,576]{2,1,0:T(8,128)}, f32[8,256,192]{2,1,0:T(8,128)}, bf16[8,256,192]{2,1,0:T(8,128)(2,1)}) custom-call(bf16[8,256,1536]{2,1,0:T(8,128)(2,1)} %bitcast.198, bf16[1536,576]{1,0:T(8,128)(2,1)} %get-tuple-element.203.matrix_ref, f32[3,192]{1,0:T(4,128)} %squeeze.27.taps_ref), custom_call_target="tpu_custom_call" | custom-call | bytes 35000000 | tf_op jit(solution)/shard_map/mixer_forward/pallas_call | solution.py:788
  174.1 63.5 %exchange_1.1 = (f32[256,1536]{1,0:T(8,128)}, bf16[2,4,256,1536]{3,2,1,0:T(8,128)(2,1)}) custom-call(bf16[2,4,256,192]{3,2,1,0:T(8,128)(2,1)} %bitcast.227, bf16[192,1536]{1,0:T(8,128)(2,1)} %select_n.272.refs_1_.matrix_ref, bf16[256,1536]{1,0:T(8,128)(2,1)} %dynamic-slice_bitcast_fusion.1.refs_2_.stream_ref, f32[1,1536]{1,0:T(1,128)} %get-tuple-element.237.refs_3_.refs_4_), custom_call_target="tpu_custom_call" | custom-call | bytes 231000000 | tf_op jit(solution)/shard_map/exchange_1/pallas_call | solution.py:369
  237.6 17.5 %ffn_forward.2 = (f32[2048,1792]{1,0:T(8,128)}, bf16[2048,864]{1,0:T(8,128)(2,1)}) custom-call(bf16[2048,1536]{1,0:T(8,128)(2,1)} %bitcast.218, bf16[1536,1792]{1,0:T(8,128)(2,1)} %all-gather.11.cloned.1.call-done.matrix_ref.refs_1_), custom_call_target="tpu_custom_call" | custom-call | bytes 56000000 | tf_op jit(solution)/shard_map/ffn_forward/pallas_call | solution.py:981
  255.1 24.6 %all-gather.13.cloned.1.call-done.refs_1_.matrix_ref = bf16[864,1536]{1,0:T(8,128)(2,1)} async-done(((bf16[216,1536]{1,0:T(8,128)(2,1)}), bf16[864,1536]{1,0:T(8,128)(2,1)}) %all-gather.13.cloned.1.call-update) | async-done | bytes 2654224 | tf_op jit(solution)/shard_map/all_gather | solution.py:1482
  280.8 67.3 %exchange_2.1 = (bf16[256,1536]{1,0:T(8,128)(2,1)}, bf16[2,4,256,1536]{3,2,1,0:T(8,128)(2,1)}) custom-call(bf16[2,4,256,864]{3,2,1,0:T(8,128)(2,1)} %bitcast.232, bf16[864,1536]{1,0:T(8,128)(2,1)} %all-gather.13.cloned.1.call-done.refs_1_.matrix_ref, f32[256,1536]{1,0:T(8,128)} %get-tuple-element.101.refs_2_.refs_3_, ...), custom_call_target="tpu_custom_call" | custom-call | bytes 231000000 | tf_op jit(solution)/shard_map/exchange_2/pallas_call | solution.py:369
  352.0 14.4 %mixer_forward.3 = (f32[8,256,576]{2,1,0:T(8,128)}, f32[8,256,192]{2,1,0:T(8,128)}, bf16[8,256,192]{2,1,0:T(8,128)(2,1)}) custom-call(bf16[8,256,1536]{2,1,0:T(8,128)(2,1)} %bitcast.200, bf16[1536,576]{1,0:T(8,128)(2,1)} %get-tuple-element.202.matrix_ref.refs_1_, f32[3,192]{1,0:T(4,128)} %squeeze.60.taps_ref), custom_call_target="tpu_custom_call" | custom-call | bytes 35000000 | tf_op jit(solution)/shard_map/mixer_forward/pallas_call | solution.py:788
  369.1 64.1 %exchange_3.1 = (f32[256,1536]{1,0:T(8,128)}, bf16[2,4,256,1536]{3,2,1,0:T(8,128)(2,1)}) custom-call(bf16[2,4,256,192]{3,2,1,0:T(8,128)(2,1)} %bitcast.229, bf16[192,1536]{1,0:T(8,128)(2,1)} %select_n.281.refs_1_.matrix_ref, bf16[256,1536]{1,0:T(8,128)(2,1)} %get-tuple-element.102.refs_2_.refs_3_, f32[1,1536]{1,0:T(1,128)} %get-tuple-element.235.refs_3_.refs_4_), custom_call_target="tpu_custom_call" | custom-call | bytes 231000000 | tf_op jit(solution)/shard_map/exchange_3/pallas_call | solution.py:369
  433.2 17.4 %ffn_forward.3 = (f32[2048,1792]{1,0:T(8,128)}, bf16[2048,864]{1,0:T(8,128)(2,1)}) custom-call(bf16[2048,1536]{1,0:T(8,128)(2,1)} %bitcast.222, bf16[1536,1792]{1,0:T(8,128)(2,1)} %all-gather.15.cloned.1.call-done.matrix_ref.refs_1_), custom_call_target="tpu_custom_call" | custom-call | bytes 56000000 | tf_op jit(solution)/shard_map/ffn_forward/pallas_call | solution.py:981
  450.6 9.2 convolution_convert_fusion.3
  459.8 14.9 %ffn_backward.2 = bf16[2048,1792]{1,0:T(8,128)(2,1)} custom-call(bf16[2048,1536]{1,0:T(8,128)(2,1)} %bitcast.202, bf16[864,1536]{1,0:T(8,128)(2,1)} %all-gather.17.cloned.1.call-done.matrix_ref.refs_7_, f32[2048,1792]{1,0:T(8,128)} %get-tuple-element.112.pairs_ref), custom_call_target="tpu_custom_call" | custom-call | bytes 56000000 | tf_op jit(solution)/shard_map/ffn_backward/pallas_call | solution.py:1018
  474.7 17.1 %convolution_convert_fusion.1 = bf16[1536,1792]{1,0:T(8,128)(2,1)} fusion(bf16[2048,1536]{1,0:T(8,128)(2,1)} %bitcast.223, bf16[2048,1792]{1,0:T(8,128)(2,1)} %ffn_backward.2), kind=kOutput, calls=%fused_computation.1 | convolution fusion | flops 11277041664 | bytes 19136512 | tf_op jit(solution)/shard_map/dot_general | solution.py:1172
  494.2 71.9 %exchange_6.1 = (f32[256,1536]{1,0:T(8,128)}, f32[1,1536]{1,0:T(1,128)}, bf16[2,4,256,1536]{3,2,1,0:T(8,128)(2,1)}) custom-call(bf16[2,4,256,1792]{3,2,1,0:T(8,128)(2,1)} %bitcast.197, bf16[1536,1792]{1,0:T(8,128)(2,1)} %all-gather.15.cloned.1.call-done.matrix_ref.refs_1_, bf16[256,1536]{1,0:T(8,128)(2,1)} %dynamic-slice_bitcast_fusion.refs_2_, ...), custom_call_target="tpu_custom_call" | custom-call | bytes 231000000 | tf_op jit(solution)/shard_map/exchange_6/pallas_call | solution.py:369
  566.1 10.2 mixer_backward.2
  576.4 12.3 %mixer_products.2 = bf16[1536,768]{1,0:T(8,128)(2,1)} custom-call(bf16[2048,1536]{1,0:T(8,128)(2,1)} %bitcast.201, bf16[2048,576]{1,0:T(8,128)(2,1)} %bitcast.212, bf16[2048,192]{1,0:T(8,128)(2,1)} %bitcast.230, bf16[2048,1536]{1,0:T(8,128)(2,1)} %bitcast.209), custom_call_target="tpu_custom_call" | custom-call | bytes 49000000 | tf_op jit(solution)/shard_map/mixer_products/pallas_call | solution.py:788
  588.8 94.1 %exchange_7.1 = (f32[256,1536]{1,0:T(8,128)}, f32[1,1536]{1,0:T(1,128)}, bf16[216,1536]{1,0:T(8,128)(2,1)}, bf16[256,1536]{1,0:T(8,128)(2,1)}, bf16[2,4,256,1536]{3,2,1,0:T(8,128)(2,1)}) custom-call(bf16[2,4,256,576]{3,2,1,0:T(8,128)(2,1)} %bitcast.213, bf16[1536,576]{1,0:T(8,128)(2,1)} %get-tuple-element.202.matrix_ref.refs_1_, ...), custom_call_target="tpu_custom_call" | custom-call | bytes 231000000 | tf_op jit(solution)/shard_map/exchange_7/pallas_call | solution.py:369
  684.2 15.1 %ffn_backward.3 = bf16[2048,1792]{1,0:T(8,128)(2,1)} custom-call(bf16[2048,1536]{1,0:T(8,128)(2,1)} %bitcast.215, bf16[864,1536]{1,0:T(8,128)(2,1)} %all-gather.13.cloned.1.call-done.refs_1_.matrix_ref, f32[2048,1792]{1,0:T(8,128)} %get-tuple-element.128.pairs_ref), custom_call_target="tpu_custom_call" | custom-call | bytes 56000000 | tf_op jit(solution)/shard_map/ffn_backward/pallas_call | solution.py:1018
  699.3 4.1 collective-permute-done.2
  703.4 16.5 %convolution_convert_fusion = bf16[1536,1792]{1,0:T(8,128)(2,1)} fusion(bf16[2048,1536]{1,0:T(8,128)(2,1)S(1)} %bitcast.221, bf16[2048,1792]{1,0:T(8,128)(2,1)} %ffn_backward.3), kind=kOutput, calls=%fused_computation | convolution fusion | flops 11277041664 | bytes 19136512 | tf_op jit(solution)/shard_map/dot_general | solution.py:1172
  722.9 10.2 convolution_convert_fusion.2
  733.0 72.3 %exchange_8.1 = (f32[256,1536]{1,0:T(8,128)}, f32[1,1536]{1,0:T(1,128)}, bf16[2,4,256,1536]{3,2,1,0:T(8,128)(2,1)}) custom-call(bf16[2,4,256,1792]{3,2,1,0:T(8,128)(2,1)} %bitcast.196, bf16[1536,1792]{1,0:T(8,128)(2,1)} %all-gather.11.cloned.1.call-done.matrix_ref.refs_1_, bf16[256,1536]{1,0:T(8,128)(2,1)} %slice_bitcast_fusion.refs_2_.later_ref, ...), custom_call_target="tpu_custom_call" | custom-call | bytes 231000000 | tf_op jit(solution)/shard_map/exchange_8/pallas_call | solution.py:369
  805.3 10.4 mixer_backward.3
  816.7 12.4 %mixer_products.3 = bf16[1536,768]{1,0:T(8,128)(2,1)} custom-call(bf16[2048,1536]{1,0:T(8,128)(2,1)} %bitcast.199, bf16[2048,576]{1,0:T(8,128)(2,1)} %bitcast.210, bf16[2048,192]{1,0:T(8,128)(2,1)} %bitcast.228, bf16[2048,1536]{1,0:T(8,128)(2,1)} %bitcast.207), custom_call_target="tpu_custom_call" | custom-call | bytes 49000000 | tf_op jit(solution)/shard_map/mixer_products/pallas_call | solution.py:788
  831.5 175.9 %last_exchange.1 = (f32[256,1536]{1,0:T(8,128)}, bf16[2,256,1536]{2,1,0:T(8,128)(2,1)}, f32[8,384]{1,0:T(8,128)}, bf16[8,384,1792]{2,1,0:T(8,128)(2,1)}, bf16[8,...) custom-call(bf16[2,4,256,576]{3,2,1,0:T(8,128)(2,1)} %bitcast.211, bf16[1536,576]{1,0:T(8,128)(2,1)} %get-tuple-element.203.matrix_ref, ...), custom_call_target="tpu_custom_call" | custom-call | bytes 455000000 | tf_op jit(solution)/shard_map/last_exchange/pallas_call | solution.py:691
  1007.4 7.0 place_columns.2
  1014.4 4.0 place_rows.1
  1019.0 12.8 %place_columns.3 = (f32[384,6912]{1,0:T(8,128)}, f32[384,6912]{1,0:T(8,128)}) custom-call(bf16[8,384,1792]{2,1,0:T(8,128)(2,1)} %get-tuple-element.154.stack_ref), custom_call_target="tpu_custom_call" | custom-call | bytes 49000000 | tf_op jit(solution)/shard_map/place_columns/pallas_call | solution.py:773
  1031.8 5.6 bitcast_convert_fusion
  (151 shorter events, 62.0 us)
Async XLA Ops:
  7.2 143.0 %all-gather.7.cloned.1.call-start = ((), (), s32[]{:S(2)}) async-start(), calls=%async_computation.3 | async-start | bytes 2949120 | tf_op jit(solution)/shard_map/all_gather | solution.py:1482
  14.5 135.7 %all-gather.9.cloned.1.call-start = ((), (), s32[]{:S(2)}) async-start(), calls=%async_computation.4 | async-start | bytes 2949120 | tf_op jit(solution)/shard_map/all_gather | solution.py:1482
  16.1 6.9 copy-start.18
  16.1 6.9 copy-start.19
  16.1 21.1 %collective-permute-start = (bf16[384,768]{1,0:T(8,128)(2,1)}, bf16[384,768]{1,0:T(8,128)(2,1)}, u32[]{:S(2)}, u32[]{:S(2)}) collective-permute-start(bf16[384,768]{1,0:T(8,128)(2,1)} %concatenate.23), channel_id=1, source_target_pairs={{0,16},{4,20},{8,24},{12,28},{16,0},{20,4},{24,8},{28,12},{1,17},{... | collective-permute-start | bytes 1769480 | tf_op jit(solution)/shard_map/ppermute | solution.py:1092
  37.3 200.4 %all-gather.11.cloned.1.call-start = ((), (), s32[]{:S(2)}) async-start(), calls=%async_computation.5 | async-start | bytes 6881280 | tf_op jit(solution)/shard_map/all_gather | solution.py:1482
  37.3 55.4 %copy-start = (bf16[384,2656]{1,0:T(8,128)(2,1)S(1)}, bf16[384,2656]{1,0:T(8,128)(2,1)}, u32[]{:S(2)}) copy-start(bf16[384,2656]{1,0:T(8,128)(2,1)} %concatenate.24) | copy-start | bytes 6119428
  97.2 182.5 %all-gather.13.cloned.1.call-start = ((), (), s32[]{:S(2)}) async-start(), calls=%async_computation.6 | async-start | bytes 3317760 | tf_op jit(solution)/shard_map/all_gather | solution.py:1482
  142.9 290.3 %all-gather.15.cloned.1.call-start = ((), (), s32[]{:S(2)}) async-start(), calls=%async_computation.7 | async-start | bytes 6881280 | tf_op jit(solution)/shard_map/all_gather | solution.py:1482
  150.2 5.7 copy-start.4
  279.7 180.1 %all-gather.17.cloned.1.call-start = ((), (), s32[]{:S(2)}) async-start(), calls=%async_computation.8 | async-start | bytes 3317760 | tf_op jit(solution)/shard_map/all_gather | solution.py:1482
  280.3 308.4 %reduce-scatter.4.cloned.1.call-start = ((), (), s32[]{:S(2)}) async-start(), calls=%async_computation.9 | async-start | bytes 6881280 | tf_op jit(solution)/shard_map/reduce_scatter | solution.py:1612
  348.0 20.2 %collective-permute-start.1 = (bf16[256,1536]{1,0:T(8,128)(2,1)}, bf16[256,1536]{1,0:T(8,128)(2,1)S(1)}, u32[]{:S(2)}, u32[]{:S(2)}) collective-permute-start(bf16[256,1536]{1,0:T(8,128)(2,1)} %get-tuple-element.102.refs_2_.refs_3_), channel_id=1, source_target_pairs={{0,16},{4,20},{8,24},{12,28},{16,0},{20,4},{24,8},{28,12},{1,17},{... | collective-permute-start | bytes 2359304 | tf_op jit(solution)/shard_map/ppermute | solution.py:1092
  369.1 81.5 %slice-start = ((s8[6291456]{0:T(1024)(128)(4,1)}), s8[2097152]{0:T(1024)(128)(4,1)S(1)}, s32[]{:S(2)}) async-start(s8[6291456]{0:T(1024)(128)(4,1)} %bitcast.203), calls=%async_computation.12 | async-start | bytes 4194304
  433.2 17.4 %slice-start.1 = ((s8[6291456]{0:T(1024)(128)(4,1)}), s8[4194304]{0:T(1024)(128)(4,1)S(1)}, s32[]{:S(2)}) async-start(s8[6291456]{0:T(1024)(128)(4,1)} %bitcast.203), calls=%async_computation.13 | async-start | bytes 8388608
  491.9 192.4 %reduce-scatter.6.cloned.1.call-start = ((), (), s32[]{:S(2)}) async-start(), calls=%async_computation.10 | async-start | bytes 2949120 | tf_op jit(solution)/shard_map/reduce_scatter | solution.py:1612
  588.7 242.7 %reduce-scatter.8.cloned.1.call-start = ((), (), s32[]{:S(2)}) async-start(), calls=%async_computation.11 | async-start | bytes 6881280 | tf_op jit(solution)/shard_map/reduce_scatter | solution.py:1612
  588.8 114.7 %slice-start.2 = ((s8[6291456]{0:T(1024)(128)(4,1)}), s8[2097152]{0:T(1024)(128)(4,1)S(1)}, s32[]{:S(2)}) async-start(s8[6291456]{0:T(1024)(128)(4,1)} %bitcast.219), calls=%async_computation.14 | async-start | bytes 4194304
  682.9 20.5 %collective-permute-start.2 = (bf16[256,1536]{1,0:T(8,128)(2,1)}, bf16[256,1536]{1,0:T(8,128)(2,1)S(1)}, u32[]{:S(2)}, u32[]{:S(2)}) collective-permute-start(bf16[256,1536]{1,0:T(8,128)(2,1)} %get-tuple-element.123), channel_id=1, source_target_pairs={{0,16},{4,20},{8,24},{12,28},{16,0},{20,4},{24,8},{28,12},{1,17},{... | collective-permute-start | bytes 2359304 | tf_op jit(solution)/shard_map/ppermute | solution.py:1092
  684.2 19.2 %slice-start.3 = ((s8[6291456]{0:T(1024)(128)(4,1)}), s8[4194304]{0:T(1024)(128)(4,1)S(1)}, s32[]{:S(2)}) async-start(s8[6291456]{0:T(1024)(128)(4,1)} %bitcast.219), calls=%async_computation.15 | async-start | bytes 8388608
  816.7 12.6 %copy-start.13 = (f32[1,1536]{1,0:T(1,128)S(1)}, f32[1,1536]{1,0:T(1,128)}, u32[]{:S(2)}) copy-start(f32[1,1536]{1,0:T(1,128)} %get-tuple-element.142) | copy-start | bytes 18436
  816.7 12.6 %copy-start.14 = (f32[1,1536]{1,0:T(1,128)S(1)}, f32[1,1536]{1,0:T(1,128)}, u32[]{:S(2)}) copy-start(f32[1,1536]{1,0:T(1,128)} %get-tuple-element.141) | copy-start | bytes 18436
  816.7 12.6 %copy-start.15 = (f32[1,1536]{1,0:T(1,128)S(1)}, f32[1,1536]{1,0:T(1,128)}, u32[]{:S(2)}) copy-start(f32[1,1536]{1,0:T(1,128)} %get-tuple-element.139) | copy-start | bytes 18436
  816.7 13.3 %copy-start.2 = (bf16[256,1536]{1,0:T(8,128)(2,1)S(1)}, bf16[256,1536]{1,0:T(8,128)(2,1)}, u32[]{:S(2)}) copy-start(bf16[256,1536]{1,0:T(8,128)(2,1)} %get-tuple-element.102.refs_2_.refs_3_) | copy-start | bytes 2359300
  816.7 13.3 %copy-start.9 = (bf16[256,1536]{1,0:T(8,128)(2,1)S(1)}, bf16[256,1536]{1,0:T(8,128)(2,1)}, u32[]{:S(2)}) copy-start(bf16[256,1536]{1,0:T(8,128)(2,1)} %copy-done.8) | copy-start | bytes 2359300
  816.7 13.3 %copy-start.10 = (bf16[256,1536]{1,0:T(8,128)(2,1)S(1)}, bf16[256,1536]{1,0:T(8,128)(2,1)}, u32[]{:S(2)}) copy-start(bf16[256,1536]{1,0:T(8,128)(2,1)} %get-tuple-element.123) | copy-start | bytes 2359300
  1014.4 4.0 copy-start.12
  1019.0 12.8 %slice-start.4 = ((s8[5308416]{0:T(1024)(128)(4,1)}), s8[4194304]{0:T(1024)(128)(4,1)S(1)}, s32[]{:S(2)}) async-start(s8[5308416]{0:T(1024)(128)(4,1)} %bitcast.224), calls=%async_computation.16 | async-start | bytes 8388608
  1019.0 12.8 %slice-start.5 = ((s8[5308416]{0:T(1024)(128)(4,1)}), s8[1114112]{0:T(1024)(128)(4,1)S(1)}, s32[]{:S(2)}) async-start(s8[5308416]{0:T(1024)(128)(4,1)} %bitcast.224), calls=%async_computation.17 | async-start | bytes 2228224
  1031.8 6.3 copy-start.5
  1031.8 6.3 copy-start.6
  1031.8 6.2 copy-start.7
  (6 other events, 11.7 us)
Sparse Core Ops, SparseCore 0:
  14.6 55.1 all-gather.6
  71.4 49.1 all-gather.8
  122.8 101.1 all-gather.10
  226.0 53.6 all-gather.12
  281.7 101.2 all-gather.14
  385.0 53.7 all-gather.16
  492.0 95.6 reduce-scatter.3
  590.6 85.5 reduce-scatter.5
  720.0 107.3 reduce-scatter.7
